TPU v7x, 32 devices: a whole 2x2x4 slice. The times are simulated.
32 devices in a mesh: dp: 4 (over y, x), ctx: 8 (over z, core).
Axes of the slice: x: 2, y: 2, z: 4, core: 2. Of those that a mesh axis runs over, the one named last changes fastest.
Arguments:
- tokens: bfloat16 [4, 2048, 4096], P('dp', 'ctx'), may hold values from -6 to 6
- queries: bfloat16 [4, 2048, 2048], P('dp', 'ctx'), may hold values from -260 to 260, as said below
- kv_weight: bfloat16 [4096, 1024], P('ctx', 'dp'), may hold values from -0.09375 to 0.09375
- doc_blocks: int32 [4, 4], P('dp'), may hold values from 1 to 8, 16 in all within a row
- block_mask: int32 [4, 16, 7], P('dp'), may hold values 0 or 1
- plan: int32 [4, 16], P('dp'), may hold values from 0 to 15, as said below
Outputs:
- attended: bfloat16 [4, 2048, 2048], P('dp', 'ctx')
- stats: float32 [4, 16, 2048], P('dp', None, 'ctx')
Inputs may be any that keep to these rules, and one draw needn't show every extreme that they name: queries of unit order, in some draws with a few rows far larger. `doc_blocks`: the documents of a pack in order, their lengths summing to 16. `block_mask`: entry [b, w] lets block b attend block b - w - 1 where that block is of the same document. plan[b] = ctx index * 2 + place; the slot lies on block b's own ctx index or on the one that differs from it in the lowest bit, and every slot is named by exactly one block.
All inputs are finite; a program needn't handle non-finite values.
Results may differ from a plain program's by a relative error of at most 0.012.
The roundings to bfloat16 on the way count: a program that leaves them out, or rounds other values in their place, can miss the bound.
Values may be sent and summed in bfloat16 or wider, within the bound.
No kernel may reach another device: no remote copies, remote signals or barrier semaphores. Data moves between devices by JAX's collectives and lax.ppermute only.
A program may use at most 128 MiB of HBM per device.

v0:
```python
import math

import jax
import jax.numpy as jnp
from jax import lax
from jax.sharding import PartitionSpec as P

HD = 128
QH = 16
KVH = 4
BLK = 128
MAXDOC = 8


def from_partner(block, axis, stride):
    count = lax.axis_size(axis)
    route = []
    for low in range(count):
        high = low | 1 << stride
        if high != low and high < count:
            route += [(low, high), (high, low)]
    return lax.ppermute(block, axis, route)


def passed_along(array, axis, by):
    size = lax.axis_size(axis)
    pairs = [(i, i + by) for i in range(size) if 0 <= i + by < size]
    return lax.ppermute(array, axis, pairs)


def document_of_blocks(doc_blocks, count):
    ends = jnp.cumsum(doc_blocks)
    blocks = jnp.arange(count, dtype=jnp.int32)
    return jnp.sum((blocks[:, None] >= ends[None, :]).astype(jnp.int32), axis=1)


def attend_block(query_block, query_index, buffer, base, documents, mask_rows):
    count = documents.shape[0]
    group = QH // KVH
    slots = buffer.shape[0]
    scale = 1.0 / math.sqrt(HD)
    heads = query_block.reshape(BLK, KVH, group, HD)
    gate_row = lax.dynamic_index_in_dim(mask_rows, query_index, 0, keepdims=False)
    gates = jnp.concatenate([gate_row[::-1], jnp.ones((1,), jnp.int32)])
    key_index = query_index - (MAXDOC - 1) + jnp.arange(MAXDOC, dtype=jnp.int32)
    key_docs = jnp.where(key_index >= 0, documents[jnp.clip(key_index, 0, count - 1)], -1)
    allowed = (key_docs == documents[query_index]) & (gates == 1)
    places = jnp.arange(BLK, dtype=jnp.int32)
    causal = places[None, :] <= places[:, None]

    def fetch(step):
        local = jnp.clip(key_index[step] - base, 0, slots - 1)
        return lax.dynamic_index_in_dim(buffer, local, 0, keepdims=False)

    def find_scores(step, carry):

        def compute(state):
            table, running = state
            keys = fetch(step)[:, : KVH * HD].reshape(BLK, KVH, HD)
            scores = (
                jnp.einsum("ikgd,lkd->kgil", heads, keys, preferred_element_type=jnp.float32)
                * scale
            )
            keep = jnp.logical_or(step < MAXDOC - 1, causal)
            scores = jnp.where(keep[None, None], scores, -jnp.inf)
            table = lax.dynamic_update_index_in_dim(table, scores, step, 0)
            return (table, jnp.maximum(running, jnp.max(scores, axis=-1)))

        return lax.cond(allowed[step], compute, lambda state: state, carry)

    table = jnp.full((MAXDOC, KVH, group, BLK, BLK), -jnp.inf, jnp.float32)
    running = jnp.full((KVH, group, BLK), -jnp.inf, jnp.float32)
    table, rowmax = lax.fori_loop(0, MAXDOC, find_scores, (table, running))

    def accumulate(step, carry):

        def add(state):
            total, summed = state
            values = fetch(step)[:, KVH * HD :].reshape(BLK, KVH, HD)
            scores = lax.dynamic_index_in_dim(table, step, 0, keepdims=False)
            weights = jnp.exp(scores - rowmax[..., None])
            total = total + jnp.sum(weights, axis=-1)
            summed = summed + jnp.einsum(
                "kgil,lkd->kgid",
                weights.astype(jnp.bfloat16),
                values,
                preferred_element_type=jnp.float32,
            )
            return (total, summed)

        return lax.cond(allowed[step], add, lambda state: state, carry)

    start = (
        jnp.zeros((KVH, group, BLK), jnp.float32),
        jnp.zeros((KVH, group, BLK, HD), jnp.float32),
    )
    total, summed = lax.fori_loop(0, MAXDOC, accumulate, start)
    out = (
        (summed / total[..., None]).transpose(2, 0, 1, 3).reshape(BLK, QH * HD).astype(jnp.bfloat16)
    )
    stats = (rowmax + jnp.log(total)).reshape(QH, BLK)
    return (out, stats)


def body(tokens, queries, kv_weight, doc_blocks, block_mask, plan):
    local_tokens = tokens[0]
    columns = lax.all_gather(kv_weight, "dp", axis=1, tiled=True)
    projected = jnp.dot(
        local_tokens,
        lax.all_gather(columns, "ctx", axis=0, tiled=True),
        preferred_element_type=jnp.float32,
    ).astype(jnp.bfloat16)
    blocks_dev = local_tokens.shape[0] // BLK
    width = projected.shape[1]
    own_pairs = projected.reshape(blocks_dev, BLK, width)
    count = plan.shape[1]
    documents = document_of_blocks(doc_blocks[0], count)
    mask_rows = block_mask[0]
    plan_row = plan[0]
    device = lax.axis_index("ctx")
    first = device * blocks_dev
    local_ids = first + jnp.arange(blocks_dev, dtype=jnp.int32)
    every_block = jnp.arange(count, dtype=jnp.int32)
    sources = jnp.sum(
        jnp.where(plan_row[None, :] == local_ids[:, None], every_block[None, :], 0), axis=1
    )
    source_picks = jnp.where(sources // blocks_dev == device, 0, blocks_dev) + sources % blocks_dev
    own_queries = queries[0].reshape(blocks_dev, BLK, queries.shape[2])
    reach = (MAXDOC + blocks_dev - 2) // blocks_dev
    partner_queries = from_partner(own_queries, "ctx", 0)
    partner_pairs = from_partner(own_pairs, "ctx", 0)
    odd = device % 2
    pair_kv = jnp.where(
        odd == 0,
        jnp.concatenate([own_pairs, partner_pairs], axis=0),
        jnp.concatenate([partner_pairs, own_pairs], axis=0),
    )
    pair_reach = (reach + 1) // 2
    behind = [passed_along(pair_kv, "ctx", 2 * step) for step in range(pair_reach, 0, -1)]
    buffer = jnp.concatenate(behind + [pair_kv], axis=0)
    base = (device - odd - 2 * pair_reach) * blocks_dev
    candidates = jnp.concatenate([own_queries, partner_queries], axis=0)
    chosen = jnp.take(candidates, source_picks, axis=0)

    def run_planned(item):
        return attend_block(item[0], item[1], buffer, base, documents, mask_rows)

    planned_out, stats_blocks = lax.map(run_planned, (chosen, sources))
    partner_out = from_partner(planned_out, "ctx", 0)
    targets = lax.dynamic_slice_in_dim(plan_row, first, blocks_dev, 0)
    target_picks = jnp.where(targets // blocks_dev == device, 0, blocks_dev) + targets % blocks_dev
    returned = jnp.concatenate([planned_out, partner_out], axis=0)
    attended = jnp.take(returned, target_picks, axis=0)
    attended = attended.reshape(1, blocks_dev * BLK, attended.shape[2])
    stats = stats_blocks.transpose(1, 0, 2).reshape(1, QH, blocks_dev * BLK)
    return (attended, stats)


def solution(mesh):
    in_specs = (
        P("dp", "ctx", None),
        P("dp", "ctx", None),
        P("ctx", "dp"),
        P("dp", None),
        P("dp", None, None),
        P("dp", None),
    )
    out_specs = (P("dp", "ctx", None), P("dp", None, "ctx"))
    return jax.shard_map(body, mesh=mesh, in_specs=in_specs, out_specs=out_specs, check_vma=False)
```

profile of v0, /device:TPU:9, one launch (start us, length us, event | category | flops | bytes accessed | tf_op | source)
XLA Modules:
  0.0 434.4 jit_solution(18178212177853257397)
XLA Ops:
  8.0 29.6 %all-gather.3.cloned.1.call-done = bf16[512,1024]{1,0:T(8,128)(2,1)} async-done(((bf16[512,256]{1,0:T(8,128)(2,1)}), bf16[512,1024]{1,0:T(8,128)(2,1)}) %all-gather.3.cloned.1.call-update) | async-done | bytes 1048592 | tf_op jit(solution)/shard_map/all_gather | solution.py:107
  37.6 81.4 %all-gather.5.cloned.1.call-done = bf16[4096,1024]{1,0:T(8,128)(2,1)} async-done(((bf16[512,1024]{1,0:T(8,128)(2,1)}), bf16[4096,1024]{1,0:T(8,128)(2,1)}) %all-gather.5.cloned.1.call-update) | async-done | bytes 8388624 | tf_op jit(solution)/shard_map/all_gather | solution.py:110
  119.0 5.7 %fusion.19 = bf16[256,1024]{1,0:T(8,128)(2,1)S(1)} fusion(bf16[4096,1024]{1,0:T(8,128)(2,1)} %all-gather.5.cloned.1.call-done, bf16[1,256,4096]{2,1,0:T(8,128)(2,1)S(1)} %copy-done), kind=kOutput, calls=%fused_computation.40 | convolution fusion | flops 2147745792 | bytes 11010048 | tf_op jit(solution)/shard_map/dot_general | solution.py:108
  128.1 4.9 %collective-permute-start.2 = (bf16[4,128,1024]{1,2,0:T(8,128)(2,1)}, bf16[4,128,1024]{1,2,0:T(8,128)(2,1)}, u32[]{:S(2)}, u32[]{:S(2)}) collective-permute-start(bf16[4,128,1024]{1,2,0:T(8,128)(2,1)} %maximum_select_fusion), channel_id=1, source_target_pairs={{0,4},{1,5},{2,6},{3,7},{8,12},{9,13},{10,14},{11,15},{16,20},{17,... | collective-permute-start | bytes 3145736 | tf_op jit(solution)/shard_map/ppermute | solution.py:28
  141.8 35.3 %collective-permute-done.2 = bf16[4,128,1024]{1,2,0:T(8,128)(2,1)} collective-permute-done((bf16[4,128,1024]{1,2,0:T(8,128)(2,1)}, bf16[4,128,1024]{1,2,0:T(8,128)(2,1)}, u32[]{:S(2)}, u32[]{:S(2)}) %collective-permute-start.2) | collective-permute-done | bytes 1048608 | tf_op jit(solution)/shard_map/ppermute | solution.py:28
  177.1 22.5 %collective-permute-done.3 = bf16[4,128,1024]{1,2,0:T(8,128)(2,1)} collective-permute-done((bf16[4,128,1024]{1,2,0:T(8,128)(2,1)}, bf16[4,128,1024]{1,2,0:T(8,128)(2,1)}, u32[]{:S(2)}, u32[]{:S(2)}) %collective-permute-start.3) | collective-permute-done | bytes 1048608 | tf_op jit(solution)/shard_map/ppermute | solution.py:28
  202.8 161.6 %while.68 = (s32[]{:T(128)}, bf16[2,128,2048]{2,1,0:T(8,128)(2,1)}, f32[2,16,128]{2,1,0:T(8,128)S(1)}, s32[2]{0:T(128)S(1)}, s32[16]{0:T(128)S(1)}, /*index=5*/s...) while((s32[]{:T(128)}, bf16[2,128,2048]{2,1,0:T(8,128)(2,1)}, ...), condition=%wide.region_14.16_spmd, body=%wide.region_3.15_spmd.sunk | while | flops 136875136 | bytes 44226652 | solution.py:148
  214.6 14.1 %while.69 = (s32[]{:T(128)}, f32[8,4,4,128,128]{3,4,2,1,0:T(8,128)}, f32[4,4,128]{2,1,0:T(4,128)S(1)}, pred[8]{0:T(512)(128)(4,1)S(1)}, s32[]{:T(128)}, /*index=...) while((s32[]{:T(128)}, ...), condition=%wide.region_8.9_spmd.clone, body=%wide.region_4.8_spmd.clone.sunk | while | flops 67928080 | bytes 4915628 | solution.py:73
  228.8 9.2 %copy.58 = f32[8,4,4,128,128]{4,3,2,1,0:T(8,128)} copy(f32[8,4,4,128,128]{3,4,2,1,0:T(8,128)} %get-tuple-element.908) | data formatting | bytes 16777216 | tf_op jit(solution)/shard_map/while
  238.1 16.7 %while.70 = (s32[]{:T(128)}, f32[4,4,128]{2,1,0:T(4,128)S(1)}, f32[4,4,128,128]{3,2,1,0:T(8,128)S(1)}, pred[8]{0:T(512)(128)(4,1)S(1)}, f32[8,4,4,128,128]{4,3,2...) while((s32[]{:T(128)}, f32[4,4,128]{2,1,0:T(4,128)S(1)}, ...), condition=%wide.region_13.14_spmd.clone, body=%wide.region_9.13_spmd.clone.sunk | while | flops 68419600 | bytes 5161378 | solution.py:97
  248.7 6.1 %conditional.7 = ((f32[4,4,128]{2,1,0:T(4,128)S(1)}, f32[4,4,128,128]{3,2,1,0:T(8,128)S(1)})) conditional(s32[]{:T(128)} %bitcast.104, (f32[4,4,128]{2,1,0:T(4,128)S(1)}, f32[4,4,128,128]{3,2,1,0:T(8,128)S(1)}) %tuple.135, (s32[]{:T(128)}, f32[8,4,4,128,128]{4,3,2,1,0:T(8,128)}, f32[4,4,128]{2,1,0:T(4,128)S(1)}, f32[4,4,128]{2,1,0:T(4,128)S(1)}, ...), branch_computations={%region_10.10_spmd, %region_11.12_spmd} | conditional | flops 68419600 | bytes 5161146 | solution.py:91
  268.7 37.4 %while.69 = (s32[]{:T(128)}, f32[8,4,4,128,128]{3,4,2,1,0:T(8,128)}, f32[4,4,128]{2,1,0:T(4,128)S(1)}, pred[8]{0:T(512)(128)(4,1)S(1)}, s32[]{:T(128)}, /*index=...) while((s32[]{:T(128)}, ...), condition=%wide.region_8.9_spmd.clone, body=%wide.region_4.8_spmd.clone.sunk | while | flops 67928080 | bytes 4915628 | solution.py:73
  272.2 4.7 %conditional.6 = ((f32[8,4,4,128,128]{3,4,2,1,0:T(8,128)}, f32[4,4,128]{2,1,0:T(4,128)S(1)})) conditional(s32[]{:T(128)} %bitcast.103, (f32[8,4,4,128,128]{3,4,2,1,0:T(8,128)}, f32[4,4,128]{2,1,0:T(4,128)S(1)}) %tuple.132, (s32[]{:T(128)}, s32[128,128]{0,1:T(8,128)S(1)}, s32[]{:T(128)}, s32[]{:T(128)}, bf16[12,128,1024]{1,2,0:T(8,128)(2,1)}, ...), branch_computations={%region_5.5_spmd, %region_6.7_spmd} | conditional | flops 67928080 | bytes 4784324 | solution.py:69
  278.0 4.7 %conditional.6 = ((f32[8,4,4,128,128]{3,4,2,1,0:T(8,128)}, f32[4,4,128]{2,1,0:T(4,128)S(1)})) conditional(s32[]{:T(128)} %bitcast.103, (f32[8,4,4,128,128]{3,4,2,1,0:T(8,128)}, f32[4,4,128]{2,1,0:T(4,128)S(1)}) %tuple.132, (s32[]{:T(128)}, s32[128,128]{0,1:T(8,128)S(1)}, s32[]{:T(128)}, s32[]{:T(128)}, bf16[12,128,1024]{1,2,0:T(8,128)(2,1)}, ...), branch_computations={%region_5.5_spmd, %region_6.7_spmd} | conditional | flops 67928080 | bytes 4784324 | solution.py:69
  283.9 4.7 %conditional.6 = ((f32[8,4,4,128,128]{3,4,2,1,0:T(8,128)}, f32[4,4,128]{2,1,0:T(4,128)S(1)})) conditional(s32[]{:T(128)} %bitcast.103, (f32[8,4,4,128,128]{3,4,2,1,0:T(8,128)}, f32[4,4,128]{2,1,0:T(4,128)S(1)}) %tuple.132, (s32[]{:T(128)}, s32[128,128]{0,1:T(8,128)S(1)}, s32[]{:T(128)}, s32[]{:T(128)}, bf16[12,128,1024]{1,2,0:T(8,128)(2,1)}, ...), branch_computations={%region_5.5_spmd, %region_6.7_spmd} | conditional | flops 67928080 | bytes 4784324 | solution.py:69
  306.1 9.2 %copy.58 = f32[8,4,4,128,128]{4,3,2,1,0:T(8,128)} copy(f32[8,4,4,128,128]{3,4,2,1,0:T(8,128)} %get-tuple-element.908) | data formatting | bytes 16777216 | tf_op jit(solution)/shard_map/while
  315.4 46.9 %while.70 = (s32[]{:T(128)}, f32[4,4,128]{2,1,0:T(4,128)S(1)}, f32[4,4,128,128]{3,2,1,0:T(8,128)S(1)}, pred[8]{0:T(512)(128)(4,1)S(1)}, f32[8,4,4,128,128]{4,3,2...) while((s32[]{:T(128)}, f32[4,4,128]{2,1,0:T(4,128)S(1)}, ...), condition=%wide.region_13.14_spmd.clone, body=%wide.region_9.13_spmd.clone.sunk | while | flops 68419600 | bytes 5161378 | solution.py:97
  319.4 6.1 %conditional.7 = ((f32[4,4,128]{2,1,0:T(4,128)S(1)}, f32[4,4,128,128]{3,2,1,0:T(8,128)S(1)})) conditional(s32[]{:T(128)} %bitcast.104, (f32[4,4,128]{2,1,0:T(4,128)S(1)}, f32[4,4,128,128]{3,2,1,0:T(8,128)S(1)}) %tuple.135, (s32[]{:T(128)}, f32[8,4,4,128,128]{4,3,2,1,0:T(8,128)}, f32[4,4,128]{2,1,0:T(4,128)S(1)}, f32[4,4,128]{2,1,0:T(4,128)S(1)}, ...), branch_computations={%region_10.10_spmd, %region_11.12_spmd} | conditional | flops 68419600 | bytes 5161146 | solution.py:91
  326.7 6.1 %conditional.7 = ((f32[4,4,128]{2,1,0:T(4,128)S(1)}, f32[4,4,128,128]{3,2,1,0:T(8,128)S(1)})) conditional(s32[]{:T(128)} %bitcast.104, (f32[4,4,128]{2,1,0:T(4,128)S(1)}, f32[4,4,128,128]{3,2,1,0:T(8,128)S(1)}) %tuple.135, (s32[]{:T(128)}, f32[8,4,4,128,128]{4,3,2,1,0:T(8,128)}, f32[4,4,128]{2,1,0:T(4,128)S(1)}, f32[4,4,128]{2,1,0:T(4,128)S(1)}, ...), branch_computations={%region_10.10_spmd, %region_11.12_spmd} | conditional | flops 68419600 | bytes 5161146 | solution.py:91
  334.1 6.1 %conditional.7 = ((f32[4,4,128]{2,1,0:T(4,128)S(1)}, f32[4,4,128,128]{3,2,1,0:T(8,128)S(1)})) conditional(s32[]{:T(128)} %bitcast.104, (f32[4,4,128]{2,1,0:T(4,128)S(1)}, f32[4,4,128,128]{3,2,1,0:T(8,128)S(1)}) %tuple.135, (s32[]{:T(128)}, f32[8,4,4,128,128]{4,3,2,1,0:T(8,128)}, f32[4,4,128]{2,1,0:T(4,128)S(1)}, f32[4,4,128]{2,1,0:T(4,128)S(1)}, ...), branch_computations={%region_10.10_spmd, %region_11.12_spmd} | conditional | flops 68419600 | bytes 5161146 | solution.py:91
  341.5 6.1 %conditional.7 = ((f32[4,4,128]{2,1,0:T(4,128)S(1)}, f32[4,4,128,128]{3,2,1,0:T(8,128)S(1)})) conditional(s32[]{:T(128)} %bitcast.104, (f32[4,4,128]{2,1,0:T(4,128)S(1)}, f32[4,4,128,128]{3,2,1,0:T(8,128)S(1)}) %tuple.135, (s32[]{:T(128)}, f32[8,4,4,128,128]{4,3,2,1,0:T(8,128)}, f32[4,4,128]{2,1,0:T(4,128)S(1)}, f32[4,4,128]{2,1,0:T(4,128)S(1)}, ...), branch_computations={%region_10.10_spmd, %region_11.12_spmd} | conditional | flops 68419600 | bytes 5161146 | solution.py:91
  348.9 6.1 %conditional.7 = ((f32[4,4,128]{2,1,0:T(4,128)S(1)}, f32[4,4,128,128]{3,2,1,0:T(8,128)S(1)})) conditional(s32[]{:T(128)} %bitcast.104, (f32[4,4,128]{2,1,0:T(4,128)S(1)}, f32[4,4,128,128]{3,2,1,0:T(8,128)S(1)}) %tuple.135, (s32[]{:T(128)}, f32[8,4,4,128,128]{4,3,2,1,0:T(8,128)}, f32[4,4,128]{2,1,0:T(4,128)S(1)}, f32[4,4,128]{2,1,0:T(4,128)S(1)}, ...), branch_computations={%region_10.10_spmd, %region_11.12_spmd} | conditional | flops 68419600 | bytes 5161146 | solution.py:91
  356.2 6.1 %conditional.7 = ((f32[4,4,128]{2,1,0:T(4,128)S(1)}, f32[4,4,128,128]{3,2,1,0:T(8,128)S(1)})) conditional(s32[]{:T(128)} %bitcast.104, (f32[4,4,128]{2,1,0:T(4,128)S(1)}, f32[4,4,128,128]{3,2,1,0:T(8,128)S(1)}) %tuple.135, (s32[]{:T(128)}, f32[8,4,4,128,128]{4,3,2,1,0:T(8,128)}, f32[4,4,128]{2,1,0:T(4,128)S(1)}, f32[4,4,128]{2,1,0:T(4,128)S(1)}, ...), branch_computations={%region_10.10_spmd, %region_11.12_spmd} | conditional | flops 68419600 | bytes 5161146 | solution.py:91
  364.3 54.6 %collective-permute-start.4 = (bf16[2,128,2048]{2,1,0:T(8,128)(2,1)}, bf16[2,128,2048]{2,1,0:T(8,128)(2,1)S(1)}, u32[]{:S(2)}, u32[]{:S(2)}) collective-permute-start(bf16[2,128,2048]{2,1,0:T(8,128)(2,1)} %get-tuple-element.515), channel_id=1, source_target_pairs={{0,1},{1,0},{2,3},{3,2},{4,5},{5,4},{6,7},{7,6},{8,9},{9,8},{10,11... | collective-permute-start | bytes 3145736 | tf_op jit(solution)/shard_map/ppermute | solution.py:22
  (305 shorter events, 151.9 us)
Async XLA Ops:
  7.2 111.8 %copy-start = (bf16[1,256,4096]{2,1,0:T(8,128)(2,1)S(1)}, bf16[1,256,4096]{2,1,0:T(8,128)(2,1)}, u32[]{:S(2)}) copy-start(bf16[1,256,4096]{2,1,0:T(8,128)(2,1)} %param.18) | copy-start | bytes 6291460
  7.2 30.3 %all-gather.3.cloned.1.call-start = ((), (), s32[]{:S(2)}) async-start(), calls=%async_computation | async-start | bytes 1310720 | tf_op jit(solution)/shard_map/all_gather | solution.py:107
  7.9 111.1 %all-gather.5.cloned.1.call-start = ((), (), s32[]{:S(2)}) async-start(), calls=%async_computation.1 | async-start | bytes 9437184 | tf_op jit(solution)/shard_map/all_gather | solution.py:110
  37.5 88.0 %copy-start.2 = (s32[1,16]{1,0:T(1,128)S(1)}, s32[1,16]{1,0:T(1,128)}, u32[]{:S(2)}) copy-start(s32[1,16]{1,0:T(1,128)} %param.23) | copy-start | bytes 196
  124.7 10.3 %copy-start.1 = (s32[1,16,7]{1,0,2:T(1,128)S(1)}, s32[1,16,7]{1,0,2:T(1,128)}, u32[]{:S(2)}) copy-start(s32[1,16,7]{1,0,2:T(1,128)} %param.22) | copy-start | bytes 1348
  124.7 10.4 %copy-start.3 = (s32[1,4]{1,0:T(1,128)S(1)}, s32[1,4]{1,0:T(1,128)}, u32[]{:S(2)}) copy-start(s32[1,4]{1,0:T(1,128)} %param.21) | copy-start | bytes 52
  125.0 2.0 collective-permute-start.1
  125.3 10.0 %collective-permute-start = (bf16[2,128,2048]{2,1,0:T(8,128)(2,1)}, bf16[2,128,2048]{2,1,0:T(8,128)(2,1)}, u32[]{:S(2)}, u32[]{:S(2)}) collective-permute-start(bf16[2,128,2048]{2,1,0:T(8,128)(2,1)} %bitcast.111), channel_id=1, source_target_pairs={{0,1},{1,0},{2,3},{3,2},{4,5},{5,4},{6,7},{7,6},{8,9},{9,8},{10,11... | collective-permute-start | bytes 3145736 | tf_op jit(solution)/shard_map/ppermute | solution.py:22
  128.1 49.0 %collective-permute-start.2 = (bf16[4,128,1024]{1,2,0:T(8,128)(2,1)}, bf16[4,128,1024]{1,2,0:T(8,128)(2,1)}, u32[]{:S(2)}, u32[]{:S(2)}) collective-permute-start(bf16[4,128,1024]{1,2,0:T(8,128)(2,1)} %maximum_select_fusion), channel_id=1, source_target_pairs={{0,4},{1,5},{2,6},{3,7},{8,12},{9,13},{10,14},{11,15},{16,20},{17,... | collective-permute-start | bytes 3145736 | tf_op jit(solution)/shard_map/ppermute | solution.py:28
  133.0 66.6 %collective-permute-start.3 = (bf16[4,128,1024]{1,2,0:T(8,128)(2,1)}, bf16[4,128,1024]{1,2,0:T(8,128)(2,1)}, u32[]{:S(2)}, u32[]{:S(2)}) collective-permute-start(bf16[4,128,1024]{1,2,0:T(8,128)(2,1)} %maximum_select_fusion), channel_id=1, source_target_pairs={{0,2},{1,3},{2,4},{3,5},{4,6},{5,7},{8,10},{9,11},{10,12},{11,13},... | collective-permute-start | bytes 3145736 | tf_op jit(solution)/shard_map/ppermute | solution.py:28
  364.3 57.1 %collective-permute-start.4 = (bf16[2,128,2048]{2,1,0:T(8,128)(2,1)}, bf16[2,128,2048]{2,1,0:T(8,128)(2,1)S(1)}, u32[]{:S(2)}, u32[]{:S(2)}) collective-permute-start(bf16[2,128,2048]{2,1,0:T(8,128)(2,1)} %get-tuple-element.515), channel_id=1, source_target_pairs={{0,1},{1,0},{2,3},{3,2},{4,5},{5,4},{6,7},{7,6},{8,9},{9,8},{10,11... | collective-permute-start | bytes 3145736 | tf_op jit(solution)/shard_map/ppermute | solution.py:22
Sparse Core Ops, SparseCore 0:
  9.8 27.6 all-gather.2
  39.1 79.8 all-gather.4
where the time goes:
time: 432 us; the launch traced here: 434 us
  waiting for transfers between devices  172 us (40%)
  local copies, waits for them, and re-layouts  86.5 us (20%)
  starting transfers between devices  62.1 us (14%)
  matrix products  35.5 us (8%)
  loops' own time  34.7 us (8%)
  other arithmetic  29 us (7%)
  between operations  14.2 us (3%)
    all_gather x1, waiting for transfers between devices, body(): lax.all_gather(columns, 'ctx', axis=0, tiled=True)  81.4 us
    ppermute x2, waiting for transfers between devices, passed_along(): return lax.ppermute(array, axis, pairs)  57.8 us
    ppermute x3, starting transfers between devices, from_partner(): return lax.ppermute(block, axis, route)  55.2 us
    all_gather x1, waiting for transfers between devices, body(): columns = lax.all_gather(kv_weight, 'dp', axis=1, tiled=True)  29.6 us
    while x4, local copies, waits for them, and re-layouts  20.5 us
    dot_general x7, matrix products, compute(): jnp.einsum('ikgd,lkd->kgil', heads, keys, preferred_element_type=jnp.floa...  16.8 us
    squeeze x14, local copies, waits for them, and re-layouts, fetch(): return lax.dynamic_index_in_dim(buffer, local, 0, keepdims=False)  13.6 us
    reduce_sum x7, other arithmetic, add(): total = total + jnp.sum(weights, axis=-1)  13.1 us
  transfers between devices with their start and end apart: 7, of which 6 were waited for; matrix products, arithmetic and copies ran while one was open for 2% of the time, Pallas kernels for 0%

commit v1 on v0

v1 whole, which is shorter than its diff:
```python
import functools
import math

import jax
import jax.numpy as jnp
from jax import lax
from jax.experimental import pallas as pl
from jax.experimental.pallas import tpu as pltpu
from jax.sharding import PartitionSpec as P

HD = 128
QH = 16
KVH = 4
BLK = 128
MAXDOC = 8
GROUP = QH // KVH
LANES = GROUP * BLK
VMEM_LIMIT = 48 * 1024 * 1024
SCALE = 1.0 / math.sqrt(HD)
LOG2E = 1.0 / math.log(2.0)


def over_dp(array, mask):
    return lax.ppermute(array, "dp", [(i, i ^ mask) for i in range(lax.axis_size("dp"))])


def other_core(array):
    return lax.ppermute(array, "ctx", [(i, i ^ 1) for i in range(lax.axis_size("ctx"))])


def around(array, pairs):
    size = lax.axis_size("ctx")
    return lax.ppermute(array, "ctx", [(i, (i + 2 * pairs) % size) for i in range(size)])


def ahead(array, pairs):
    size = lax.axis_size("ctx")
    return lax.ppermute(array, "ctx", [(i, i + 2 * pairs) for i in range(size - 2 * pairs)])


def project_kernel(slots, own_ref, other_ref, *refs):
    weights, out_ref = refs[:-1], refs[-1]
    device = lax.axis_index("ctx")
    core, pair = device % 2, device // 2
    rows = own_ref.shape[0]
    depth = weights[0].shape[0] // 2
    for tokens_ref, place in ((own_ref, core), (other_ref, 1 - core)):
        total = jnp.zeros((rows, HD), jnp.float32)
        for step, weight in enumerate(weights):
            source = lax.rem(pair + slots - step, slots)
            for half in range(2):
                group = 2 * source + (core + half) % 2
                columns = pl.ds(pl.multiple_of(group * depth, depth), depth)
                total += jnp.dot(
                    tokens_ref[:, columns],
                    weight[half * depth : (half + 1) * depth, :],
                    preferred_element_type=jnp.float32,
                )
        out_ref[pl.ds(pl.multiple_of(place * rows, rows), rows), :] = total.astype(jnp.bfloat16)


def project(own, other, weights):
    rows, width = own.shape
    spec = pl.BlockSpec(memory_space=pltpu.VMEM)
    return pl.pallas_call(
        functools.partial(project_kernel, len(weights)),
        out_shape=jax.ShapeDtypeStruct((2 * rows, HD), jnp.bfloat16),
        in_specs=[spec] * (2 + len(weights)),
        out_specs=spec,
        compiler_params=pltpu.CompilerParams(vmem_limit_bytes=VMEM_LIMIT),
        cost_estimate=pl.CostEstimate(
            flops=8 * rows * width * HD, bytes_accessed=4 * rows * width, transcendentals=0
        ),
    )(own, other, *weights)


def attend_kernel(
    second,
    docs_ref,
    mask_ref,
    plan_ref,
    q_own_ref,
    q_other_ref,
    near_a,
    near_b,
    back_a,
    back_b,
    far_a,
    far_b,
    out_own,
    out_other,
    stats_own,
    stats_other,
    kv,
    table,
    top,
    total,
    summed,
):
    device = lax.axis_index("ctx")
    slice_of = lax.axis_index("dp")
    core, pair = device % 2, device // 2
    column, kind = slice_of % 2, slice_of // 2
    head_pair = (column + second) % 2
    head = 2 * head_pair + core
    pair_blocks = near_a.shape[0] // BLK
    far_blocks = far_a.shape[0] // BLK
    dev_blocks = pair_blocks // 2
    count = plan_ref.shape[1]
    documents = docs_ref.shape[1]
    first = pair * pair_blocks
    own_row = (far_blocks + pair_blocks) * BLK
    for which, near, back, far in ((kind, near_a, back_a, far_a), (1 - kind, near_b, back_b, far_b)):
        kv[which, : far_blocks * BLK, :] = far[...]
        kv[which, far_blocks * BLK : own_row, :] = back[...]
        kv[which, own_row:, :] = near[...]
    causal = lax.broadcasted_iota(jnp.int32, (BLK, BLK), 0) <= lax.broadcasted_iota(
        jnp.int32, (BLK, BLK), 1
    )
    columns = pl.ds(pl.multiple_of(head * LANES, LANES), LANES)

    for is_own, q_ref, out_ref in ((1, q_own_ref, out_own), (0, q_other_ref, out_other)):
        owner = core if is_own else 1 - core
        for place in range(dev_blocks):
            index = owner * dev_blocks + place
            block = first + index
            rows = slice(place * BLK, (place + 1) * BLK)
            query = q_ref[rows, columns]
            stacked = jnp.concatenate(
                [query[:, g * HD : (g + 1) * HD] for g in range(GROUP)], axis=0
            )

            def ends(j, carry):
                end, start = carry
                end = end + docs_ref[0, j]
                return end, jnp.where(end <= block, end, start)

            _, start = lax.fori_loop(0, documents, ends, (jnp.int32(0), jnp.int32(0)))

            def row_of(back):
                return pl.multiple_of(own_row + (index - back) * BLK, BLK)

            def scores(back):
                keys = kv[0, pl.ds(row_of(back), BLK), :]
                return lax.dot_general(
                    keys, stacked, (((1,), (1,)), ((), ())), preferred_element_type=jnp.float32
                )

            def admitted(back):
                return jnp.logical_and(block - back >= start, mask_ref[0, block, back - 1] == 1)

            own_scores = jnp.where(jnp.tile(causal, (1, GROUP)), scores(0), -jnp.inf)
            table[0] = own_scores
            top[...] = jnp.max(own_scores, axis=0, keepdims=True)
            for back in range(1, MAXDOC):

                @pl.when(admitted(back))
                def _():
                    got = scores(back)
                    table[back] = got
                    top[...] = jnp.maximum(top[...], jnp.max(got, axis=0, keepdims=True))

            def weigh(back):
                weights = jnp.exp2((table[back] - top[...]) * (SCALE * LOG2E))
                values = kv[1, pl.ds(row_of(back), BLK), :]
                part = lax.dot_general(
                    values,
                    weights.astype(jnp.bfloat16),
                    (((0,), (0,)), ((), ())),
                    preferred_element_type=jnp.float32,
                )
                return jnp.sum(weights, axis=0, keepdims=True), part

            total[...], summed[...] = weigh(0)
            for back in range(1, MAXDOC):

                @pl.when(admitted(back))
                def _():
                    more, part = weigh(back)
                    total[...] += more
                    summed[...] += part

            result = summed[...] / total[...]
            for g in range(GROUP):
                out_ref[rows, g * HD : (g + 1) * HD] = (
                    result[:, g * BLK : (g + 1) * BLK].T.astype(jnp.bfloat16)
                )
            lse = top[...] * SCALE + jnp.log(total[...])
            slot = plan_ref[0, block] - first
            keep_here = slot // dev_blocks == core
            at = slot % dev_blocks

            @pl.when(keep_here)
            def _():
                for g in range(GROUP):
                    stats_own[at, g : g + 1, :] = lse[:, g * BLK : (g + 1) * BLK]

            @pl.when(jnp.logical_not(keep_here))
            def _():
                for g in range(GROUP):
                    stats_other[at, g : g + 1, :] = lse[:, g * BLK : (g + 1) * BLK]


def attend(second, docs, mask, plan, q_own, q_other, first_set, second_set):
    vmem = pl.BlockSpec(memory_space=pltpu.VMEM)
    smem = pl.BlockSpec(memory_space=pltpu.SMEM)
    rows = q_own.shape[0]
    dev_blocks = rows // BLK
    near_a, back_a, far_a = first_set
    near_b, back_b, far_b = second_set
    window = near_a.shape[0] + back_a.shape[0] + far_a.shape[0]
    out = jax.ShapeDtypeStruct((rows, LANES), jnp.bfloat16)
    stats = jax.ShapeDtypeStruct((dev_blocks, GROUP, BLK), jnp.float32)
    return pl.pallas_call(
        functools.partial(attend_kernel, second),
        out_shape=(out, out, stats, stats),
        in_specs=[smem] * 3 + [vmem] * 8,
        out_specs=(vmem,) * 4,
        scratch_shapes=[
            pltpu.VMEM((2, window, HD), jnp.bfloat16),
            pltpu.VMEM((MAXDOC, BLK, LANES), jnp.float32),
            pltpu.VMEM((1, LANES), jnp.float32),
            pltpu.VMEM((1, LANES), jnp.float32),
            pltpu.VMEM((HD, LANES), jnp.float32),
        ],
        compiler_params=pltpu.CompilerParams(vmem_limit_bytes=VMEM_LIMIT),
        cost_estimate=pl.CostEstimate(
            flops=2 * dev_blocks * MAXDOC * BLK * LANES * HD * 4,
            bytes_accessed=8 * rows * QH * HD,
            transcendentals=2 * dev_blocks * MAXDOC * BLK * LANES,
        ),
    )(docs, mask, plan, q_own, q_other, near_a, near_b, back_a, back_b, far_a, far_b)


def finish_kernel(
    own_a, own_b, got_a, got_b, st_own_a, st_own_b, st_got_a, st_got_b, out_ref, stats_ref
):
    core = lax.axis_index("ctx") % 2
    column = lax.axis_index("dp") % 2
    pieces = (
        (own_a, column, core),
        (own_b, 1 - column, core),
        (got_a, column, 1 - core),
        (got_b, 1 - column, 1 - core),
    )
    for piece, head_pair, side in pieces:
        head = 2 * head_pair + side
        out_ref[0, :, pl.ds(pl.multiple_of(head * LANES, LANES), LANES)] = piece[...]
    for head in range(KVH):
        is_a = head // 2 == column
        is_own = head % 2 == core
        own = jnp.where(is_a, st_own_a[...], st_own_b[...])
        got = jnp.where(is_a, st_got_a[...], st_got_b[...])
        lse = jnp.where(is_own, own, got)
        for place in range(lse.shape[0]):
            stats_ref[0, head * GROUP : (head + 1) * GROUP, place * BLK : (place + 1) * BLK] = lse[place]


def body(tokens, queries, kv_weight, doc_blocks, block_mask, plan):
    size = lax.axis_size("ctx")
    device = lax.axis_index("ctx")
    core = device % 2
    slots = size // 2
    own_tokens, own_queries = tokens[0], queries[0]
    rows = own_tokens.shape[0]
    other_weight = other_core(kv_weight)
    other_tokens = other_core(own_tokens)
    other_queries = other_core(own_queries)

    def my_half(array):
        return lax.dynamic_slice_in_dim(array, core * HD, HD, 1)

    mine = my_half(kv_weight)
    others = my_half(other_weight)
    if slots == 4:
        slab = jnp.concatenate([mine, others], axis=0)
        own_set = [slab] + [around(slab, step) for step in (1, 2, 3)]

        def multiply(weights):
            return project(own_tokens, other_tokens, weights)

        x_set = [over_dp(w, 1) for w in own_set]
        y_set = [over_dp(w, 2) for w in own_set]
        d_set = [over_dp(x_set[0], 2), over_dp(y_set[1], 1), over_dp(x_set[2], 2), over_dp(y_set[3], 1)]
    else:
        even = jnp.where(core == 0, mine, others)
        odd = jnp.where(core == 0, others, mine)
        groups = [list(range(0, size, 2)), list(range(1, size, 2))]
        slab = jnp.concatenate([even, odd], axis=0)
        own_set = lax.all_gather(slab, "ctx", axis=0, axis_index_groups=groups, tiled=True)
        pair_tokens = jnp.where(
            core == 0,
            jnp.concatenate([own_tokens, other_tokens], axis=0),
            jnp.concatenate([other_tokens, own_tokens], axis=0),
        )

        def multiply(weights):
            total = jnp.dot(pair_tokens, weights, preferred_element_type=jnp.float32)
            return total.astype(jnp.bfloat16)

        x_set = over_dp(own_set, 1)
        y_set = over_dp(own_set, 2)
        d_set = over_dp(x_set, 2)

    spare = 2 * rows // BLK - (MAXDOC - 1) % (2 * rows // BLK)

    def reach(near):
        return near, ahead(near, 1), ahead(near[spare * BLK :], 2)

    own_kv = reach(multiply(own_set))
    y_kv = reach(multiply(y_set))
    x_kv = reach(multiply(x_set))
    d_kv = reach(multiply(d_set))
    first = attend(0, doc_blocks, block_mask, plan, own_queries, other_queries, own_kv, y_kv)
    second = attend(1, doc_blocks, block_mask, plan, own_queries, other_queries, x_kv, d_kv)
    got_a, got_b = other_core(first[1]), other_core(second[1])
    st_got_a, st_got_b = other_core(first[3]), other_core(second[3])
    vmem = pl.BlockSpec(memory_space=pltpu.VMEM)
    return pl.pallas_call(
        finish_kernel,
        out_shape=(
            jax.ShapeDtypeStruct((1, rows, QH * HD), jnp.bfloat16),
            jax.ShapeDtypeStruct((1, QH, rows), jnp.float32),
        ),
        in_specs=[vmem] * 8,
        out_specs=(vmem, vmem),
        compiler_params=pltpu.CompilerParams(vmem_limit_bytes=VMEM_LIMIT),
    )(first[0], second[0], got_a, got_b, first[2], second[2], st_got_a, st_got_b)


def solution(mesh):
    in_specs = (
        P("dp", "ctx", None),
        P("dp", "ctx", None),
        P("ctx", "dp"),
        P("dp", None),
        P("dp", None, None),
        P("dp", None),
    )
    out_specs = (P("dp", "ctx", None), P("dp", None, "ctx"))
    return jax.shard_map(body, mesh=mesh, in_specs=in_specs, out_specs=out_specs, check_vma=False)
```

time: 432 us -> 114 us (0.26)
  the two profiles are of different devices: /device:TPU:9 before, /device:TPU:13 now
where the time goes in v1:
time: 114 us; the launch traced here: 115 us
  waiting for transfers between devices  41.2 us (36%)
  starting transfers between devices  39.8 us (35%)
  Pallas kernels  27.2 us (24%)
  local copies, waits for them, and re-layouts  6.06 us (5%)
    pallas_call x2, Pallas kernels, attend(): pl.pallas_call(functools.partial(attend_kernel, second), out_shape=(out,...  21.1 us
    ppermute x3, waiting for transfers between devices, around(): lax.ppermute(array, 'ctx', [(i, (i + 2 * pairs) % size) for i in range(si...  19.5 us
    ppermute x12, waiting for transfers between devices, over_dp(): lax.ppermute(array, 'dp', [(i, i ^ mask) for i in range(lax.axis_size('dp...  17.2 us
    ppermute x8, starting transfers between devices, ahead(): lax.ppermute(array, 'ctx', [(i, i + 2 * pairs) for i in range(size - 2 *...  14.1 us
    ppermute x7, starting transfers between devices, other_core(): lax.ppermute(array, 'ctx', [(i, i ^ 1) for i in range(lax.axis_size('ctx'...  12.2 us
    ppermute x12, starting transfers between devices, over_dp(): lax.ppermute(array, 'dp', [(i, i ^ mask) for i in range(lax.axis_size('dp...  9.7 us
    unnamed x17, local copies, waits for them, and re-layouts  5.11 us
    pallas_call x4, Pallas kernels, project(): pl.pallas_call(functools.partial(project_kernel, len(weights)), out_shape...  5 us
  transfers between devices with their start and end apart: 30, of which 11 were waited for; matrix products, arithmetic and copies ran while one was open for 1% of the time, Pallas kernels for 23%

profile of v1, /device:TPU:13, one launch (start us, length us, event | category | flops | bytes accessed | tf_op | source)
XLA Modules:
  0.0 115.2 jit_solution(18010110662198027340)
XLA Ops:
  2.4 3.4 %collective-permute-done.2 = bf16[512,256]{1,0:T(8,128)(2,1)S(1)} collective-permute-done((bf16[512,256]{1,0:T(8,128)(2,1)}, bf16[512,256]{1,0:T(8,128)(2,1)S(1)}, u32[]{:S(2)}, u32[]{:S(2)}) %collective-permute-start.2) | collective-permute-done | bytes 262176 | tf_op jit(solution)/shard_map/ppermute | solution.py:28
  5.8 1.3 %collective-permute-start.3 = (bf16[1024,128]{1,0:T(8,128)(2,1)S(1)}, bf16[1024,128]{1,0:T(8,128)(2,1)S(1)}, u32[]{:S(2)}, u32[]{:S(2)}) collective-permute-start(bf16[1024,128]{1,0:T(8,128)(2,1)S(1)} %pad_maximum_fusion.refs_0_), channel_id=1, source_target_pairs={{0,2},{1,3},{2,4},{3,5},{4,6},{5,7},{6,0},{7,1},{8,10},{9,11},{10,... | collective-permute-start | bytes 786440 | tf_op jit(solution)/shard_map/ppermute | solution.py:33
  8.2 1.4 %collective-permute-start.5 = (bf16[1024,128]{1,0:T(8,128)(2,1)S(1)}, bf16[1024,128]{1,0:T(8,128)(2,1)S(1)}, u32[]{:S(2)}, u32[]{:S(2)}) collective-permute-start(bf16[1024,128]{1,0:T(8,128)(2,1)S(1)} %pad_maximum_fusion.refs_0_), channel_id=1, source_target_pairs={{0,6},{1,7},{2,0},{3,1},{4,2},{5,3},{6,4},{7,5},{8,14},{9,15},{10,... | collective-permute-start | bytes 786440 | tf_op jit(solution)/shard_map/ppermute | solution.py:33
  10.8 2.5 %collective-permute-done.3.refs_1_ = bf16[1024,128]{1,0:T(8,128)(2,1)S(1)} collective-permute-done((bf16[1024,128]{1,0:T(8,128)(2,1)S(1)}, bf16[1024,128]{1,0:T(8,128)(2,1)S(1)}, u32[]{:S(2)}, u32[]{:S(2)}) %collective-permute-start.3) | collective-permute-done | bytes 262176 | tf_op jit(solution)/shard_map/ppermute | solution.py:33
  13.6 15.7 %collective-permute-done.4.refs_2_ = bf16[1024,128]{1,0:T(8,128)(2,1)S(1)} collective-permute-done((bf16[1024,128]{1,0:T(8,128)(2,1)S(1)}, bf16[1024,128]{1,0:T(8,128)(2,1)S(1)}, u32[]{:S(2)}, u32[]{:S(2)}) %collective-permute-start.4) | collective-permute-done | bytes 262176 | tf_op jit(solution)/shard_map/ppermute | solution.py:33
  30.5 1.3 %collective-permute-done.5.refs_3_ = bf16[1024,128]{1,0:T(8,128)(2,1)S(1)} collective-permute-done((bf16[1024,128]{1,0:T(8,128)(2,1)S(1)}, bf16[1024,128]{1,0:T(8,128)(2,1)S(1)}, u32[]{:S(2)}, u32[]{:S(2)}) %collective-permute-start.5) | collective-permute-done | bytes 262176 | tf_op jit(solution)/shard_map/ppermute | solution.py:33
  34.1 1.8 %collective-permute-done.16.refs_2_ = bf16[1024,128]{1,0:T(8,128)(2,1)S(1)} collective-permute-done((bf16[1024,128]{1,0:T(8,128)(2,1)S(1)}, bf16[1024,128]{1,0:T(8,128)(2,1)S(1)}, u32[]{:S(2)}, u32[]{:S(2)}) %collective-permute-start.16) | collective-permute-done | bytes 262176 | tf_op jit(solution)/shard_map/ppermute | solution.py:24
  37.1 2.1 %collective-permute-done.9.refs_3_ = bf16[1024,128]{1,0:T(8,128)(2,1)S(1)} collective-permute-done((bf16[1024,128]{1,0:T(8,128)(2,1)S(1)}, bf16[1024,128]{1,0:T(8,128)(2,1)S(1)}, u32[]{:S(2)}, u32[]{:S(2)}) %collective-permute-start.9) | collective-permute-done | bytes 262176 | tf_op jit(solution)/shard_map/ppermute | solution.py:24
  39.4 5.4 %collective-permute-done.18.refs_0_ = bf16[1024,128]{1,0:T(8,128)(2,1)S(1)} collective-permute-done((bf16[1024,128]{1,0:T(8,128)(2,1)S(1)}, bf16[1024,128]{1,0:T(8,128)(2,1)S(1)}, u32[]{:S(2)}, u32[]{:S(2)}) %collective-permute-start.18) | collective-permute-done | bytes 262176 | tf_op jit(solution)/shard_map/ppermute | solution.py:24
  46.3 4.1 %collective-permute-done.20.refs_2_ = bf16[1024,128]{1,0:T(8,128)(2,1)S(1)} collective-permute-done((bf16[1024,128]{1,0:T(8,128)(2,1)S(1)}, bf16[1024,128]{1,0:T(8,128)(2,1)S(1)}, u32[]{:S(2)}, u32[]{:S(2)}) %collective-permute-start.20) | collective-permute-done | bytes 262176 | tf_op jit(solution)/shard_map/ppermute | solution.py:24
  53.1 1.6 %copy-done = bf16[1,256,4096]{2,1,0:T(8,128)(2,1)S(1)} copy-done((bf16[1,256,4096]{2,1,0:T(8,128)(2,1)S(1)}, bf16[1,256,4096]{2,1,0:T(8,128)(2,1)}, u32[]{:S(2)}) %copy-start) | copy-done | bytes 2097176
  56.0 1.9 %collective-permute-start.23 = (bf16[512,128]{1,0:T(8,128)(2,1)S(1)}, bf16[512,128]{1,0:T(8,128)(2,1)S(1)}, u32[]{:S(2)}, u32[]{:S(2)}) collective-permute-start(bf16[512,128]{1,0:T(8,128)(2,1)S(1)} %shard_map.81.near_b), channel_id=1, source_target_pairs={{0,2},{1,3},{2,4},{3,5},{4,6},{5,7},{8,10},{9,11},{10,12},{11,13},... | collective-permute-start | bytes 393224 | tf_op jit(solution)/shard_map/ppermute | solution.py:38
  57.9 3.7 %collective-permute-done.17.refs_3_ = bf16[1024,128]{1,0:T(8,128)(2,1)S(1)} collective-permute-done((bf16[1024,128]{1,0:T(8,128)(2,1)S(1)}, bf16[1024,128]{1,0:T(8,128)(2,1)S(1)}, u32[]{:S(2)}, u32[]{:S(2)}) %collective-permute-start.17) | collective-permute-done | bytes 262176 | tf_op jit(solution)/shard_map/ppermute | solution.py:24
  62.8 1.9 %collective-permute-start.22 = (bf16[512,128]{1,0:T(8,128)(2,1)S(1)}, bf16[512,128]{1,0:T(8,128)(2,1)S(1)}, u32[]{:S(2)}, u32[]{:S(2)}) collective-permute-start(bf16[512,128]{1,0:T(8,128)(2,1)S(1)} %shard_map.80.near_a), channel_id=1, source_target_pairs={{0,2},{1,3},{2,4},{3,5},{4,6},{5,7},{8,10},{9,11},{10,12},{11,13},... | collective-permute-start | bytes 393224 | tf_op jit(solution)/shard_map/ppermute | solution.py:38
  66.1 1.3 %collective-permute-start.25 = (bf16[384,128]{1,0:T(8,128)(2,1)S(1)}, bf16[384,128]{1,0:T(8,128)(2,1)S(1)}, u32[]{:S(2)}, u32[]{:S(2)}) collective-permute-start(bf16[384,128]{1,0:T(8,128)(2,1)S(1)} %slice.19), channel_id=1, source_target_pairs={{0,4},{1,5},{2,6},{3,7},{8,12},{9,13},{10,14},{11,15},{16,20},{17,... | collective-permute-start | bytes 294920 | tf_op jit(solution)/shard_map/ppermute | solution.py:38
  67.4 1.3 %collective-permute-start.24 = (bf16[384,128]{1,0:T(8,128)(2,1)S(1)}, bf16[384,128]{1,0:T(8,128)(2,1)S(1)}, u32[]{:S(2)}, u32[]{:S(2)}) collective-permute-start(bf16[384,128]{1,0:T(8,128)(2,1)S(1)} %slice.18), channel_id=1, source_target_pairs={{0,4},{1,5},{2,6},{3,7},{8,12},{9,13},{10,14},{11,15},{16,20},{17,... | collective-permute-start | bytes 294920 | tf_op jit(solution)/shard_map/ppermute | solution.py:38
  68.7 1.3 %shard_map.78.near_b = bf16[512,128]{1,0:T(8,128)(2,1)S(1)} custom-call(bf16[256,4096]{1,0:T(8,128)(2,1)S(1)} %bitcast.6, bf16[256,4096]{1,0:T(8,128)(2,1)S(1)} %collective-permute-done.1.other_ref, bf16[1024,128]{1,0:T(8,128)(2,1)S(1)} %collective-permute-done.6.refs_0_, bf16[1024,128]{1,0:T(8,128)(2,1)S(1)} %collective-permute-done.7.refs_1_, ...), custom_call_target="tpu_custom_call" | custom-call | flops 1073741824 | bytes 4194304 | tf_op jit(solution)/shard_map/pallas_call | solution.py:65
  70.9 1.9 %collective-permute-start.11 = (bf16[512,128]{1,0:T(8,128)(2,1)S(1)}, bf16[512,128]{1,0:T(8,128)(2,1)S(1)}, u32[]{:S(2)}, u32[]{:S(2)}) collective-permute-start(bf16[512,128]{1,0:T(8,128)(2,1)S(1)} %shard_map.78.near_b), channel_id=1, source_target_pairs={{0,2},{1,3},{2,4},{3,5},{4,6},{5,7},{8,10},{9,11},{10,12},{11,13},... | collective-permute-start | bytes 393224 | tf_op jit(solution)/shard_map/ppermute | solution.py:38
  72.9 1.9 %collective-permute-start.10 = (bf16[512,128]{1,0:T(8,128)(2,1)S(1)}, bf16[512,128]{1,0:T(8,128)(2,1)S(1)}, u32[]{:S(2)}, u32[]{:S(2)}) collective-permute-start(bf16[512,128]{1,0:T(8,128)(2,1)S(1)} %shard_map.77.near_a), channel_id=1, source_target_pairs={{0,2},{1,3},{2,4},{3,5},{4,6},{5,7},{8,10},{9,11},{10,12},{11,13},... | collective-permute-start | bytes 393224 | tf_op jit(solution)/shard_map/ppermute | solution.py:38
  74.9 2.5 %collective-permute-start.13 = (bf16[384,128]{1,0:T(8,128)(2,1)S(1)}, bf16[384,128]{1,0:T(8,128)(2,1)S(1)}, u32[]{:S(2)}, u32[]{:S(2)}) collective-permute-start(bf16[384,128]{1,0:T(8,128)(2,1)S(1)} %slice.17), channel_id=1, source_target_pairs={{0,4},{1,5},{2,6},{3,7},{8,12},{9,13},{10,14},{11,15},{16,20},{17,... | collective-permute-start | bytes 294920 | tf_op jit(solution)/shard_map/ppermute | solution.py:38
  77.5 1.3 %collective-permute-start.12 = (bf16[384,128]{1,0:T(8,128)(2,1)S(1)}, bf16[384,128]{1,0:T(8,128)(2,1)S(1)}, u32[]{:S(2)}, u32[]{:S(2)}) collective-permute-start(bf16[384,128]{1,0:T(8,128)(2,1)S(1)} %slice.16), channel_id=1, source_target_pairs={{0,4},{1,5},{2,6},{3,7},{8,12},{9,13},{10,14},{11,15},{16,20},{17,... | collective-permute-start | bytes 294920 | tf_op jit(solution)/shard_map/ppermute | solution.py:38
  81.3 10.6 %shard_map.82 = (bf16[256,512]{1,0:T(8,128)(2,1)S(1)}, bf16[256,512]{1,0:T(8,128)(2,1)S(1)}, f32[2,4,128]{2,1,0:T(4,128)S(1)}, f32[2,4,128]{2,1,0:T(4,128)S(1)}) custom-call(s32[1,4]{1,0:T(1,128)S(1)} %copy-done.5, s32[1,16,7]{2,1,0:T(8,128)S(1)} %copy.8.mask_ref, s32[1,16]{1,0:T(1,128)S(1)} %copy-done.6, bf16[256,2048]{1,0:T(8,128)(2,1)S(1)} %bitcast.8, ...), custom_call_target="tpu_custom_call" | custom-call | flops 1073741824 | bytes 4194304 | tf_op jit(solution)/shard_map/pallas_call | solution.py:214
  91.9 10.0 %collective-permute-start.27 = (bf16[256,512]{1,0:T(8,128)(2,1)S(1)}, bf16[256,512]{1,0:T(8,128)(2,1)S(1)}, u32[]{:S(2)}, u32[]{:S(2)}) collective-permute-start(bf16[256,512]{1,0:T(8,128)(2,1)S(1)} %get-tuple-element.13), channel_id=1, source_target_pairs={{0,1},{1,0},{2,3},{3,2},{4,5},{5,4},{6,7},{7,6},{8,9},{9,8},{10,11... | collective-permute-start | bytes 786440 | tf_op jit(solution)/shard_map/ppermute | solution.py:28
  101.9 10.5 %shard_map.79 = (bf16[256,512]{1,0:T(8,128)(2,1)S(1)}, bf16[256,512]{1,0:T(8,128)(2,1)S(1)}, f32[2,4,128]{2,1,0:T(4,128)S(1)}, f32[2,4,128]{2,1,0:T(4,128)S(1)}) custom-call(s32[1,4]{1,0:T(1,128)S(1)} %copy-done.5, s32[1,16,7]{2,1,0:T(8,128)S(1)} %copy.8.mask_ref, s32[1,16]{1,0:T(1,128)S(1)} %copy-done.6, bf16[256,2048]{1,0:T(8,128)(2,1)S(1)} %bitcast.9, ...), custom_call_target="tpu_custom_call" | custom-call | flops 1073741824 | bytes 4194304 | tf_op jit(solution)/shard_map/pallas_call | solution.py:214
  (67 shorter events, 23.5 us)
Async XLA Ops:
  0.6 51.2 %collective-permute-start.1 = (bf16[256,4096]{1,0:T(8,128)(2,1)}, bf16[256,4096]{1,0:T(8,128)(2,1)S(1)}, u32[]{:S(2)}, u32[]{:S(2)}) collective-permute-start(bf16[256,4096]{1,0:T(8,128)(2,1)} %bitcast.2), channel_id=1, source_target_pairs={{0,1},{1,0},{2,3},{3,2},{4,5},{5,4},{6,7},{7,6},{8,9},{9,8},{10,11... | collective-permute-start | bytes 6291464 | tf_op jit(solution)/shard_map/ppermute | solution.py:28
  5.8 7.6 %collective-permute-start.3 = (bf16[1024,128]{1,0:T(8,128)(2,1)S(1)}, bf16[1024,128]{1,0:T(8,128)(2,1)S(1)}, u32[]{:S(2)}, u32[]{:S(2)}) collective-permute-start(bf16[1024,128]{1,0:T(8,128)(2,1)S(1)} %pad_maximum_fusion.refs_0_), channel_id=1, source_target_pairs={{0,2},{1,3},{2,4},{3,5},{4,6},{5,7},{6,0},{7,1},{8,10},{9,11},{10,... | collective-permute-start | bytes 786440 | tf_op jit(solution)/shard_map/ppermute | solution.py:33
  7.1 22.2 %collective-permute-start.4 = (bf16[1024,128]{1,0:T(8,128)(2,1)S(1)}, bf16[1024,128]{1,0:T(8,128)(2,1)S(1)}, u32[]{:S(2)}, u32[]{:S(2)}) collective-permute-start(bf16[1024,128]{1,0:T(8,128)(2,1)S(1)} %pad_maximum_fusion.refs_0_), channel_id=1, source_target_pairs={{0,4},{1,5},{2,6},{3,7},{4,0},{5,1},{6,2},{7,3},{8,12},{9,13},{10,... | collective-permute-start | bytes 786440 | tf_op jit(solution)/shard_map/ppermute | solution.py:33
  8.2 23.6 %collective-permute-start.5 = (bf16[1024,128]{1,0:T(8,128)(2,1)S(1)}, bf16[1024,128]{1,0:T(8,128)(2,1)S(1)}, u32[]{:S(2)}, u32[]{:S(2)}) collective-permute-start(bf16[1024,128]{1,0:T(8,128)(2,1)S(1)} %pad_maximum_fusion.refs_0_), channel_id=1, source_target_pairs={{0,6},{1,7},{2,0},{3,1},{4,2},{5,3},{6,4},{7,5},{8,14},{9,15},{10,... | collective-permute-start | bytes 786440 | tf_op jit(solution)/shard_map/ppermute | solution.py:33
  9.6 22.4 %collective-permute-start.14 = (bf16[1024,128]{1,0:T(8,128)(2,1)S(1)}, bf16[1024,128]{1,0:T(8,128)(2,1)S(1)}, u32[]{:S(2)}, u32[]{:S(2)}) collective-permute-start(bf16[1024,128]{1,0:T(8,128)(2,1)S(1)} %pad_maximum_fusion.refs_0_), channel_id=1, source_target_pairs={{0,8},{8,0},{16,24},{24,16},{1,9},{9,1},{17,25},{25,17},{2,10},{10... | collective-permute-start | bytes 786440 | tf_op jit(solution)/shard_map/ppermute | solution.py:24
  13.4 19.5 %collective-permute-start.7 = (bf16[1024,128]{1,0:T(8,128)(2,1)S(1)}, bf16[1024,128]{1,0:T(8,128)(2,1)S(1)}, u32[]{:S(2)}, u32[]{:S(2)}) collective-permute-start(bf16[1024,128]{1,0:T(8,128)(2,1)S(1)} %collective-permute-done.3.refs_1_), channel_id=1, source_target_pairs={{0,16},{8,24},{16,0},{24,8},{1,17},{9,25},{17,1},{25,9},{2,18},{10... | collective-permute-start | bytes 786440 | tf_op jit(solution)/shard_map/ppermute | solution.py:24
  31.8 7.4 %collective-permute-start.9 = (bf16[1024,128]{1,0:T(8,128)(2,1)S(1)}, bf16[1024,128]{1,0:T(8,128)(2,1)S(1)}, u32[]{:S(2)}, u32[]{:S(2)}) collective-permute-start(bf16[1024,128]{1,0:T(8,128)(2,1)S(1)} %collective-permute-done.5.refs_3_), channel_id=1, source_target_pairs={{0,16},{8,24},{16,0},{24,8},{1,17},{9,25},{17,1},{25,9},{2,18},{10... | collective-permute-start | bytes 786440 | tf_op jit(solution)/shard_map/ppermute | solution.py:24
  32.0 37.9 %collective-permute-start = (bf16[256,2048]{1,0:T(8,128)(2,1)}, bf16[256,2048]{1,0:T(8,128)(2,1)S(1)}, u32[]{:S(2)}, u32[]{:S(2)}) collective-permute-start(bf16[256,2048]{1,0:T(8,128)(2,1)} %bitcast.7), channel_id=1, source_target_pairs={{0,1},{1,0},{2,3},{3,2},{4,5},{5,4},{6,7},{7,6},{8,9},{9,8},{10,11... | collective-permute-start | bytes 3145736 | tf_op jit(solution)/shard_map/ppermute | solution.py:28
  32.8 12.0 %collective-permute-start.18 = (bf16[1024,128]{1,0:T(8,128)(2,1)S(1)}, bf16[1024,128]{1,0:T(8,128)(2,1)S(1)}, u32[]{:S(2)}, u32[]{:S(2)}) collective-permute-start(bf16[1024,128]{1,0:T(8,128)(2,1)S(1)} %collective-permute-done.14.refs_0_), channel_id=1, source_target_pairs={{0,16},{8,24},{16,0},{24,8},{1,17},{9,25},{17,1},{25,9},{2,18},{10... | collective-permute-start | bytes 786440 | tf_op jit(solution)/shard_map/ppermute | solution.py:24
  35.9 10.1 %collective-permute-start.19 = (bf16[1024,128]{1,0:T(8,128)(2,1)S(1)}, bf16[1024,128]{1,0:T(8,128)(2,1)S(1)}, u32[]{:S(2)}, u32[]{:S(2)}) collective-permute-start(bf16[1024,128]{1,0:T(8,128)(2,1)S(1)} %collective-permute-done.7.refs_1_), channel_id=1, source_target_pairs={{0,8},{8,0},{16,24},{24,16},{1,9},{9,1},{17,25},{25,17},{2,10},{10... | collective-permute-start | bytes 786440 | tf_op jit(solution)/shard_map/ppermute | solution.py:24
  39.2 11.2 %collective-permute-start.20 = (bf16[1024,128]{1,0:T(8,128)(2,1)S(1)}, bf16[1024,128]{1,0:T(8,128)(2,1)S(1)}, u32[]{:S(2)}, u32[]{:S(2)}) collective-permute-start(bf16[1024,128]{1,0:T(8,128)(2,1)S(1)} %collective-permute-done.16.refs_2_), channel_id=1, source_target_pairs={{0,16},{8,24},{16,0},{24,8},{1,17},{9,25},{17,1},{25,9},{2,18},{10... | collective-permute-start | bytes 786440 | tf_op jit(solution)/shard_map/ppermute | solution.py:24
  44.8 6.8 %collective-permute-start.21 = (bf16[1024,128]{1,0:T(8,128)(2,1)S(1)}, bf16[1024,128]{1,0:T(8,128)(2,1)S(1)}, u32[]{:S(2)}, u32[]{:S(2)}) collective-permute-start(bf16[1024,128]{1,0:T(8,128)(2,1)S(1)} %collective-permute-done.9.refs_3_), channel_id=1, source_target_pairs={{0,8},{8,0},{16,24},{24,16},{1,9},{9,1},{17,25},{25,17},{2,10},{10... | collective-permute-start | bytes 786440 | tf_op jit(solution)/shard_map/ppermute | solution.py:24
  46.0 9.9 %collective-permute-start.15 = (bf16[1024,128]{1,0:T(8,128)(2,1)S(1)}, bf16[1024,128]{1,0:T(8,128)(2,1)S(1)}, u32[]{:S(2)}, u32[]{:S(2)}) collective-permute-start(bf16[1024,128]{1,0:T(8,128)(2,1)S(1)} %collective-permute-done.3.refs_1_), channel_id=1, source_target_pairs={{0,8},{8,0},{16,24},{24,16},{1,9},{9,1},{17,25},{25,17},{2,10},{10... | collective-permute-start | bytes 786440 | tf_op jit(solution)/shard_map/ppermute | solution.py:24
  50.4 11.1 %collective-permute-start.17 = (bf16[1024,128]{1,0:T(8,128)(2,1)S(1)}, bf16[1024,128]{1,0:T(8,128)(2,1)S(1)}, u32[]{:S(2)}, u32[]{:S(2)}) collective-permute-start(bf16[1024,128]{1,0:T(8,128)(2,1)S(1)} %collective-permute-done.5.refs_3_), channel_id=1, source_target_pairs={{0,8},{8,0},{16,24},{24,16},{1,9},{9,1},{17,25},{25,17},{2,10},{10... | collective-permute-start | bytes 786440 | tf_op jit(solution)/shard_map/ppermute | solution.py:24
  51.6 14.4 %collective-permute-start.6 = (bf16[1024,128]{1,0:T(8,128)(2,1)S(1)}, bf16[1024,128]{1,0:T(8,128)(2,1)S(1)}, u32[]{:S(2)}, u32[]{:S(2)}) collective-permute-start(bf16[1024,128]{1,0:T(8,128)(2,1)S(1)} %pad_maximum_fusion.refs_0_), channel_id=1, source_target_pairs={{0,16},{8,24},{16,0},{24,8},{1,17},{9,25},{17,1},{25,9},{2,18},{10... | collective-permute-start | bytes 786440 | tf_op jit(solution)/shard_map/ppermute | solution.py:24
  51.9 15.5 %collective-permute-start.8 = (bf16[1024,128]{1,0:T(8,128)(2,1)S(1)}, bf16[1024,128]{1,0:T(8,128)(2,1)S(1)}, u32[]{:S(2)}, u32[]{:S(2)}) collective-permute-start(bf16[1024,128]{1,0:T(8,128)(2,1)S(1)} %collective-permute-done.4.refs_2_), channel_id=1, source_target_pairs={{0,16},{8,24},{16,0},{24,8},{1,17},{9,25},{17,1},{25,9},{2,18},{10... | collective-permute-start | bytes 786440 | tf_op jit(solution)/shard_map/ppermute | solution.py:24
  56.0 21.5 %collective-permute-start.23 = (bf16[512,128]{1,0:T(8,128)(2,1)S(1)}, bf16[512,128]{1,0:T(8,128)(2,1)S(1)}, u32[]{:S(2)}, u32[]{:S(2)}) collective-permute-start(bf16[512,128]{1,0:T(8,128)(2,1)S(1)} %shard_map.81.near_b), channel_id=1, source_target_pairs={{0,2},{1,3},{2,4},{3,5},{4,6},{5,7},{8,10},{9,11},{10,12},{11,13},... | collective-permute-start | bytes 393224 | tf_op jit(solution)/shard_map/ppermute | solution.py:38
  62.8 16.0 %collective-permute-start.22 = (bf16[512,128]{1,0:T(8,128)(2,1)S(1)}, bf16[512,128]{1,0:T(8,128)(2,1)S(1)}, u32[]{:S(2)}, u32[]{:S(2)}) collective-permute-start(bf16[512,128]{1,0:T(8,128)(2,1)S(1)} %shard_map.80.near_a), channel_id=1, source_target_pairs={{0,2},{1,3},{2,4},{3,5},{4,6},{5,7},{8,10},{9,11},{10,12},{11,13},... | collective-permute-start | bytes 393224 | tf_op jit(solution)/shard_map/ppermute | solution.py:38
  67.4 7.5 %collective-permute-start.24 = (bf16[384,128]{1,0:T(8,128)(2,1)S(1)}, bf16[384,128]{1,0:T(8,128)(2,1)S(1)}, u32[]{:S(2)}, u32[]{:S(2)}) collective-permute-start(bf16[384,128]{1,0:T(8,128)(2,1)S(1)} %slice.18), channel_id=1, source_target_pairs={{0,4},{1,5},{2,6},{3,7},{8,12},{9,13},{10,14},{11,15},{16,20},{17,... | collective-permute-start | bytes 294920 | tf_op jit(solution)/shard_map/ppermute | solution.py:38
  70.9 30.9 %collective-permute-start.11 = (bf16[512,128]{1,0:T(8,128)(2,1)S(1)}, bf16[512,128]{1,0:T(8,128)(2,1)S(1)}, u32[]{:S(2)}, u32[]{:S(2)}) collective-permute-start(bf16[512,128]{1,0:T(8,128)(2,1)S(1)} %shard_map.78.near_b), channel_id=1, source_target_pairs={{0,2},{1,3},{2,4},{3,5},{4,6},{5,7},{8,10},{9,11},{10,12},{11,13},... | collective-permute-start | bytes 393224 | tf_op jit(solution)/shard_map/ppermute | solution.py:38
  72.9 29.0 %collective-permute-start.10 = (bf16[512,128]{1,0:T(8,128)(2,1)S(1)}, bf16[512,128]{1,0:T(8,128)(2,1)S(1)}, u32[]{:S(2)}, u32[]{:S(2)}) collective-permute-start(bf16[512,128]{1,0:T(8,128)(2,1)S(1)} %shard_map.77.near_a), channel_id=1, source_target_pairs={{0,2},{1,3},{2,4},{3,5},{4,6},{5,7},{8,10},{9,11},{10,12},{11,13},... | collective-permute-start | bytes 393224 | tf_op jit(solution)/shard_map/ppermute | solution.py:38
  74.9 26.9 %collective-permute-start.13 = (bf16[384,128]{1,0:T(8,128)(2,1)S(1)}, bf16[384,128]{1,0:T(8,128)(2,1)S(1)}, u32[]{:S(2)}, u32[]{:S(2)}) collective-permute-start(bf16[384,128]{1,0:T(8,128)(2,1)S(1)} %slice.17), channel_id=1, source_target_pairs={{0,4},{1,5},{2,6},{3,7},{8,12},{9,13},{10,14},{11,15},{16,20},{17,... | collective-permute-start | bytes 294920 | tf_op jit(solution)/shard_map/ppermute | solution.py:38
  77.5 24.4 %collective-permute-start.12 = (bf16[384,128]{1,0:T(8,128)(2,1)S(1)}, bf16[384,128]{1,0:T(8,128)(2,1)S(1)}, u32[]{:S(2)}, u32[]{:S(2)}) collective-permute-start(bf16[384,128]{1,0:T(8,128)(2,1)S(1)} %slice.16), channel_id=1, source_target_pairs={{0,4},{1,5},{2,6},{3,7},{8,12},{9,13},{10,14},{11,15},{16,20},{17,... | collective-permute-start | bytes 294920 | tf_op jit(solution)/shard_map/ppermute | solution.py:38
  91.9 22.2 %collective-permute-start.27 = (bf16[256,512]{1,0:T(8,128)(2,1)S(1)}, bf16[256,512]{1,0:T(8,128)(2,1)S(1)}, u32[]{:S(2)}, u32[]{:S(2)}) collective-permute-start(bf16[256,512]{1,0:T(8,128)(2,1)S(1)} %get-tuple-element.13), channel_id=1, source_target_pairs={{0,1},{1,0},{2,3},{3,2},{4,5},{5,4},{6,7},{7,6},{8,9},{9,8},{10,11... | collective-permute-start | bytes 786440 | tf_op jit(solution)/shard_map/ppermute | solution.py:28
  (14 other events, 82.1 us)

commit v2 on v1

v2 whole, which is shorter than its diff:
```python
import functools
import math

import jax
import jax.numpy as jnp
from jax import lax
from jax.experimental import pallas as pl
from jax.experimental.pallas import tpu as pltpu
from jax.sharding import PartitionSpec as P

HD = 128
QH = 16
KVH = 4
BLK = 128
MAXDOC = 8
GROUP = QH // KVH
LANES = GROUP * BLK
VMEM_LIMIT = 48 * 1024 * 1024
SCALE = 1.0 / math.sqrt(HD)
LOG2E = 1.0 / math.log(2.0)
PAUSE = 50_000_000_000


def over_dp(array, mask):
    return lax.ppermute(array, "dp", [(i, i ^ mask) for i in range(lax.axis_size("dp"))])


def other_core(array):
    return lax.ppermute(array, "ctx", [(i, i ^ 1) for i in range(lax.axis_size("ctx"))])


def around(array, pairs):
    size = lax.axis_size("ctx")
    return lax.ppermute(array, "ctx", [(i, (i + 2 * pairs) % size) for i in range(size)])


def after(array, *others):
    return lax.optimization_barrier((array,) + others)[0]


def pause_kernel(token_ref, out_ref):
    out_ref[...] = token_ref[...]


def pause(token, *others):
    return pl.pallas_call(
        pause_kernel,
        out_shape=jax.ShapeDtypeStruct(token.shape, token.dtype),
        in_specs=[pl.BlockSpec(memory_space=pltpu.VMEM)],
        out_specs=pl.BlockSpec(memory_space=pltpu.VMEM),
        cost_estimate=pl.CostEstimate(flops=PAUSE, bytes_accessed=0, transcendentals=0),
    )(after(token, *others))


def project_kernel(slots, spare, own_ref, other_ref, *refs):
    sets = len(refs[:-2]) // slots
    weights, near_ref, far_ref = refs[:-2], refs[-2], refs[-1]
    device = lax.axis_index("ctx")
    core, pair = device % 2, device // 2
    rows = own_ref.shape[0]
    depth = weights[0].shape[0] // 2
    tall, short = 2 * rows, 2 * rows - spare
    for tokens_ref, place in ((own_ref, core), (other_ref, 1 - core)):
        total = jnp.zeros((rows, sets * HD), jnp.float32)
        for step in range(slots):
            source = lax.rem(pair + slots - step, slots)
            for half in range(2):
                group = 2 * source + (core + half) % 2
                columns = pl.ds(pl.multiple_of(group * depth, depth), depth)
                part = slice(half * depth, (half + 1) * depth)
                weight = jnp.concatenate(
                    [weights[s * slots + step][part, :] for s in range(sets)], axis=1
                )
                total += jnp.dot(
                    tokens_ref[:, columns], weight, preferred_element_type=jnp.float32
                )
        total = total.astype(jnp.bfloat16)
        for s in range(sets):
            near_ref[pl.ds(pl.multiple_of(s * tall + place * rows, rows), rows), :] = total[
                :, s * HD : (s + 1) * HD
            ]
    for s in range(sets):
        far_ref[s * short : (s + 1) * short, :] = near_ref[s * tall + spare : (s + 1) * tall, :]


def project(own, other, sets, spare):
    rows, width = own.shape
    weights = [w for one in sets for w in one]
    count = len(sets)
    spec = pl.BlockSpec(memory_space=pltpu.VMEM)
    return pl.pallas_call(
        functools.partial(project_kernel, len(sets[0]), spare),
        out_shape=(
            jax.ShapeDtypeStruct((count * 2 * rows, HD), jnp.bfloat16),
            jax.ShapeDtypeStruct((count * (2 * rows - spare), HD), jnp.bfloat16),
        ),
        in_specs=[spec] * (2 + len(weights)),
        out_specs=(spec, spec),
        compiler_params=pltpu.CompilerParams(vmem_limit_bytes=VMEM_LIMIT),
        cost_estimate=pl.CostEstimate(
            flops=8 * rows * width * HD * count,
            bytes_accessed=4 * rows * width,
            transcendentals=0,
        ),
    )(own, other, *weights)


def attend_kernel(
    second,
    at_a,
    at_b,
    docs_ref,
    mask_ref,
    plan_ref,
    q_own_ref,
    q_other_ref,
    near_a,
    near_b,
    back_a,
    back_b,
    far_a,
    far_b,
    out_own,
    out_other,
    stats_own,
    stats_other,
    kv,
    table,
    top,
    total,
    summed,
    places,
):
    device = lax.axis_index("ctx")
    slice_of = lax.axis_index("dp")
    core, pair = device % 2, device // 2
    column, kind = slice_of % 2, slice_of // 2
    head_pair = (column + second) % 2
    head = 2 * head_pair + core
    dev_blocks = q_own_ref.shape[0] // BLK
    pair_blocks = 2 * dev_blocks
    far_blocks = (MAXDOC - 1) % pair_blocks
    count = plan_ref.shape[1]
    documents = docs_ref.shape[1]
    first = pair * pair_blocks
    own_row = (far_blocks + pair_blocks) * BLK
    tall, short = pair_blocks * BLK, far_blocks * BLK
    for which, at, near, back, far in (
        (kind, at_a, near_a, back_a, far_a),
        (1 - kind, at_b, near_b, back_b, far_b),
    ):
        kv[which, :short, :] = far[at * short : (at + 1) * short, :]
        kv[which, short:own_row, :] = back[at * tall : (at + 1) * tall, :]
        kv[which, own_row:, :] = near[at * tall : (at + 1) * tall, :]
    causal = lax.broadcasted_iota(jnp.int32, (BLK, BLK), 0) <= lax.broadcasted_iota(
        jnp.int32, (BLK, BLK), 1
    )
    causal = jnp.tile(causal, (1, GROUP))
    columns = pl.ds(pl.multiple_of(head * LANES, LANES), LANES)

    for is_own, q_ref, out_ref in ((1, q_own_ref, out_own), (0, q_other_ref, out_other)):
        owner = core if is_own else 1 - core
        for place in range(dev_blocks):
            index = owner * dev_blocks + place
            block = first + index
            rows = slice(place * BLK, (place + 1) * BLK)

            def ends(j, carry):
                end, start = carry
                end = end + docs_ref[0, j]
                return end, jnp.where(end <= block, end, start)

            _, start = lax.fori_loop(0, documents, ends, (jnp.int32(0), jnp.int32(0)))
            for back in range(MAXDOC):
                places[back] = own_row + index * BLK
            found = jnp.int32(1)
            for back in range(1, MAXDOC):
                places[found] = own_row + (index - back) * BLK
                admitted = jnp.logical_and(
                    block - back >= start, mask_ref[0, block, back - 1] == 1
                )
                found += admitted.astype(jnp.int32)

            query = q_ref[rows, columns]
            stacked = jnp.concatenate(
                [query[:, g * HD : (g + 1) * HD] for g in range(GROUP)], axis=0
            )

            def fetch(which, step):
                return kv[which, pl.ds(pl.multiple_of(places[step], BLK), BLK), :]

            def score(steps):
                best = None
                for step in steps:
                    got = lax.dot_general(
                        fetch(0, step),
                        stacked,
                        (((1,), (1,)), ((), ())),
                        preferred_element_type=jnp.float32,
                    )
                    got = jnp.where(causal if step == 0 else step < found, got, -jnp.inf)
                    table[step * BLK : (step + 1) * BLK, :] = got
                    best = got if best is None else jnp.maximum(best, got)
                return jnp.max(best, axis=0, keepdims=True)

            def weigh(steps, highest):
                weights = jnp.exp2(
                    (table[steps[0] * BLK : (steps[-1] + 1) * BLK, :] - highest) * (SCALE * LOG2E)
                )
                values = jnp.concatenate([fetch(1, step) for step in steps], axis=0)
                part = lax.dot_general(
                    values,
                    weights.astype(jnp.bfloat16),
                    (((0,), (0,)), ((), ())),
                    preferred_element_type=jnp.float32,
                )
                return jnp.sum(weights, axis=0, keepdims=True), part

            half = MAXDOC // 2
            top[...] = score(range(half))

            @pl.when(found > half)
            def _():
                top[...] = jnp.maximum(top[...], score(range(half, MAXDOC)))

            total[...], summed[...] = weigh(range(half), top[...])

            @pl.when(found > half)
            def _():
                more, part = weigh(range(half, MAXDOC), top[...])
                total[...] += more
                summed[...] += part

            result = summed[...] / total[...]
            for g in range(GROUP):
                out_ref[rows, g * HD : (g + 1) * HD] = (
                    result[:, g * BLK : (g + 1) * BLK].T.astype(jnp.bfloat16)
                )
            lse = top[...] * SCALE + jnp.log(total[...])
            slot = plan_ref[0, block] - first
            keep_here = slot // dev_blocks == core
            at = slot % dev_blocks

            @pl.when(keep_here)
            def _():
                for g in range(GROUP):
                    stats_own[at, g : g + 1, :] = lse[:, g * BLK : (g + 1) * BLK]

            @pl.when(jnp.logical_not(keep_here))
            def _():
                for g in range(GROUP):
                    stats_other[at, g : g + 1, :] = lse[:, g * BLK : (g + 1) * BLK]


def attend(second, docs, mask, plan, q_own, q_other, first_set, second_set):
    vmem = pl.BlockSpec(memory_space=pltpu.VMEM)
    smem = pl.BlockSpec(memory_space=pltpu.SMEM)
    rows = q_own.shape[0]
    dev_blocks = rows // BLK
    at_a, near_a, back_a, far_a = first_set
    at_b, near_b, back_b, far_b = second_set
    window = (4 * dev_blocks + (MAXDOC - 1) % (2 * dev_blocks)) * BLK
    out = jax.ShapeDtypeStruct((rows, LANES), jnp.bfloat16)
    stats = jax.ShapeDtypeStruct((dev_blocks, GROUP, BLK), jnp.float32)
    return pl.pallas_call(
        functools.partial(attend_kernel, second, at_a, at_b),
        out_shape=(out, out, stats, stats),
        in_specs=[smem] * 3 + [vmem] * 8,
        out_specs=(vmem,) * 4,
        scratch_shapes=[
            pltpu.VMEM((2, window, HD), jnp.bfloat16),
            pltpu.VMEM((MAXDOC * BLK, LANES), jnp.float32),
            pltpu.VMEM((1, LANES), jnp.float32),
            pltpu.VMEM((1, LANES), jnp.float32),
            pltpu.VMEM((HD, LANES), jnp.float32),
            pltpu.SMEM((MAXDOC + 1,), jnp.int32),
        ],
        compiler_params=pltpu.CompilerParams(vmem_limit_bytes=VMEM_LIMIT),
        cost_estimate=pl.CostEstimate(
            flops=2 * dev_blocks * MAXDOC * BLK * LANES * HD * 4,
            bytes_accessed=8 * rows * QH * HD,
            transcendentals=2 * dev_blocks * MAXDOC * BLK * LANES,
        ),
    )(docs, mask, plan, q_own, q_other, near_a, near_b, back_a, back_b, far_a, far_b)


def finish_kernel(
    own_a, own_b, got_a, got_b, st_own_a, st_own_b, st_got_a, st_got_b, out_ref, stats_ref
):
    core = lax.axis_index("ctx") % 2
    column = lax.axis_index("dp") % 2
    pieces = (
        (own_a, column, core),
        (own_b, 1 - column, core),
        (got_a, column, 1 - core),
        (got_b, 1 - column, 1 - core),
    )
    for piece, head_pair, side in pieces:
        head = 2 * head_pair + side
        out_ref[0, :, pl.ds(pl.multiple_of(head * LANES, LANES), LANES)] = piece[...]
    for head in range(KVH):
        is_a = head // 2 == column
        is_own = head % 2 == core
        own = jnp.where(is_a, st_own_a[...], st_own_b[...])
        got = jnp.where(is_a, st_got_a[...], st_got_b[...])
        lse = jnp.where(is_own, own, got)
        for place in range(lse.shape[0]):
            stats_ref[0, head * GROUP : (head + 1) * GROUP, place * BLK : (place + 1) * BLK] = lse[place]


def body(tokens, queries, kv_weight, doc_blocks, block_mask, plan):
    size = lax.axis_size("ctx")
    device = lax.axis_index("ctx")
    core = device % 2
    slots = size // 2
    own_tokens, own_queries = tokens[0], queries[0]
    rows = own_tokens.shape[0]
    other_weight = other_core(kv_weight)
    other_tokens = other_core(after(own_tokens, other_weight))
    other_queries = other_core(after(own_queries, other_weight))

    def my_half(array):
        return lax.dynamic_slice_in_dim(array, core * HD, HD, 1)

    def send(near, far):
        return near, around(near, 1), around(far, 2)

    mine = my_half(kv_weight)
    others = my_half(other_weight)
    pair_blocks = 2 * rows // BLK
    spare = (pair_blocks - (MAXDOC - 1) % pair_blocks) * BLK
    if slots == 4:

        def multiply(*sets):
            return project(own_tokens, other_tokens, sets, spare)

        slab = jnp.concatenate([mine, others], axis=0)
        token = slab[:16, :]
        x0 = over_dp(slab, 1)
        y0 = over_dp(slab, 2)
        z1 = around(slab, 1)
        token = pause(token, x0, y0, other_tokens, other_queries)
        z3 = around(after(slab, token), 3)
        d0 = over_dp(after(x0, token), 2)
        token = pause(token, z1)
        x1 = over_dp(after(z1, token), 1)
        y1 = over_dp(after(z1, token), 2)
        z2 = around(after(slab, token), 2)
        token = pause(token, z3, d0)
        x3 = over_dp(after(z3, token), 1)
        y3 = over_dp(after(z3, token), 2)
        token = pause(token, x1, y1, z2)
        x2 = over_dp(after(z2, token), 1)
        y2 = over_dp(after(z2, token), 2)
        token = pause(token, x3, y3)
        own_kv = multiply([after(slab, token), z1, z2, z3])
        own_kv = send(*own_kv)
        token = pause(token, own_kv[0], x2, y2)
        d1 = over_dp(after(y1, token), 1)
        d3 = over_dp(after(x3, token), 2)
        d2 = over_dp(after(y2, token), 1)
        xy_near, xy_far = multiply([x0, x1, after(x2, token), x3], [y0, y1, y2, y3])
        token = pause(token, xy_near, own_kv[1], own_kv[2])
        xy_kv = send(after(xy_near, token), after(xy_far, token))
        token = pause(token, d1, d2, d3)
        d_kv = send(*multiply([d0, d1, after(d2, token), d3]))
        token = pause(token, d_kv[0])
    else:
        even = jnp.where(core == 0, mine, others)
        odd = jnp.where(core == 0, others, mine)
        groups = [list(range(0, size, 2)), list(range(1, size, 2))]
        slab = jnp.concatenate([even, odd], axis=0)
        own_set = lax.all_gather(slab, "ctx", axis=0, axis_index_groups=groups, tiled=True)
        pair_tokens = jnp.where(
            core == 0,
            jnp.concatenate([own_tokens, other_tokens], axis=0),
            jnp.concatenate([other_tokens, own_tokens], axis=0),
        )

        def multiply(*sets):
            parts = [
                jnp.dot(pair_tokens, w, preferred_element_type=jnp.float32).astype(jnp.bfloat16)
                for w in sets
            ]
            return jnp.concatenate(parts, axis=0), jnp.concatenate(
                [part[spare:] for part in parts], axis=0
            )

        x_set = over_dp(own_set, 1)
        y_set = over_dp(own_set, 2)
        d_set = over_dp(x_set, 2)
        own_kv = send(*multiply(own_set))
        xy_kv = send(*multiply(x_set, y_set))
        d_kv = send(*multiply(d_set))
        token = slab[:16, :]

    def attend_with(second, one, other):
        return attend(
            second, doc_blocks, block_mask, plan, own_queries, other_queries, one, other
        )

    own_near, own_back, own_far = own_kv
    first = attend_with(0, (0, after(own_near, token), own_back, own_far), (1,) + xy_kv)
    second = attend_with(1, (0,) + xy_kv, (0,) + d_kv)
    got_a, got_b = other_core(first[1]), other_core(second[1])
    st_got_a, st_got_b = other_core(first[3]), other_core(second[3])
    vmem = pl.BlockSpec(memory_space=pltpu.VMEM)
    return pl.pallas_call(
        finish_kernel,
        out_shape=(
            jax.ShapeDtypeStruct((1, rows, QH * HD), jnp.bfloat16),
            jax.ShapeDtypeStruct((1, QH, rows), jnp.float32),
        ),
        in_specs=[vmem] * 8,
        out_specs=(vmem, vmem),
        compiler_params=pltpu.CompilerParams(vmem_limit_bytes=VMEM_LIMIT),
    )(first[0], second[0], got_a, got_b, first[2], second[2], st_got_a, st_got_b)


def solution(mesh):
    in_specs = (
        P("dp", "ctx", None),
        P("dp", "ctx", None),
        P("ctx", "dp"),
        P("dp", None),
        P("dp", None, None),
        P("dp", None),
    )
    out_specs = (P("dp", "ctx", None), P("dp", None, "ctx"))
    return jax.shard_map(body, mesh=mesh, in_specs=in_specs, out_specs=out_specs, check_vma=False)
```

time: 114 us -> 86.4 us (0.76)
  the two profiles are of different devices: /device:TPU:13 before, /device:TPU:0 now
where the time goes in v2:
time: 86.4 us; the launch traced here: 85.2 us
  waiting for transfers between devices  38 us (44%)
  starting transfers between devices  27.6 us (32%)
  Pallas kernels  14.6 us (17%)
  local copies, waits for them, and re-layouts  4.16 us (5%)
    ppermute x9, waiting for transfers between devices, around(): lax.ppermute(array, 'ctx', [(i, (i + 2 * pairs) % size) for i in range(si...  17.9 us
    ppermute x12, waiting for transfers between devices, over_dp(): lax.ppermute(array, 'dp', [(i, i ^ mask) for i in range(lax.axis_size('dp...  17.8 us
    ppermute x9, starting transfers between devices, around(): lax.ppermute(array, 'ctx', [(i, (i + 2 * pairs) % size) for i in range(si...  12.8 us
    ppermute x12, starting transfers between devices, over_dp(): lax.ppermute(array, 'dp', [(i, i ^ mask) for i in range(lax.axis_size('dp...  12.7 us
    pallas_call x2, Pallas kernels, attend(): pl.pallas_call(functools.partial(attend_kernel, second, at_a, at_b), out_...  8.1 us
    pallas_call x3, Pallas kernels, project(): pl.pallas_call(functools.partial(project_kernel, len(sets[0]), spare), ou...  5.43 us
    unnamed x21, local copies, waits for them, and re-layouts  3.23 us
    ppermute x7, waiting for transfers between devices, other_core(): lax.ppermute(array, 'ctx', [(i, i ^ 1) for i in range(lax.axis_size('ctx'...  2.21 us
  transfers between devices with their start and end apart: 28, of which 16 were waited for; matrix products, arithmetic and copies ran while one was open for 1% of the time, Pallas kernels for 16%

profile of v2, /device:TPU:0, one launch (start us, length us, event | category | flops | bytes accessed | tf_op | source)
XLA Modules:
  0.0 85.2 jit_solution(14817553023863093225)
XLA Ops:
  1.1 1.4 %collective-permute-done = bf16[512,256]{1,0:T(8,128)(2,1)S(1)} collective-permute-done((bf16[512,256]{1,0:T(8,128)(2,1)}, bf16[512,256]{1,0:T(8,128)(2,1)S(1)}, u32[]{:S(2)}, u32[]{:S(2)}) %collective-permute-start) | collective-permute-done | bytes 262176 | tf_op jit(solution)/shard_map/ppermute | solution.py:29
  4.0 2.9 %collective-permute-start.3 = (bf16[1024,128]{1,0:T(8,128)(2,1)S(1)}, bf16[1024,128]{1,0:T(8,128)(2,1)S(1)}, u32[]{:S(2)}, u32[]{:S(2)}) collective-permute-start(bf16[1024,128]{1,0:T(8,128)(2,1)S(1)} %pad_maximum_fusion.refs_0_), channel_id=1, source_target_pairs={{0,8},{8,0},{16,24},{24,16},{1,9},{9,1},{17,25},{25,17},{2,10},{10... | collective-permute-start | bytes 786440 | tf_op jit(solution)/shard_map/ppermute | solution.py:25
  6.9 1.5 %collective-permute-start.4 = (bf16[1024,128]{1,0:T(8,128)(2,1)S(1)}, bf16[1024,128]{1,0:T(8,128)(2,1)S(1)}, u32[]{:S(2)}, u32[]{:S(2)}) collective-permute-start(bf16[1024,128]{1,0:T(8,128)(2,1)S(1)} %pad_maximum_fusion.refs_0_), channel_id=1, source_target_pairs={{0,16},{8,24},{16,0},{24,8},{1,17},{9,25},{17,1},{25,9},{2,18},{10... | collective-permute-start | bytes 786440 | tf_op jit(solution)/shard_map/ppermute | solution.py:25
  8.4 1.6 %collective-permute-start.5 = (bf16[1024,128]{1,0:T(8,128)(2,1)S(1)}, bf16[1024,128]{1,0:T(8,128)(2,1)S(1)}, u32[]{:S(2)}, u32[]{:S(2)}) collective-permute-start(bf16[1024,128]{1,0:T(8,128)(2,1)S(1)} %pad_maximum_fusion.refs_0_), channel_id=1, source_target_pairs={{0,2},{1,3},{2,4},{3,5},{4,6},{5,7},{6,0},{7,1},{8,10},{9,11},{10,... | collective-permute-start | bytes 786440 | tf_op jit(solution)/shard_map/ppermute | solution.py:34
  10.0 3.5 %collective-permute-done.3.refs_0_ = bf16[1024,128]{1,0:T(8,128)(2,1)S(1)} collective-permute-done((bf16[1024,128]{1,0:T(8,128)(2,1)S(1)}, bf16[1024,128]{1,0:T(8,128)(2,1)S(1)}, u32[]{:S(2)}, u32[]{:S(2)}) %collective-permute-start.3) | collective-permute-done | bytes 262176 | tf_op jit(solution)/shard_map/ppermute | solution.py:25
  13.5 1.5 %collective-permute-done.4.refs_4_ = bf16[1024,128]{1,0:T(8,128)(2,1)S(1)} collective-permute-done((bf16[1024,128]{1,0:T(8,128)(2,1)S(1)}, bf16[1024,128]{1,0:T(8,128)(2,1)S(1)}, u32[]{:S(2)}, u32[]{:S(2)}) %collective-permute-start.4) | collective-permute-done | bytes 262176 | tf_op jit(solution)/shard_map/ppermute | solution.py:25
  15.0 3.1 %collective-permute-done.5.refs_1_ = bf16[1024,128]{1,0:T(8,128)(2,1)S(1)} collective-permute-done((bf16[1024,128]{1,0:T(8,128)(2,1)S(1)}, bf16[1024,128]{1,0:T(8,128)(2,1)S(1)}, u32[]{:S(2)}, u32[]{:S(2)}) %collective-permute-start.5) | collective-permute-done | bytes 262176 | tf_op jit(solution)/shard_map/ppermute | solution.py:34
  18.1 1.7 %collective-permute-start.6 = (bf16[1024,128]{1,0:T(8,128)(2,1)S(1)}, bf16[1024,128]{1,0:T(8,128)(2,1)S(1)}, u32[]{:S(2)}, u32[]{:S(2)}) collective-permute-start(bf16[1024,128]{1,0:T(8,128)(2,1)S(1)} %pad_maximum_fusion.refs_0_), channel_id=1, source_target_pairs={{0,6},{1,7},{2,0},{3,1},{4,2},{5,3},{6,4},{7,5},{8,14},{9,15},{10,... | collective-permute-start | bytes 786440 | tf_op jit(solution)/shard_map/ppermute | solution.py:34
  20.9 1.5 %collective-permute-start.9 = (bf16[1024,128]{1,0:T(8,128)(2,1)S(1)}, bf16[1024,128]{1,0:T(8,128)(2,1)S(1)}, u32[]{:S(2)}, u32[]{:S(2)}) collective-permute-start(bf16[1024,128]{1,0:T(8,128)(2,1)S(1)} %collective-permute-done.5.refs_1_), channel_id=1, source_target_pairs={{0,16},{8,24},{16,0},{24,8},{1,17},{9,25},{17,1},{25,9},{2,18},{10... | collective-permute-start | bytes 786440 | tf_op jit(solution)/shard_map/ppermute | solution.py:25
  22.4 4.2 %collective-permute-done.6.refs_3_ = bf16[1024,128]{1,0:T(8,128)(2,1)S(1)} collective-permute-done((bf16[1024,128]{1,0:T(8,128)(2,1)S(1)}, bf16[1024,128]{1,0:T(8,128)(2,1)S(1)}, u32[]{:S(2)}, u32[]{:S(2)}) %collective-permute-start.6) | collective-permute-done | bytes 262176 | tf_op jit(solution)/shard_map/ppermute | solution.py:34
  26.6 2.4 %collective-permute-done.7.refs_0_ = bf16[1024,128]{1,0:T(8,128)(2,1)S(1)} collective-permute-done((bf16[1024,128]{1,0:T(8,128)(2,1)S(1)}, bf16[1024,128]{1,0:T(8,128)(2,1)S(1)}, u32[]{:S(2)}, u32[]{:S(2)}) %collective-permute-start.7) | collective-permute-done | bytes 262176 | tf_op jit(solution)/shard_map/ppermute | solution.py:25
  30.1 4.6 %collective-permute-done.9.refs_5_ = bf16[1024,128]{1,0:T(8,128)(2,1)S(1)} collective-permute-done((bf16[1024,128]{1,0:T(8,128)(2,1)S(1)}, bf16[1024,128]{1,0:T(8,128)(2,1)S(1)}, u32[]{:S(2)}, u32[]{:S(2)}) %collective-permute-start.9) | collective-permute-done | bytes 262176 | tf_op jit(solution)/shard_map/ppermute | solution.py:25
  37.7 1.6 %copy-done = bf16[1,256,4096]{2,1,0:T(8,128)(2,1)S(1)} copy-done((bf16[1,256,4096]{2,1,0:T(8,128)(2,1)S(1)}, bf16[1,256,4096]{2,1,0:T(8,128)(2,1)}, u32[]{:S(2)}) %copy-start) | copy-done | bytes 2097176
  41.2 1.5 %collective-permute-done.13.refs_2_ = bf16[1024,128]{1,0:T(8,128)(2,1)S(1)} collective-permute-done((bf16[1024,128]{1,0:T(8,128)(2,1)S(1)}, bf16[1024,128]{1,0:T(8,128)(2,1)S(1)}, u32[]{:S(2)}, u32[]{:S(2)}) %collective-permute-start.13) | collective-permute-done | bytes 262176 | tf_op jit(solution)/shard_map/ppermute | solution.py:25
  43.3 1.3 %collective-permute-start.16 = (bf16[384,128]{1,0:T(8,128)(2,1)S(1)}, bf16[384,128]{1,0:T(8,128)(2,1)S(1)}, u32[]{:S(2)}, u32[]{:S(2)}) collective-permute-start(bf16[384,128]{1,0:T(8,128)(2,1)S(1)} %get-tuple-element.56), channel_id=1, source_target_pairs={{0,4},{1,5},{2,6},{3,7},{4,0},{5,1},{6,2},{7,3},{8,12},{9,13},{10,... | collective-permute-start | bytes 294920 | tf_op jit(solution)/shard_map/ppermute | solution.py:34
  44.6 1.4 %collective-permute-start.19 = (bf16[1024,128]{1,0:T(8,128)(2,1)S(1)}, bf16[1024,128]{1,0:T(8,128)(2,1)S(1)}, u32[]{:S(2)}, u32[]{:S(2)}) collective-permute-start(bf16[1024,128]{1,0:T(8,128)(2,1)S(1)} %collective-permute-done.9.refs_5_), channel_id=1, source_target_pairs={{0,8},{8,0},{16,24},{24,16},{1,9},{9,1},{17,25},{25,17},{2,10},{10... | collective-permute-start | bytes 786440 | tf_op jit(solution)/shard_map/ppermute | solution.py:25
  47.9 2.9 %shard_map.78 = (bf16[1024,128]{1,0:T(8,128)(2,1)S(1)}, bf16[768,128]{1,0:T(8,128)(2,1)S(1)}) custom-call(bf16[256,4096]{1,0:T(8,128)(2,1)S(1)} %bitcast.4, bf16[256,4096]{1,0:T(8,128)(2,1)} %copy-done.1, bf16[1024,128]{1,0:T(8,128)(2,1)S(1)} %collective-permute-done.3.refs_0_, bf16[1024,128]{1,0:T(8,128)(2,1)S(1)} %collective-permute-done.8.refs_1_, ...), custom_call_target="tpu_custom_call" | custom-call | flops 2147483648 | bytes 4194304 | tf_op jit(solution)/shard_map/pallas_call | solution.py:91
  51.3 3.3 %collective-permute-start.17 = (bf16[1024,128]{1,0:T(8,128)(2,1)S(1)}, bf16[1024,128]{1,0:T(8,128)(2,1)S(1)}, u32[]{:S(2)}, u32[]{:S(2)}) collective-permute-start(bf16[1024,128]{1,0:T(8,128)(2,1)S(1)} %get-tuple-element.58.near_b.near_a), channel_id=1, source_target_pairs={{0,2},{1,3},{2,4},{3,5},{4,6},{5,7},{6,0},{7,1},{8,10},{9,11},{10,... | collective-permute-start | bytes 786440 | tf_op jit(solution)/shard_map/ppermute | solution.py:34
  54.6 2.7 %collective-permute-done.20.refs_2_ = bf16[1024,128]{1,0:T(8,128)(2,1)S(1)} collective-permute-done((bf16[1024,128]{1,0:T(8,128)(2,1)S(1)}, bf16[1024,128]{1,0:T(8,128)(2,1)S(1)}, u32[]{:S(2)}, u32[]{:S(2)}) %collective-permute-start.20) | collective-permute-done | bytes 262176 | tf_op jit(solution)/shard_map/ppermute | solution.py:25
  57.3 1.3 %shard_map.80 = (bf16[512,128]{1,0:T(8,128)(2,1)S(1)}, bf16[384,128]{1,0:T(8,128)(2,1)S(1)}) custom-call(bf16[256,4096]{1,0:T(8,128)(2,1)S(1)} %bitcast.5, bf16[256,4096]{1,0:T(8,128)(2,1)S(1)} %copy-done.2, bf16[1024,128]{1,0:T(8,128)(2,1)S(1)} %collective-permute-done.7.refs_0_, bf16[1024,128]{1,0:T(8,128)(2,1)S(1)} %collective-permute-done.19.refs_1_, ...), custom_call_target="tpu_custom_call" | custom-call | flops 1073741824 | bytes 4194304 | tf_op jit(solution)/shard_map/pallas_call | solution.py:91
  59.3 3.9 %collective-permute-start.22 = (bf16[512,128]{1,0:T(8,128)(2,1)S(1)}, bf16[512,128]{1,0:T(8,128)(2,1)}, u32[]{:S(2)}, u32[]{:S(2)}) collective-permute-start(bf16[512,128]{1,0:T(8,128)(2,1)S(1)} %get-tuple-element.65.near_b), channel_id=1, source_target_pairs={{0,2},{1,3},{2,4},{3,5},{4,6},{5,7},{6,0},{7,1},{8,10},{9,11},{10,... | collective-permute-start | bytes 393224 | tf_op jit(solution)/shard_map/ppermute | solution.py:34
  63.7 9.4 %collective-permute-done.18.far_b.far_a = bf16[768,128]{1,0:T(8,128)(2,1)S(1)} collective-permute-done((bf16[768,128]{1,0:T(8,128)(2,1)S(1)}, bf16[768,128]{1,0:T(8,128)(2,1)S(1)}, u32[]{:S(2)}, u32[]{:S(2)}) %collective-permute-start.18) | collective-permute-done | bytes 196640 | tf_op jit(solution)/shard_map/ppermute | solution.py:34
  74.0 3.9 %shard_map.79 = (bf16[256,512]{1,0:T(8,128)(2,1)S(1)}, bf16[256,512]{1,0:T(8,128)(2,1)S(1)}, f32[2,4,128]{2,1,0:T(4,128)S(1)}, f32[2,4,128]{2,1,0:T(4,128)S(1)}) custom-call(s32[1,4]{1,0:T(1,128)S(1)} %copy-done.7, s32[1,16,7]{2,1,0:T(8,128)S(1)} %copy.8.mask_ref, s32[1,16]{1,0:T(1,128)S(1)} %copy-done.8, bf16[256,2048]{1,0:T(8,128)(2,1)S(1)} %bitcast.7, ...), custom_call_target="tpu_custom_call" | custom-call | flops 1073741824 | bytes 4194304 | tf_op jit(solution)/shard_map/pallas_call | solution.py:265
  78.0 4.2 %shard_map.81 = (bf16[256,512]{1,0:T(8,128)(2,1)S(1)}, bf16[256,512]{1,0:T(8,128)(2,1)S(1)}, f32[2,4,128]{2,1,0:T(4,128)S(1)}, f32[2,4,128]{2,1,0:T(4,128)S(1)}) custom-call(s32[1,4]{1,0:T(1,128)S(1)} %copy-done.7, s32[1,16,7]{2,1,0:T(8,128)S(1)} %copy.8.mask_ref, s32[1,16]{1,0:T(1,128)S(1)} %copy-done.8, bf16[256,2048]{1,0:T(8,128)(2,1)S(1)} %bitcast.8, ...), custom_call_target="tpu_custom_call" | custom-call | flops 1073741824 | bytes 4194304 | tf_op jit(solution)/shard_map/pallas_call | solution.py:265
  (62 shorter events, 17.0 us)
Async XLA Ops:
  2.5 12.5 %collective-permute-start.2 = (bf16[256,4096]{1,0:T(8,128)(2,1)}, bf16[256,4096]{1,0:T(8,128)(2,1)S(1)}, u32[]{:S(2)}, u32[]{:S(2)}) collective-permute-start(bf16[256,4096]{1,0:T(8,128)(2,1)} %bitcast.2), channel_id=1, source_target_pairs={{0,1},{1,0},{2,3},{3,2},{4,5},{5,4},{6,7},{7,6},{8,9},{9,8},{10,11... | collective-permute-start | bytes 6291464 | tf_op jit(solution)/shard_map/ppermute | solution.py:29
  2.9 12.1 %collective-permute-start.1 = (bf16[256,2048]{1,0:T(8,128)(2,1)}, bf16[256,2048]{1,0:T(8,128)(2,1)S(1)}, u32[]{:S(2)}, u32[]{:S(2)}) collective-permute-start(bf16[256,2048]{1,0:T(8,128)(2,1)} %bitcast.6), channel_id=1, source_target_pairs={{0,1},{1,0},{2,3},{3,2},{4,5},{5,4},{6,7},{7,6},{8,9},{9,8},{10,11... | collective-permute-start | bytes 3145736 | tf_op jit(solution)/shard_map/ppermute | solution.py:29
  4.0 9.5 %collective-permute-start.3 = (bf16[1024,128]{1,0:T(8,128)(2,1)S(1)}, bf16[1024,128]{1,0:T(8,128)(2,1)S(1)}, u32[]{:S(2)}, u32[]{:S(2)}) collective-permute-start(bf16[1024,128]{1,0:T(8,128)(2,1)S(1)} %pad_maximum_fusion.refs_0_), channel_id=1, source_target_pairs={{0,8},{8,0},{16,24},{24,16},{1,9},{9,1},{17,25},{25,17},{2,10},{10... | collective-permute-start | bytes 786440 | tf_op jit(solution)/shard_map/ppermute | solution.py:25
  6.9 8.1 %collective-permute-start.4 = (bf16[1024,128]{1,0:T(8,128)(2,1)S(1)}, bf16[1024,128]{1,0:T(8,128)(2,1)S(1)}, u32[]{:S(2)}, u32[]{:S(2)}) collective-permute-start(bf16[1024,128]{1,0:T(8,128)(2,1)S(1)} %pad_maximum_fusion.refs_0_), channel_id=1, source_target_pairs={{0,16},{8,24},{16,0},{24,8},{1,17},{9,25},{17,1},{25,9},{2,18},{10... | collective-permute-start | bytes 786440 | tf_op jit(solution)/shard_map/ppermute | solution.py:25
  8.4 9.6 %collective-permute-start.5 = (bf16[1024,128]{1,0:T(8,128)(2,1)S(1)}, bf16[1024,128]{1,0:T(8,128)(2,1)S(1)}, u32[]{:S(2)}, u32[]{:S(2)}) collective-permute-start(bf16[1024,128]{1,0:T(8,128)(2,1)S(1)} %pad_maximum_fusion.refs_0_), channel_id=1, source_target_pairs={{0,2},{1,3},{2,4},{3,5},{4,6},{5,7},{6,0},{7,1},{8,10},{9,11},{10,... | collective-permute-start | bytes 786440 | tf_op jit(solution)/shard_map/ppermute | solution.py:34
  18.1 8.5 %collective-permute-start.6 = (bf16[1024,128]{1,0:T(8,128)(2,1)S(1)}, bf16[1024,128]{1,0:T(8,128)(2,1)S(1)}, u32[]{:S(2)}, u32[]{:S(2)}) collective-permute-start(bf16[1024,128]{1,0:T(8,128)(2,1)S(1)} %pad_maximum_fusion.refs_0_), channel_id=1, source_target_pairs={{0,6},{1,7},{2,0},{3,1},{4,2},{5,3},{6,4},{7,5},{8,14},{9,15},{10,... | collective-permute-start | bytes 786440 | tf_op jit(solution)/shard_map/ppermute | solution.py:34
  19.8 9.2 %collective-permute-start.7 = (bf16[1024,128]{1,0:T(8,128)(2,1)S(1)}, bf16[1024,128]{1,0:T(8,128)(2,1)S(1)}, u32[]{:S(2)}, u32[]{:S(2)}) collective-permute-start(bf16[1024,128]{1,0:T(8,128)(2,1)S(1)} %collective-permute-done.3.refs_0_), channel_id=1, source_target_pairs={{0,16},{8,24},{16,0},{24,8},{1,17},{9,25},{17,1},{25,9},{2,18},{10... | collective-permute-start | bytes 786440 | tf_op jit(solution)/shard_map/ppermute | solution.py:25
  20.3 9.8 %collective-permute-start.8 = (bf16[1024,128]{1,0:T(8,128)(2,1)S(1)}, bf16[1024,128]{1,0:T(8,128)(2,1)S(1)}, u32[]{:S(2)}, u32[]{:S(2)}) collective-permute-start(bf16[1024,128]{1,0:T(8,128)(2,1)S(1)} %collective-permute-done.5.refs_1_), channel_id=1, source_target_pairs={{0,8},{8,0},{16,24},{24,16},{1,9},{9,1},{17,25},{25,17},{2,10},{10... | collective-permute-start | bytes 786440 | tf_op jit(solution)/shard_map/ppermute | solution.py:25
  20.9 13.8 %collective-permute-start.9 = (bf16[1024,128]{1,0:T(8,128)(2,1)S(1)}, bf16[1024,128]{1,0:T(8,128)(2,1)S(1)}, u32[]{:S(2)}, u32[]{:S(2)}) collective-permute-start(bf16[1024,128]{1,0:T(8,128)(2,1)S(1)} %collective-permute-done.5.refs_1_), channel_id=1, source_target_pairs={{0,16},{8,24},{16,0},{24,8},{1,17},{9,25},{17,1},{25,9},{2,18},{10... | collective-permute-start | bytes 786440 | tf_op jit(solution)/shard_map/ppermute | solution.py:25
  22.4 13.0 %collective-permute-start.10 = (bf16[1024,128]{1,0:T(8,128)(2,1)S(1)}, bf16[1024,128]{1,0:T(8,128)(2,1)S(1)}, u32[]{:S(2)}, u32[]{:S(2)}) collective-permute-start(bf16[1024,128]{1,0:T(8,128)(2,1)S(1)} %pad_maximum_fusion.refs_0_), channel_id=1, source_target_pairs={{0,4},{1,5},{2,6},{3,7},{4,0},{5,1},{6,2},{7,3},{8,12},{9,13},{10,... | collective-permute-start | bytes 786440 | tf_op jit(solution)/shard_map/ppermute | solution.py:34
  29.1 7.6 %collective-permute-start.11 = (bf16[1024,128]{1,0:T(8,128)(2,1)S(1)}, bf16[1024,128]{1,0:T(8,128)(2,1)S(1)}, u32[]{:S(2)}, u32[]{:S(2)}) collective-permute-start(bf16[1024,128]{1,0:T(8,128)(2,1)S(1)} %collective-permute-done.6.refs_3_), channel_id=1, source_target_pairs={{0,8},{8,0},{16,24},{24,16},{1,9},{9,1},{17,25},{25,17},{2,10},{10... | collective-permute-start | bytes 786440 | tf_op jit(solution)/shard_map/ppermute | solution.py:25
  29.6 8.1 %collective-permute-start.12 = (bf16[1024,128]{1,0:T(8,128)(2,1)S(1)}, bf16[1024,128]{1,0:T(8,128)(2,1)S(1)}, u32[]{:S(2)}, u32[]{:S(2)}) collective-permute-start(bf16[1024,128]{1,0:T(8,128)(2,1)S(1)} %collective-permute-done.6.refs_3_), channel_id=1, source_target_pairs={{0,16},{8,24},{16,0},{24,8},{1,17},{9,25},{17,1},{25,9},{2,18},{10... | collective-permute-start | bytes 786440 | tf_op jit(solution)/shard_map/ppermute | solution.py:25
  35.4 7.3 %collective-permute-start.13 = (bf16[1024,128]{1,0:T(8,128)(2,1)S(1)}, bf16[1024,128]{1,0:T(8,128)(2,1)S(1)}, u32[]{:S(2)}, u32[]{:S(2)}) collective-permute-start(bf16[1024,128]{1,0:T(8,128)(2,1)S(1)} %collective-permute-done.10.refs_2_), channel_id=1, source_target_pairs={{0,8},{8,0},{16,24},{24,16},{1,9},{9,1},{17,25},{25,17},{2,10},{10... | collective-permute-start | bytes 786440 | tf_op jit(solution)/shard_map/ppermute | solution.py:25
  36.1 7.2 %collective-permute-start.14 = (bf16[1024,128]{1,0:T(8,128)(2,1)S(1)}, bf16[1024,128]{1,0:T(8,128)(2,1)S(1)}, u32[]{:S(2)}, u32[]{:S(2)}) collective-permute-start(bf16[1024,128]{1,0:T(8,128)(2,1)S(1)} %collective-permute-done.10.refs_2_), channel_id=1, source_target_pairs={{0,16},{8,24},{16,0},{24,8},{1,17},{9,25},{17,1},{25,9},{2,18},{10... | collective-permute-start | bytes 786440 | tf_op jit(solution)/shard_map/ppermute | solution.py:25
  40.6 10.7 %collective-permute-start.15 = (bf16[512,128]{1,0:T(8,128)(2,1)S(1)}, bf16[512,128]{1,0:T(8,128)(2,1)S(1)}, u32[]{:S(2)}, u32[]{:S(2)}) collective-permute-start(bf16[512,128]{1,0:T(8,128)(2,1)S(1)} %get-tuple-element.51.near_a), channel_id=1, source_target_pairs={{0,2},{1,3},{2,4},{3,5},{4,6},{5,7},{6,0},{7,1},{8,10},{9,11},{10,... | collective-permute-start | bytes 393224 | tf_op jit(solution)/shard_map/ppermute | solution.py:34
  43.3 8.0 %collective-permute-start.16 = (bf16[384,128]{1,0:T(8,128)(2,1)S(1)}, bf16[384,128]{1,0:T(8,128)(2,1)S(1)}, u32[]{:S(2)}, u32[]{:S(2)}) collective-permute-start(bf16[384,128]{1,0:T(8,128)(2,1)S(1)} %get-tuple-element.56), channel_id=1, source_target_pairs={{0,4},{1,5},{2,6},{3,7},{4,0},{5,1},{6,2},{7,3},{8,12},{9,13},{10,... | collective-permute-start | bytes 294920 | tf_op jit(solution)/shard_map/ppermute | solution.py:34
  44.6 12.7 %collective-permute-start.19 = (bf16[1024,128]{1,0:T(8,128)(2,1)S(1)}, bf16[1024,128]{1,0:T(8,128)(2,1)S(1)}, u32[]{:S(2)}, u32[]{:S(2)}) collective-permute-start(bf16[1024,128]{1,0:T(8,128)(2,1)S(1)} %collective-permute-done.9.refs_5_), channel_id=1, source_target_pairs={{0,8},{8,0},{16,24},{24,16},{1,9},{9,1},{17,25},{25,17},{2,10},{10... | collective-permute-start | bytes 786440 | tf_op jit(solution)/shard_map/ppermute | solution.py:25
  46.0 11.3 %collective-permute-start.20 = (bf16[1024,128]{1,0:T(8,128)(2,1)S(1)}, bf16[1024,128]{1,0:T(8,128)(2,1)S(1)}, u32[]{:S(2)}, u32[]{:S(2)}) collective-permute-start(bf16[1024,128]{1,0:T(8,128)(2,1)S(1)} %collective-permute-done.14.refs_6_), channel_id=1, source_target_pairs={{0,8},{8,0},{16,24},{24,16},{1,9},{9,1},{17,25},{25,17},{2,10},{10... | collective-permute-start | bytes 786440 | tf_op jit(solution)/shard_map/ppermute | solution.py:25
  46.6 10.7 %collective-permute-start.21 = (bf16[1024,128]{1,0:T(8,128)(2,1)S(1)}, bf16[1024,128]{1,0:T(8,128)(2,1)S(1)}, u32[]{:S(2)}, u32[]{:S(2)}) collective-permute-start(bf16[1024,128]{1,0:T(8,128)(2,1)S(1)} %collective-permute-done.11.refs_3_), channel_id=1, source_target_pairs={{0,16},{8,24},{16,0},{24,8},{1,17},{9,25},{17,1},{25,9},{2,18},{10... | collective-permute-start | bytes 786440 | tf_op jit(solution)/shard_map/ppermute | solution.py:25
  51.3 21.8 %collective-permute-start.17 = (bf16[1024,128]{1,0:T(8,128)(2,1)S(1)}, bf16[1024,128]{1,0:T(8,128)(2,1)S(1)}, u32[]{:S(2)}, u32[]{:S(2)}) collective-permute-start(bf16[1024,128]{1,0:T(8,128)(2,1)S(1)} %get-tuple-element.58.near_b.near_a), channel_id=1, source_target_pairs={{0,2},{1,3},{2,4},{3,5},{4,6},{5,7},{6,0},{7,1},{8,10},{9,11},{10,... | collective-permute-start | bytes 786440 | tf_op jit(solution)/shard_map/ppermute | solution.py:34
  54.6 18.5 %collective-permute-start.18 = (bf16[768,128]{1,0:T(8,128)(2,1)S(1)}, bf16[768,128]{1,0:T(8,128)(2,1)S(1)}, u32[]{:S(2)}, u32[]{:S(2)}) collective-permute-start(bf16[768,128]{1,0:T(8,128)(2,1)S(1)} %get-tuple-element.60), channel_id=1, source_target_pairs={{0,4},{1,5},{2,6},{3,7},{4,0},{5,1},{6,2},{7,3},{8,12},{9,13},{10,... | collective-permute-start | bytes 589832 | tf_op jit(solution)/shard_map/ppermute | solution.py:34
  59.3 18.7 %collective-permute-start.22 = (bf16[512,128]{1,0:T(8,128)(2,1)S(1)}, bf16[512,128]{1,0:T(8,128)(2,1)}, u32[]{:S(2)}, u32[]{:S(2)}) collective-permute-start(bf16[512,128]{1,0:T(8,128)(2,1)S(1)} %get-tuple-element.65.near_b), channel_id=1, source_target_pairs={{0,2},{1,3},{2,4},{3,5},{4,6},{5,7},{6,0},{7,1},{8,10},{9,11},{10,... | collective-permute-start | bytes 393224 | tf_op jit(solution)/shard_map/ppermute | solution.py:34
  63.3 14.7 %collective-permute-start.23 = (bf16[384,128]{1,0:T(8,128)(2,1)}, bf16[384,128]{1,0:T(8,128)(2,1)S(1)}, u32[]{:S(2)}, u32[]{:S(2)}) collective-permute-start(bf16[384,128]{1,0:T(8,128)(2,1)} %copy-done.6), channel_id=1, source_target_pairs={{0,4},{1,5},{2,6},{3,7},{4,0},{5,1},{6,2},{7,3},{8,12},{9,13},{10,... | collective-permute-start | bytes 294920 | tf_op jit(solution)/shard_map/ppermute | solution.py:34
  77.9 6.2 %collective-permute-start.24 = (bf16[256,512]{1,0:T(8,128)(2,1)S(1)}, bf16[256,512]{1,0:T(8,128)(2,1)S(1)}, u32[]{:S(2)}, u32[]{:S(2)}) collective-permute-start(bf16[256,512]{1,0:T(8,128)(2,1)S(1)} %get-tuple-element.68), channel_id=1, source_target_pairs={{0,1},{1,0},{2,3},{3,2},{4,5},{5,4},{6,7},{7,6},{8,9},{9,8},{10,11... | collective-permute-start | bytes 786440 | tf_op jit(solution)/shard_map/ppermute | solution.py:29
  (14 other events, 120.5 us)

commit v3 on v1

v3 whole, which is shorter than its diff:
```python
import functools
import math

import jax
import jax.numpy as jnp
from jax import lax
from jax.experimental import pallas as pl
from jax.experimental.pallas import tpu as pltpu
from jax.sharding import PartitionSpec as P

HD = 128
QH = 16
KVH = 4
BLK = 128
MAXDOC = 8
GROUP = QH // KVH
LANES = GROUP * BLK
VMEM_LIMIT = 20 * 1024 * 1024
SCALE = 1.0 / math.sqrt(HD)
LOG2E = 1.0 / math.log(2.0)


def over_dp(array, mask):
    return lax.ppermute(array, "dp", [(i, i ^ mask) for i in range(lax.axis_size("dp"))])


def other_core(array):
    return lax.ppermute(array, "ctx", [(i, i ^ 1) for i in range(lax.axis_size("ctx"))])


def around(array, pairs):
    size = lax.axis_size("ctx")
    return lax.ppermute(array, "ctx", [(i, (i + 2 * pairs) % size) for i in range(size)])


def tie(*arrays):
    return lax.optimization_barrier(arrays)


def project_kernel(slots, steps, sets, passed, has_sum, last, keep, depth, *refs):
    refs = list(refs)
    whole = keep is not None
    tokens = [refs.pop(0) for _ in range(2 if whole else 1)]
    weights = []
    for _ in range(len(steps) * sets):
        array = refs.pop(0)
        if array.shape[0] == depth:
            weights.append(((array, 0), (refs.pop(0), 0)))
        else:
            weights.append(((array, 0), (array, depth)))
    kept_ref = refs.pop() if keep else None
    out_ref = refs.pop()
    extras = refs
    device = lax.axis_index("ctx")
    core, pair = device % 2, device // 2
    rows = tokens[0].shape[0] // (1 if whole else 2)

    def group_columns(step, half):
        source = lax.rem(pair + slots - step, slots)
        group = 2 * source + (core + half) % 2
        return pl.ds(pl.multiple_of(group * depth, depth), depth)

    for side in range(2):
        place = core if side == 0 else 1 - core
        here = pl.ds(pl.multiple_of(place * rows, rows), rows)
        if has_sum:
            total = extras[0][here, :]
        else:
            total = jnp.zeros((rows, sets * HD), jnp.float32)
        for position, step in enumerate(steps):
            for half in range(2):
                if whole:
                    piece = tokens[side][:, group_columns(step, half)]
                else:
                    at = (2 * (step - steps[0]) + half) * depth
                    piece = tokens[0][side * rows : (side + 1) * rows, at : at + depth]
                parts = [weights[s * len(steps) + position][half] for s in range(sets)]
                weight = jnp.concatenate([array[at : at + depth, :] for array, at in parts], axis=1)
                total += jnp.dot(piece, weight, preferred_element_type=jnp.float32)
        for position, step in enumerate(keep or ()):
            for half in range(2):
                at = (2 * position + half) * depth
                kept_ref[side * rows : (side + 1) * rows, at : at + depth] = tokens[side][
                    :, group_columns(step, half)
                ]
        if not last:
            out_ref[here, :] = total
            continue
        total = total.astype(jnp.bfloat16)
        for s in range(sets):
            at = pl.multiple_of(s * 2 * rows + place * rows, rows)
            out_ref[pl.ds(at, rows), :] = total[:, s * HD : (s + 1) * HD]
    at = sets * 2 * rows
    for begin, end in passed:
        out_ref[at : at + end - begin, :] = extras[-1][begin:end, :]
        at += end - begin


def project(tokens, slots, steps, sets, total=None, last=True, passed=(), extra=None, keep=()):
    whole = len(tokens) == 2
    rows = tokens[0].shape[0] * len(tokens)
    weights = []
    for one in sets:
        for w in one:
            weights += w if isinstance(w, tuple) else [w]
    first = sets[0][0]
    depth = first[0].shape[0] if isinstance(first, tuple) else first.shape[0] // 2
    extras = [array for array in (total, extra) if array is not None]
    count = len(sets)
    tall = count * rows + sum(end - begin for begin, end in passed)
    if last:
        out = [jax.ShapeDtypeStruct((tall, HD), jnp.bfloat16)]
    else:
        out = [jax.ShapeDtypeStruct((rows, count * HD), jnp.float32)]
    if keep:
        out.append(jax.ShapeDtypeStruct((rows, len(keep) * 2 * depth), jnp.bfloat16))
    spec = pl.BlockSpec(memory_space=pltpu.VMEM)
    got = pl.pallas_call(
        functools.partial(
            project_kernel,
            slots,
            steps,
            count,
            passed,
            total is not None,
            last,
            keep if whole else None,
            depth,
        ),
        out_shape=tuple(out),
        in_specs=[spec] * (len(tokens) + len(weights) + len(extras)),
        out_specs=(spec,) * len(out),
        compiler_params=pltpu.CompilerParams(vmem_limit_bytes=VMEM_LIMIT),
        cost_estimate=pl.CostEstimate(
            flops=4 * rows * depth * HD * len(steps) * count,
            bytes_accessed=4 * rows * depth * len(steps),
            transcendentals=0,
        ),
    )(*tokens, *weights, *extras)
    return got if keep else got[0]


def document_start(docs_ref, block):
    def ends(j, carry):
        end, start = carry
        end = end + docs_ref[0, j]
        return end, jnp.where(end <= block, end, start)

    return lax.fori_loop(0, docs_ref.shape[1], ends, (jnp.int32(0), jnp.int32(0)))[1]


def score_blocks(keys, query, steps, found, causal, table):
    got = lax.dot_general(
        jnp.concatenate([keys(step) for step in steps], axis=0),
        query,
        (((1,), (1,)), ((), ())),
        preferred_element_type=jnp.float32,
    )
    best = None
    for at, step in enumerate(steps):
        part = got[at * BLK : (at + 1) * BLK, :]
        keep = causal if step == 0 and causal is not None else step < found
        part = jnp.where(keep, part, -jnp.inf)
        table[step * BLK : (step + 1) * BLK, :] = part
        best = part if best is None else jnp.maximum(best, part)
    return jnp.max(best, axis=0, keepdims=True)


def weigh_blocks(values, steps, highest, table):
    weights = jnp.exp2(
        (table[steps[0] * BLK : (steps[-1] + 1) * BLK, :] - highest) * (SCALE * LOG2E)
    )
    part = lax.dot_general(
        jnp.concatenate([values(step) for step in steps], axis=0),
        weights.astype(jnp.bfloat16),
        (((0,), (0,)), ((), ())),
        preferred_element_type=jnp.float32,
    )
    return jnp.sum(weights, axis=0, keepdims=True), part


def where_am_i(second):
    device = lax.axis_index("ctx")
    slice_of = lax.axis_index("dp")
    core, pair = device % 2, device // 2
    column, kind = slice_of % 2, slice_of // 2
    return core, pair, kind, 2 * ((column + second) % 2) + core


def stack_kernel(docs_ref, mask_ref, plan_ref, q_own_ref, q_other_ref, out_ref, facts):
    core, pair, _, _ = where_am_i(0)
    blocks = q_own_ref.shape[0] // BLK
    for side in range(2):
        for place in range(blocks):
            item = side * blocks + place
            index = (core if side == 0 else 1 - core) * blocks + place
            block = 2 * blocks * pair + index
            start = document_start(docs_ref, block)
            for back in range(1, MAXDOC):
                admitted = jnp.logical_and(
                    block - back >= start, mask_ref[0, block, back - 1] == 1
                )
                facts[item, back] = admitted.astype(jnp.int32)
            facts[item, 0] = index
            facts[item, MAXDOC] = plan_ref[0, block] - 2 * blocks * pair
    for second in range(2):
        head = where_am_i(second)[3]
        columns = pl.ds(pl.multiple_of(head * LANES, LANES), LANES)
        for side, q_ref in enumerate((q_own_ref, q_other_ref)):
            for place in range(blocks):
                query = q_ref[place * BLK : (place + 1) * BLK, columns]
                for g in range(GROUP):
                    out_ref[second, side * blocks + place, g * BLK : (g + 1) * BLK, :] = query[
                        :, g * HD : (g + 1) * HD
                    ]


def stack(docs, mask, plan, q_own, q_other):
    vmem = pl.BlockSpec(memory_space=pltpu.VMEM)
    smem = pl.BlockSpec(memory_space=pltpu.SMEM)
    items = 2 * q_own.shape[0] // BLK
    return pl.pallas_call(
        stack_kernel,
        out_shape=(
            jax.ShapeDtypeStruct((2, items, LANES, HD), jnp.bfloat16),
            jax.ShapeDtypeStruct((items, MAXDOC + 1), jnp.int32),
        ),
        in_specs=[smem] * 3 + [vmem] * 2,
        out_specs=(vmem, smem),
        compiler_params=pltpu.CompilerParams(vmem_limit_bytes=VMEM_LIMIT),
        cost_estimate=pl.CostEstimate(
            flops=0, bytes_accessed=4 * items * LANES * HD, transcendentals=0
        ),
    )(docs, mask, plan, q_own, q_other)


def near_kernel(
    second,
    starts,
    facts,
    queries_ref,
    near_a,
    near_b,
    back_a,
    back_b,
    summed,
    stat,
    kv,
    table,
    places,
):
    kind = where_am_i(second)[2]
    pair_blocks = queries_ref.shape[1]
    tall = pair_blocks * BLK
    for which, near, back, at in (
        (kind, near_a, back_a, starts[0]),
        (1 - kind, near_b, back_b, starts[1]),
    ):
        kv[which, :tall, :] = back[at[1] : at[1] + tall, :]
        kv[which, tall:, :] = near[at[0] : at[0] + tall, :]
    causal = lax.broadcasted_iota(jnp.int32, (BLK, BLK), 0) <= lax.broadcasted_iota(
        jnp.int32, (BLK, BLK), 1
    )
    causal = jnp.tile(causal, (1, GROUP))

    for item in range(pair_blocks):
        index = facts[item, 0]
        for step in range(MAXDOC + 1):
            places[step] = tall + index * BLK
        found = jnp.int32(1)
        for back in range(1, MAXDOC):
            places[found] = tall + (index - back) * BLK
            found += jnp.where(back <= index + pair_blocks, facts[item, back], 0)
        places[found] = tall + index * BLK
        rows = queries_ref[second, item]

        def fetch(which, step):
            return kv[which, pl.ds(pl.multiple_of(places[step], BLK), BLK), :]

        keys = functools.partial(fetch, 0)
        values = functools.partial(fetch, 1)
        half = MAXDOC // 2
        low, high = range(half), range(half, MAXDOC)
        stat[item, 0:1, :] = score_blocks(keys, rows, low, found, causal, table)

        @pl.when(found > half)
        def _():
            stat[item, 0:1, :] = jnp.maximum(
                stat[item, 0:1, :], score_blocks(keys, rows, high, found, None, table)
            )

        stat[item, 1:2, :], summed[item] = weigh_blocks(values, low, stat[item, 0:1, :], table)

        @pl.when(found > half)
        def _():
            more, part = weigh_blocks(values, high, stat[item, 0:1, :], table)
            stat[item, 1:2, :] += more
            summed[item] += part


def far_kernel(
    second,
    starts,
    facts,
    summed_ref,
    stat_ref,
    queries_ref,
    far_a,
    far_b,
    out_own,
    out_other,
    stats_own,
    stats_other,
    kv,
    table,
    top,
    total,
    summed,
    places,
):
    core, _, kind, _ = where_am_i(second)
    pair_blocks = queries_ref.shape[1]
    dev_blocks = pair_blocks // 2
    far_blocks = (MAXDOC - 1) % pair_blocks
    short = far_blocks * BLK
    for which, far, at in ((kind, far_a, starts[0]), (1 - kind, far_b, starts[1])):
        kv[which, :, :] = far[at[2] : at[2] + short, :]

    for item in range(pair_blocks):
        side, place = divmod(item, dev_blocks)
        out_ref = (out_own, out_other)[side]
        rows = slice(place * BLK, (place + 1) * BLK)
        index = facts[item, 0]
        for step in range(far_blocks + 1):
            places[step] = 0
        found = jnp.int32(0)
        for back in range(MAXDOC - far_blocks, MAXDOC):
            places[found] = (far_blocks + pair_blocks + index - back) * BLK
            found += jnp.where(back > index + pair_blocks, facts[item, back], 0)
        places[found] = 0
        top[...] = stat_ref[item, 0:1, :]
        total[...] = stat_ref[item, 1:2, :]
        summed[...] = summed_ref[item]

        @pl.when(found > 0)
        def _():
            query = queries_ref[second, item]

            def fetch(which, step):
                return kv[which, pl.ds(pl.multiple_of(places[step], BLK), BLK), :]

            steps = range(far_blocks)
            before = top[...]
            highest = jnp.maximum(
                before,
                score_blocks(functools.partial(fetch, 0), query, steps, found, None, table),
            )
            more, part = weigh_blocks(functools.partial(fetch, 1), steps, highest, table)
            shrink = jnp.exp2((before - highest) * (SCALE * LOG2E))
            top[...] = highest
            total[...] = total[...] * shrink + more
            summed[...] = summed[...] * shrink + part

        result = summed[...] / total[...]
        for g in range(GROUP):
            out_ref[rows, g * HD : (g + 1) * HD] = (
                result[:, g * BLK : (g + 1) * BLK].T.astype(jnp.bfloat16)
            )
        lse = top[...] * SCALE + jnp.log(total[...])
        slot = facts[item, MAXDOC]
        keep_here = slot // dev_blocks == core
        slot_at = slot % dev_blocks

        @pl.when(keep_here)
        def _():
            for g in range(GROUP):
                stats_own[slot_at, g : g + 1, :] = lse[:, g * BLK : (g + 1) * BLK]

        @pl.when(jnp.logical_not(keep_here))
        def _():
            for g in range(GROUP):
                stats_other[slot_at, g : g + 1, :] = lse[:, g * BLK : (g + 1) * BLK]


def attend_near(second, facts, queries, first_set, second_set):
    vmem = pl.BlockSpec(memory_space=pltpu.VMEM)
    smem = pl.BlockSpec(memory_space=pltpu.SMEM)
    items = queries.shape[1]
    (near_a, back_a, _), start_a = first_set
    (near_b, back_b, _), start_b = second_set
    return pl.pallas_call(
        functools.partial(near_kernel, second, (start_a, start_b)),
        out_shape=(
            jax.ShapeDtypeStruct((items, HD, LANES), jnp.float32),
            jax.ShapeDtypeStruct((items, 8, LANES), jnp.float32),
        ),
        in_specs=[smem] + [vmem] * 5,
        out_specs=(vmem,) * 2,
        scratch_shapes=[
            pltpu.VMEM((2, 2 * items * BLK, HD), jnp.bfloat16),
            pltpu.VMEM((MAXDOC * BLK, LANES), jnp.float32),
            pltpu.SMEM((MAXDOC + 1,), jnp.int32),
        ],
        compiler_params=pltpu.CompilerParams(vmem_limit_bytes=VMEM_LIMIT),
        cost_estimate=pl.CostEstimate(
            flops=items * MAXDOC * BLK * LANES * HD * 4,
            bytes_accessed=4 * items * BLK * QH * HD,
            transcendentals=items * MAXDOC * BLK * LANES,
        ),
    )(facts, queries, near_a, near_b, back_a, back_b)


def attend_far(second, facts, queries, carried, first_set, second_set):
    vmem = pl.BlockSpec(memory_space=pltpu.VMEM)
    smem = pl.BlockSpec(memory_space=pltpu.SMEM)
    items = queries.shape[1]
    dev_blocks = items // 2
    rows = dev_blocks * BLK
    far_blocks = (MAXDOC - 1) % items
    (_, _, far_a), start_a = first_set
    (_, _, far_b), start_b = second_set
    out = jax.ShapeDtypeStruct((rows, LANES), jnp.bfloat16)
    stats = jax.ShapeDtypeStruct((dev_blocks, GROUP, BLK), jnp.float32)
    return pl.pallas_call(
        functools.partial(far_kernel, second, (start_a, start_b)),
        out_shape=(out, out, stats, stats),
        in_specs=[smem] + [vmem] * 5,
        out_specs=(vmem,) * 4,
        scratch_shapes=[
            pltpu.VMEM((2, far_blocks * BLK, HD), jnp.bfloat16),
            pltpu.VMEM((far_blocks * BLK, LANES), jnp.float32),
            pltpu.VMEM((1, LANES), jnp.float32),
            pltpu.VMEM((1, LANES), jnp.float32),
            pltpu.VMEM((HD, LANES), jnp.float32),
            pltpu.SMEM((far_blocks + 1,), jnp.int32),
        ],
        compiler_params=pltpu.CompilerParams(vmem_limit_bytes=VMEM_LIMIT),
        cost_estimate=pl.CostEstimate(
            flops=items * far_blocks * BLK * LANES * HD * 4,
            bytes_accessed=8 * rows * LANES,
            transcendentals=items * far_blocks * BLK * LANES,
        ),
    )(facts, *carried, queries, far_a, far_b)


def finish_kernel(
    own_a, own_b, got_a, got_b, st_own_a, st_own_b, st_got_a, st_got_b, out_ref, stats_ref
):
    core = lax.axis_index("ctx") % 2
    column = lax.axis_index("dp") % 2
    pieces = (
        (own_a, column, core),
        (own_b, 1 - column, core),
        (got_a, column, 1 - core),
        (got_b, 1 - column, 1 - core),
    )
    for piece, head_pair, side in pieces:
        head = 2 * head_pair + side
        out_ref[0, :, pl.ds(pl.multiple_of(head * LANES, LANES), LANES)] = piece[...]
    for head in range(KVH):
        is_a = head // 2 == column
        is_own = head % 2 == core
        own = jnp.where(is_a, st_own_a[...], st_own_b[...])
        got = jnp.where(is_a, st_got_a[...], st_got_b[...])
        lse = jnp.where(is_own, own, got)
        for place in range(lse.shape[0]):
            stats_ref[0, head * GROUP : (head + 1) * GROUP, place * BLK : (place + 1) * BLK] = lse[place]


def body(tokens, queries, kv_weight, doc_blocks, block_mask, plan):
    size = lax.axis_size("ctx")
    device = lax.axis_index("ctx")
    core = device % 2
    slots = size // 2
    own_tokens, own_queries = tokens[0], queries[0]
    rows = own_tokens.shape[0]
    other_weight = other_core(kv_weight)
    other_weight, own_tokens, own_queries = tie(other_weight, own_tokens, own_queries)
    other_queries = other_core(own_queries)

    def my_half(array):
        return lax.dynamic_slice_in_dim(array, core * HD, HD, 1)

    other_tokens = other_core(own_tokens)
    mine = my_half(kv_weight)
    others = my_half(other_weight)
    tall = 2 * rows
    spare = tall - (MAXDOC - 1) % (tall // BLK) * BLK
    short = tall - spare
    step_xy = ((spare, tall),)
    step_d = ((spare, tall), (tall + spare, 2 * tall))
    if slots == 4:

        def multiply(steps, sets, *rest, **more):
            return project((own_tokens, other_tokens), slots, steps, sets, *rest, **more)

        def multiply_kept(steps, sets, *rest, **more):
            return project((kept,), slots, steps, sets, *rest, **more)

        slab = jnp.concatenate([mine, others], axis=0)
        x0 = over_dp(slab, 1)
        y0 = over_dp(slab, 2)
        z1 = around(slab, 1)
        stacked, facts = stack(doc_blocks, block_mask, plan, own_queries, other_queries)
        slab, x0, y0, other_tokens, stacked, facts = tie(
            slab, x0, y0, other_tokens, stacked, facts
        )
        z3 = around(slab, 3)
        d0 = over_dp(x0, 2)
        slab, z1 = tie(slab, z1)
        z2 = around(slab, 2)
        x1 = over_dp(z1, 1)
        y1 = over_dp(z1, 2)
        z3, d0 = tie(z3, d0)
        x3 = over_dp(z3, 1)
        y3 = over_dp(z3, 2)
        half = slab.shape[0] // 2

        def diagonal(x, y):
            return over_dp(x[:half], 2), over_dp(y[half:], 1)

        d1_low, d1_high = diagonal(x1, y1)
        z2, d1_low, d1_high = tie(z2, d1_low, d1_high)
        x2 = over_dp(z2, 1)
        y2 = over_dp(z2, 2)
        slab, z1, z2, z3, x1, y1 = tie(slab, z1, z2, z3, x1, y1)
        own_near, kept = multiply((0, 1, 2, 3), [[slab, z1, z2, z3]], keep=(2, 3))
        own_back = around(own_near, 1)
        own_near, x3, y3 = tie(own_near, x3, y3)
        xy_sum = multiply((0, 1, 3), [[x0, x1, x3], [y0, y1, y3]], last=False)
        xy_sum, x2, y2, x3, y3 = tie(xy_sum, x2, y2, x3, y3)
        d2 = diagonal(x2, y2)
        d3 = diagonal(x3, y3)
        xy_near = multiply_kept((2,), [[x2], [y2]], xy_sum, passed=step_xy, extra=own_back)
        xy_back = around(xy_near, 1)
        d0, d1_low, d1_high, xy_near = tie(d0, d1_low, d1_high, xy_near)
        d1 = (d1_low, d1_high)
        d_sum = multiply((0, 1), [[d0, d1]], last=False)
        d_near = multiply_kept((2, 3), [[d2, d3]], d_sum, passed=step_d, extra=xy_back)
        d_back = around(d_near, 1)
        d_far = around(d_back[spare:tall], 1)
    else:
        stacked, facts = stack(doc_blocks, block_mask, plan, own_queries, other_queries)
        even = jnp.where(core == 0, mine, others)
        odd = jnp.where(core == 0, others, mine)
        groups = [list(range(0, size, 2)), list(range(1, size, 2))]
        slab = jnp.concatenate([even, odd], axis=0)
        own_set = lax.all_gather(slab, "ctx", axis=0, axis_index_groups=groups, tiled=True)
        pair_tokens = jnp.where(
            core == 0,
            jnp.concatenate([own_tokens, other_tokens], axis=0),
            jnp.concatenate([other_tokens, own_tokens], axis=0),
        )

        def multiply(sets, passed=(), extra=None):
            parts = [
                jnp.dot(pair_tokens, w, preferred_element_type=jnp.float32).astype(jnp.bfloat16)
                for w in sets
            ]
            parts += [extra[begin:end] for begin, end in passed]
            return jnp.concatenate(parts, axis=0)

        x_set = over_dp(own_set, 1)
        y_set = over_dp(own_set, 2)
        d_set = over_dp(x_set, 2)
        own_near = multiply([own_set])
        own_back = around(own_near, 1)
        xy_near = multiply([x_set, y_set], step_xy, own_back)
        xy_back = around(xy_near, 1)
        d_near = multiply([d_set], step_d, xy_back)
        d_back = around(d_near, 1)
        d_far = around(d_back[spare:tall], 1)

    own_set = (own_near, own_back, xy_back), (0, 0, 2 * tall)
    y_set = (xy_near, xy_back, d_back), (tall, tall, tall + short)
    x_set = (xy_near, xy_back, d_back), (0, 0, tall)
    d_set = (d_near, d_back, d_far), (0, 0, 0)
    near_a = attend_near(0, facts, stacked, own_set, y_set)
    near_b = attend_near(1, facts, stacked, x_set, d_set)
    first = attend_far(0, facts, stacked, near_a, own_set, y_set)
    second = attend_far(1, facts, stacked, near_b, x_set, d_set)
    got_a, got_b = other_core(first[1]), other_core(second[1])
    st_got_a, st_got_b = other_core(first[3]), other_core(second[3])
    vmem = pl.BlockSpec(memory_space=pltpu.VMEM)
    return pl.pallas_call(
        finish_kernel,
        out_shape=(
            jax.ShapeDtypeStruct((1, rows, QH * HD), jnp.bfloat16),
            jax.ShapeDtypeStruct((1, QH, rows), jnp.float32),
        ),
        in_specs=[vmem] * 8,
        out_specs=(vmem, vmem),
        compiler_params=pltpu.CompilerParams(vmem_limit_bytes=VMEM_LIMIT),
    )(first[0], second[0], got_a, got_b, first[2], second[2], st_got_a, st_got_b)


def solution(mesh):
    in_specs = (
        P("dp", "ctx", None),
        P("dp", "ctx", None),
        P("ctx", "dp"),
        P("dp", None),
        P("dp", None, None),
        P("dp", None),
    )
    out_specs = (P("dp", "ctx", None), P("dp", None, "ctx"))
    return jax.shard_map(body, mesh=mesh, in_specs=in_specs, out_specs=out_specs, check_vma=False)
```

time: 114 us -> 80.2 us (0.70)
  the two profiles are of different devices: /device:TPU:13 before, /device:TPU:0 now
where the time goes in v3:
time: 80.2 us; the launch traced here: 79.9 us
  waiting for transfers between devices  32.7 us (41%)
  starting transfers between devices  21.4 us (27%)
  Pallas kernels  20.6 us (26%)
  local copies, waits for them, and re-layouts  4.3 us (5%)
  between operations  0.86 us (1%)
    ppermute x7, waiting for transfers between devices, around(): lax.ppermute(array, 'ctx', [(i, (i + 2 * pairs) % size) for i in range(si...  18.9 us
    ppermute x15, starting transfers between devices, over_dp(): lax.ppermute(array, 'dp', [(i, i ^ mask) for i in range(lax.axis_size('dp...  14.9 us
    ppermute x15, waiting for transfers between devices, over_dp(): lax.ppermute(array, 'dp', [(i, i ^ mask) for i in range(lax.axis_size('dp...  11.3 us
    pallas_call x5, Pallas kernels, project(): pl.pallas_call(functools.partial(project_kernel, slots, steps, count, pas...  9.06 us
    pallas_call x2, Pallas kernels, attend_near(): pl.pallas_call(functools.partial(near_kernel, second, (start_a, start_b))...  6.57 us
    ppermute x7, starting transfers between devices, around(): lax.ppermute(array, 'ctx', [(i, (i + 2 * pairs) % size) for i in range(si...  4.75 us
    unnamed x9, local copies, waits for them, and re-layouts  3.3 us
    ppermute x7, waiting for transfers between devices, other_core(): lax.ppermute(array, 'ctx', [(i, i ^ 1) for i in range(lax.axis_size('ctx'...  2.47 us
  transfers between devices with their start and end apart: 29, of which 15 were waited for; matrix products, arithmetic and copies ran while one was open for 2% of the time, Pallas kernels for 23%

profile of v3, /device:TPU:0, one launch (start us, length us, event | category | flops | bytes accessed | tf_op | source)
XLA Modules:
  0.0 79.9 jit_solution(1628939346729945750)
XLA Ops:
  1.2 1.4 %collective-permute-done = bf16[512,256]{1,0:T(8,128)(2,1)S(1)} collective-permute-done((bf16[512,256]{1,0:T(8,128)(2,1)}, bf16[512,256]{1,0:T(8,128)(2,1)S(1)}, u32[]{:S(2)}, u32[]{:S(2)}) %collective-permute-start) | collective-permute-done | bytes 262176 | tf_op jit(solution)/shard_map/ppermute | solution.py:28
  4.0 2.9 %collective-permute-start.1 = (bf16[1024,128]{1,0:T(8,128)(2,1)S(1)}, bf16[1024,128]{1,0:T(8,128)(2,1)}, u32[]{:S(2)}, u32[]{:S(2)}) collective-permute-start(bf16[1024,128]{1,0:T(8,128)(2,1)S(1)} %pad_maximum_fusion.refs_2_), channel_id=1, source_target_pairs={{0,8},{8,0},{16,24},{24,16},{1,9},{9,1},{17,25},{25,17},{2,10},{10... | collective-permute-start | bytes 786440 | tf_op jit(solution)/shard_map/ppermute | solution.py:24
  6.9 1.5 %collective-permute-start.2 = (bf16[1024,128]{1,0:T(8,128)(2,1)S(1)}, bf16[1024,128]{1,0:T(8,128)(2,1)}, u32[]{:S(2)}, u32[]{:S(2)}) collective-permute-start(bf16[1024,128]{1,0:T(8,128)(2,1)S(1)} %pad_maximum_fusion.refs_2_), channel_id=1, source_target_pairs={{0,16},{8,24},{16,0},{24,8},{1,17},{9,25},{17,1},{25,9},{2,18},{10... | collective-permute-start | bytes 786440 | tf_op jit(solution)/shard_map/ppermute | solution.py:24
  8.5 1.6 %collective-permute-start.5 = (bf16[1024,128]{1,0:T(8,128)(2,1)S(1)}, bf16[1024,128]{1,0:T(8,128)(2,1)}, u32[]{:S(2)}, u32[]{:S(2)}) collective-permute-start(bf16[1024,128]{1,0:T(8,128)(2,1)S(1)} %pad_maximum_fusion.refs_2_), channel_id=1, source_target_pairs={{0,2},{1,3},{2,4},{3,5},{4,6},{5,7},{6,0},{7,1},{8,10},{9,11},{10,... | collective-permute-start | bytes 786440 | tf_op jit(solution)/shard_map/ppermute | solution.py:33
  10.8 1.2 %copy-done.1 = bf16[1,256,2048]{2,1,0:T(8,128)(2,1)S(1)} copy-done((bf16[1,256,2048]{2,1,0:T(8,128)(2,1)S(1)}, bf16[1,256,2048]{2,1,0:T(8,128)(2,1)}, u32[]{:S(2)}) %copy-start.1) | copy-done | bytes 1048600
  13.3 1.6 %shard_map.77 = (bf16[2,4,512,128]{3,2,1,0:T(8,128)(2,1)S(1)}, s32[4,9]{1,0:T(4,128)S(1)}) custom-call(s32[1,4]{1,0:T(1,128)S(1)} %copy-done.2, s32[1,16,7]{2,1,0:T(8,128)S(1)} %copy.8.mask_ref, s32[1,16]{1,0:T(1,128)S(1)} %copy-done.3, bf16[256,2048]{1,0:T(8,128)(2,1)S(1)} %bitcast.7, bf16[256,2048]{1,0:T(8,128)(2,1)S(1)} %collective-permute-done.4.q_other_ref), custom_call_target="tpu_custom_call" | custom-call | bytes 1048576 | tf_op jit(solution)/shard_map/pallas_call | solution.py:222
  15.1 3.1 %collective-permute-done.5.refs_3_ = bf16[1024,128]{1,0:T(8,128)(2,1)} collective-permute-done((bf16[1024,128]{1,0:T(8,128)(2,1)S(1)}, bf16[1024,128]{1,0:T(8,128)(2,1)}, u32[]{:S(2)}, u32[]{:S(2)}) %collective-permute-start.5) | collective-permute-done | bytes 262176 | tf_op jit(solution)/shard_map/ppermute | solution.py:33
  19.3 1.7 %collective-permute-start.11 = (bf16[1024,128]{1,0:T(8,128)(2,1)S(1)}, bf16[1024,128]{1,0:T(8,128)(2,1)S(1)}, u32[]{:S(2)}, u32[]{:S(2)}) collective-permute-start(bf16[1024,128]{1,0:T(8,128)(2,1)S(1)} %pad_maximum_fusion.refs_2_), channel_id=1, source_target_pairs={{0,6},{1,7},{2,0},{3,1},{4,2},{5,3},{6,4},{7,5},{8,14},{9,15},{10,... | collective-permute-start | bytes 786440 | tf_op jit(solution)/shard_map/ppermute | solution.py:33
  21.0 1.5 %collective-permute-start.12 = (bf16[1024,128]{1,0:T(8,128)(2,1)}, bf16[1024,128]{1,0:T(8,128)(2,1)S(1)}, u32[]{:S(2)}, u32[]{:S(2)}) collective-permute-start(bf16[1024,128]{1,0:T(8,128)(2,1)} %collective-permute-done.1.refs_2_), channel_id=1, source_target_pairs={{0,16},{8,24},{16,0},{24,8},{1,17},{9,25},{17,1},{25,9},{2,18},{10... | collective-permute-start | bytes 786440 | tf_op jit(solution)/shard_map/ppermute | solution.py:24
  22.5 5.1 %collective-permute-done.9.refs_6_ = bf16[1024,128]{1,0:T(8,128)(2,1)S(1)} collective-permute-done((bf16[1024,128]{1,0:T(8,128)(2,1)}, bf16[1024,128]{1,0:T(8,128)(2,1)S(1)}, u32[]{:S(2)}, u32[]{:S(2)}) %collective-permute-start.9) | collective-permute-done | bytes 262176 | tf_op jit(solution)/shard_map/ppermute | solution.py:24
  28.8 4.3 %collective-permute-done.12.refs_2_ = bf16[1024,128]{1,0:T(8,128)(2,1)S(1)} collective-permute-done((bf16[1024,128]{1,0:T(8,128)(2,1)}, bf16[1024,128]{1,0:T(8,128)(2,1)S(1)}, u32[]{:S(2)}, u32[]{:S(2)}) %collective-permute-start.12) | collective-permute-done | bytes 262176 | tf_op jit(solution)/shard_map/ppermute | solution.py:24
  33.7 3.4 %collective-permute-done.6.refs_4_ = bf16[1024,128]{1,0:T(8,128)(2,1)S(1)} collective-permute-done((bf16[1024,128]{1,0:T(8,128)(2,1)S(1)}, bf16[1024,128]{1,0:T(8,128)(2,1)S(1)}, u32[]{:S(2)}, u32[]{:S(2)}) %collective-permute-start.6) | collective-permute-done | bytes 262176 | tf_op jit(solution)/shard_map/ppermute | solution.py:33
  37.6 1.4 %collective-permute-start.16 = (bf16[1024,128]{1,0:T(8,128)(2,1)S(1)}, bf16[1024,128]{1,0:T(8,128)(2,1)S(1)}, u32[]{:S(2)}, u32[]{:S(2)}) collective-permute-start(bf16[1024,128]{1,0:T(8,128)(2,1)S(1)} %collective-permute-done.6.refs_4_), channel_id=1, source_target_pairs={{0,16},{8,24},{16,0},{24,8},{1,17},{9,25},{17,1},{25,9},{2,18},{10... | collective-permute-start | bytes 786440 | tf_op jit(solution)/shard_map/ppermute | solution.py:24
  39.0 3.0 %shard_map.78 = (bf16[512,128]{1,0:T(8,128)(2,1)S(1)}, bf16[512,2048]{1,0:T(8,128)(2,1)S(1)}) custom-call(bf16[256,4096]{1,0:T(8,128)(2,1)S(1)} %bitcast.3, bf16[256,4096]{1,0:T(8,128)(2,1)} %collective-permute-done.3.refs_1_, bf16[1024,128]{1,0:T(8,128)(2,1)S(1)} %pad_maximum_fusion.refs_2_, bf16[1024,128]{1,0:T(8,128)(2,1)} %collective-permute-done.5.refs_3_, ...), custom_call_target="tpu_custom_call" | custom-call | flops 536870912 | bytes 4194304 | tf_op jit(solution)/shard_map/pallas_call | solution.py:118
  42.0 1.3 %collective-permute-start.17 = (bf16[512,128]{1,0:T(8,128)(2,1)S(1)}, bf16[512,128]{1,0:T(8,128)(2,1)S(1)}, u32[]{:S(2)}, u32[]{:S(2)}) collective-permute-start(bf16[512,128]{1,0:T(8,128)(2,1)S(1)} %get-tuple-element.71.near_a), channel_id=1, source_target_pairs={{0,2},{1,3},{2,4},{3,5},{4,6},{5,7},{6,0},{7,1},{8,10},{9,11},{10,... | collective-permute-start | bytes 393224 | tf_op jit(solution)/shard_map/ppermute | solution.py:33
  43.3 2.7 %shard_map.79.refs_3_ = f32[512,256]{1,0:T(8,128)S(1)} custom-call(bf16[256,4096]{1,0:T(8,128)(2,1)S(1)} %bitcast.4, bf16[256,4096]{1,0:T(8,128)(2,1)} %collective-permute-done.3.refs_1_, bf16[1024,128]{1,0:T(8,128)(2,1)} %collective-permute-done.1.refs_2_, bf16[1024,128]{1,0:T(8,128)(2,1)S(1)} %collective-permute-done.7.refs_3_, ...), custom_call_target="tpu_custom_call" | custom-call | flops 805306368 | bytes 3145728 | tf_op jit(solution)/shard_map/pallas_call | solution.py:118
  46.0 3.1 %collective-permute-done.17.refs_4_.back_a = bf16[512,128]{1,0:T(8,128)(2,1)S(1)} collective-permute-done((bf16[512,128]{1,0:T(8,128)(2,1)S(1)}, bf16[512,128]{1,0:T(8,128)(2,1)S(1)}, u32[]{:S(2)}, u32[]{:S(2)}) %collective-permute-start.17) | collective-permute-done | bytes 131104 | tf_op jit(solution)/shard_map/ppermute | solution.py:33
  53.9 2.3 %shard_map.82.refs_5_ = f32[512,128]{1,0:T(8,128)S(1)} custom-call(bf16[256,4096]{1,0:T(8,128)(2,1)S(1)} %bitcast.5, bf16[256,4096]{1,0:T(8,128)(2,1)} %collective-permute-done.3.refs_1_, bf16[1024,128]{1,0:T(8,128)(2,1)S(1)} %collective-permute-done.12.refs_2_, bf16[512,128]{1,0:T(8,128)(2,1)S(1)} %collective-permute-done.8.refs_3_, ...), custom_call_target="tpu_custom_call" | custom-call | flops 268435456 | bytes 2097152 | tf_op jit(solution)/shard_map/pallas_call | solution.py:118
  56.7 1.2 %collective-permute-done.22.refs_4_ = bf16[512,128]{1,0:T(8,128)(2,1)S(1)} collective-permute-done((bf16[512,128]{1,0:T(8,128)(2,1)S(1)}, bf16[512,128]{1,0:T(8,128)(2,1)S(1)}, u32[]{:S(2)}, u32[]{:S(2)}) %collective-permute-start.22) | collective-permute-done | bytes 131104 | tf_op jit(solution)/shard_map/ppermute | solution.py:24
  57.9 1.9 %collective-permute-done.18.back_b.refs_6_.far_a.back_a = bf16[1408,128]{1,0:T(8,128)(2,1)S(1)} collective-permute-done((bf16[1408,128]{1,0:T(8,128)(2,1)S(1)}, bf16[1408,128]{1,0:T(8,128)(2,1)S(1)}, u32[]{:S(2)}, u32[]{:S(2)}) %collective-permute-start.18) | collective-permute-done | bytes 360480 | tf_op jit(solution)/shard_map/ppermute | solution.py:33
  60.6 3.2 %shard_map.81 = (f32[4,128,512]{2,1,0:T(8,128)S(1)}, f32[4,8,512]{2,1,0:T(8,128)S(1)}) custom-call(s32[4,9]{1,0:T(4,128)S(1)} %get-tuple-element.57.facts, bf16[2,4,512,128]{3,2,1,0:T(8,128)(2,1)S(1)} %get-tuple-element.58.queries_ref, bf16[512,128]{1,0:T(8,128)(2,1)S(1)} %get-tuple-element.71.near_a, bf16[1408,128]{1,0:T(8,128)(2,1)S(1)} %shard_map.80.near_b.near_a, ...), custom_call_target="tpu_custom_call" | custom-call | flops 1073741824 | bytes 4194304 | tf_op jit(solution)/shard_map/pallas_call | solution.py:391
  63.8 5.7 %collective-permute-done.23.far_b.back_b.far_a = bf16[1280,128]{1,0:T(8,128)(2,1)S(1)} collective-permute-done((bf16[1280,128]{1,0:T(8,128)(2,1)S(1)}, bf16[1280,128]{1,0:T(8,128)(2,1)S(1)}, u32[]{:S(2)}, u32[]{:S(2)}) %collective-permute-start.23) | collective-permute-done | bytes 327712 | tf_op jit(solution)/shard_map/ppermute | solution.py:33
  70.7 3.4 %shard_map.85 = (f32[4,128,512]{2,1,0:T(8,128)S(1)}, f32[4,8,512]{2,1,0:T(8,128)S(1)}) custom-call(s32[4,9]{1,0:T(4,128)S(1)} %get-tuple-element.57.facts, bf16[2,4,512,128]{3,2,1,0:T(8,128)(2,1)S(1)} %get-tuple-element.58.queries_ref, bf16[1408,128]{1,0:T(8,128)(2,1)S(1)} %shard_map.80.near_b.near_a, bf16[1280,128]{1,0:T(8,128)(2,1)S(1)} %shard_map.83.near_b, ...), custom_call_target="tpu_custom_call" | custom-call | flops 1073741824 | bytes 4194304 | tf_op jit(solution)/shard_map/pallas_call | solution.py:391
  74.1 1.8 %collective-permute-done.24.far_b = bf16[384,128]{1,0:T(8,128)(2,1)S(1)} collective-permute-done((bf16[384,128]{1,0:T(8,128)(2,1)S(1)}, bf16[384,128]{1,0:T(8,128)(2,1)S(1)}, u32[]{:S(2)}, u32[]{:S(2)}) %collective-permute-start.24) | collective-permute-done | bytes 98336 | tf_op jit(solution)/shard_map/ppermute | solution.py:33
  (64 shorter events, 18.8 us)
Async XLA Ops:
  2.5 12.6 %collective-permute-start.3 = (bf16[256,4096]{1,0:T(8,128)(2,1)}, bf16[256,4096]{1,0:T(8,128)(2,1)}, u32[]{:S(2)}, u32[]{:S(2)}) collective-permute-start(bf16[256,4096]{1,0:T(8,128)(2,1)} %bitcast.2), channel_id=1, source_target_pairs={{0,1},{1,0},{2,3},{3,2},{4,5},{5,4},{6,7},{7,6},{8,9},{9,8},{10,11... | collective-permute-start | bytes 6291464 | tf_op jit(solution)/shard_map/ppermute | solution.py:28
  2.9 7.9 %collective-permute-start.4 = (bf16[256,2048]{1,0:T(8,128)(2,1)}, bf16[256,2048]{1,0:T(8,128)(2,1)S(1)}, u32[]{:S(2)}, u32[]{:S(2)}) collective-permute-start(bf16[256,2048]{1,0:T(8,128)(2,1)} %bitcast.6), channel_id=1, source_target_pairs={{0,1},{1,0},{2,3},{3,2},{4,5},{5,4},{6,7},{7,6},{8,9},{9,8},{10,11... | collective-permute-start | bytes 3145736 | tf_op jit(solution)/shard_map/ppermute | solution.py:28
  4.0 11.0 %collective-permute-start.1 = (bf16[1024,128]{1,0:T(8,128)(2,1)S(1)}, bf16[1024,128]{1,0:T(8,128)(2,1)}, u32[]{:S(2)}, u32[]{:S(2)}) collective-permute-start(bf16[1024,128]{1,0:T(8,128)(2,1)S(1)} %pad_maximum_fusion.refs_2_), channel_id=1, source_target_pairs={{0,8},{8,0},{16,24},{24,16},{1,9},{9,1},{17,25},{25,17},{2,10},{10... | collective-permute-start | bytes 786440 | tf_op jit(solution)/shard_map/ppermute | solution.py:24
  6.9 8.2 %collective-permute-start.2 = (bf16[1024,128]{1,0:T(8,128)(2,1)S(1)}, bf16[1024,128]{1,0:T(8,128)(2,1)}, u32[]{:S(2)}, u32[]{:S(2)}) collective-permute-start(bf16[1024,128]{1,0:T(8,128)(2,1)S(1)} %pad_maximum_fusion.refs_2_), channel_id=1, source_target_pairs={{0,16},{8,24},{16,0},{24,8},{1,17},{9,25},{17,1},{25,9},{2,18},{10... | collective-permute-start | bytes 786440 | tf_op jit(solution)/shard_map/ppermute | solution.py:24
  8.5 9.8 %collective-permute-start.5 = (bf16[1024,128]{1,0:T(8,128)(2,1)S(1)}, bf16[1024,128]{1,0:T(8,128)(2,1)}, u32[]{:S(2)}, u32[]{:S(2)}) collective-permute-start(bf16[1024,128]{1,0:T(8,128)(2,1)S(1)} %pad_maximum_fusion.refs_2_), channel_id=1, source_target_pairs={{0,2},{1,3},{2,4},{3,5},{4,6},{5,7},{6,0},{7,1},{8,10},{9,11},{10,... | collective-permute-start | bytes 786440 | tf_op jit(solution)/shard_map/ppermute | solution.py:33
  18.2 9.5 %collective-permute-start.9 = (bf16[1024,128]{1,0:T(8,128)(2,1)}, bf16[1024,128]{1,0:T(8,128)(2,1)S(1)}, u32[]{:S(2)}, u32[]{:S(2)}) collective-permute-start(bf16[1024,128]{1,0:T(8,128)(2,1)} %collective-permute-done.5.refs_3_), channel_id=1, source_target_pairs={{0,16},{8,24},{16,0},{24,8},{1,17},{9,25},{17,1},{25,9},{2,18},{10... | collective-permute-start | bytes 786440 | tf_op jit(solution)/shard_map/ppermute | solution.py:24
  18.7 9.6 %collective-permute-start.7 = (bf16[1024,128]{1,0:T(8,128)(2,1)}, bf16[1024,128]{1,0:T(8,128)(2,1)S(1)}, u32[]{:S(2)}, u32[]{:S(2)}) collective-permute-start(bf16[1024,128]{1,0:T(8,128)(2,1)} %collective-permute-done.5.refs_3_), channel_id=1, source_target_pairs={{0,8},{8,0},{16,24},{24,16},{1,9},{9,1},{17,25},{25,17},{2,10},{10... | collective-permute-start | bytes 786440 | tf_op jit(solution)/shard_map/ppermute | solution.py:24
  19.3 9.5 %collective-permute-start.11 = (bf16[1024,128]{1,0:T(8,128)(2,1)S(1)}, bf16[1024,128]{1,0:T(8,128)(2,1)S(1)}, u32[]{:S(2)}, u32[]{:S(2)}) collective-permute-start(bf16[1024,128]{1,0:T(8,128)(2,1)S(1)} %pad_maximum_fusion.refs_2_), channel_id=1, source_target_pairs={{0,6},{1,7},{2,0},{3,1},{4,2},{5,3},{6,4},{7,5},{8,14},{9,15},{10,... | collective-permute-start | bytes 786440 | tf_op jit(solution)/shard_map/ppermute | solution.py:33
  21.0 12.1 %collective-permute-start.12 = (bf16[1024,128]{1,0:T(8,128)(2,1)}, bf16[1024,128]{1,0:T(8,128)(2,1)S(1)}, u32[]{:S(2)}, u32[]{:S(2)}) collective-permute-start(bf16[1024,128]{1,0:T(8,128)(2,1)} %collective-permute-done.1.refs_2_), channel_id=1, source_target_pairs={{0,16},{8,24},{16,0},{24,8},{1,17},{9,25},{17,1},{25,9},{2,18},{10... | collective-permute-start | bytes 786440 | tf_op jit(solution)/shard_map/ppermute | solution.py:24
  22.5 14.6 %collective-permute-start.6 = (bf16[1024,128]{1,0:T(8,128)(2,1)S(1)}, bf16[1024,128]{1,0:T(8,128)(2,1)S(1)}, u32[]{:S(2)}, u32[]{:S(2)}) collective-permute-start(bf16[1024,128]{1,0:T(8,128)(2,1)S(1)} %pad_maximum_fusion.refs_2_), channel_id=1, source_target_pairs={{0,4},{1,5},{2,6},{3,7},{4,0},{5,1},{6,2},{7,3},{8,12},{9,13},{10,... | collective-permute-start | bytes 786440 | tf_op jit(solution)/shard_map/ppermute | solution.py:33
  27.7 9.4 %collective-permute-start.10 = (bf16[512,128]{1,0:T(8,128)(2,1)S(1)}, bf16[512,128]{1,0:T(8,128)(2,1)S(1)}, u32[]{:S(2)}, u32[]{:S(2)}) collective-permute-start(bf16[512,128]{1,0:T(8,128)(2,1)S(1)} %slice.29), channel_id=1, source_target_pairs={{0,8},{8,0},{16,24},{24,16},{1,9},{9,1},{17,25},{25,17},{2,10},{10... | collective-permute-start | bytes 393224 | tf_op jit(solution)/shard_map/ppermute | solution.py:24
  28.3 8.8 %collective-permute-start.8 = (bf16[512,128]{1,0:T(8,128)(2,1)S(1)}, bf16[512,128]{1,0:T(8,128)(2,1)S(1)}, u32[]{:S(2)}, u32[]{:S(2)}) collective-permute-start(bf16[512,128]{1,0:T(8,128)(2,1)S(1)} %slice.28), channel_id=1, source_target_pairs={{0,16},{8,24},{16,0},{24,8},{1,17},{9,25},{17,1},{25,9},{2,18},{10... | collective-permute-start | bytes 393224 | tf_op jit(solution)/shard_map/ppermute | solution.py:24
  33.1 10.2 %collective-permute-start.13 = (bf16[1024,128]{1,0:T(8,128)(2,1)S(1)}, bf16[1024,128]{1,0:T(8,128)(2,1)S(1)}, u32[]{:S(2)}, u32[]{:S(2)}) collective-permute-start(bf16[1024,128]{1,0:T(8,128)(2,1)S(1)} %collective-permute-done.11.refs_5_), channel_id=1, source_target_pairs={{0,8},{8,0},{16,24},{24,16},{1,9},{9,1},{17,25},{25,17},{2,10},{10... | collective-permute-start | bytes 786440 | tf_op jit(solution)/shard_map/ppermute | solution.py:24
  33.1 10.2 %collective-permute-start.14 = (bf16[1024,128]{1,0:T(8,128)(2,1)S(1)}, bf16[1024,128]{1,0:T(8,128)(2,1)S(1)}, u32[]{:S(2)}, u32[]{:S(2)}) collective-permute-start(bf16[1024,128]{1,0:T(8,128)(2,1)S(1)} %collective-permute-done.11.refs_5_), channel_id=1, source_target_pairs={{0,16},{8,24},{16,0},{24,8},{1,17},{9,25},{17,1},{25,9},{2,18},{10... | collective-permute-start | bytes 786440 | tf_op jit(solution)/shard_map/ppermute | solution.py:24
  37.1 8.9 %collective-permute-start.15 = (bf16[1024,128]{1,0:T(8,128)(2,1)S(1)}, bf16[1024,128]{1,0:T(8,128)(2,1)S(1)}, u32[]{:S(2)}, u32[]{:S(2)}) collective-permute-start(bf16[1024,128]{1,0:T(8,128)(2,1)S(1)} %collective-permute-done.6.refs_4_), channel_id=1, source_target_pairs={{0,8},{8,0},{16,24},{24,16},{1,9},{9,1},{17,25},{25,17},{2,10},{10... | collective-permute-start | bytes 786440 | tf_op jit(solution)/shard_map/ppermute | solution.py:24
  37.6 8.3 %collective-permute-start.16 = (bf16[1024,128]{1,0:T(8,128)(2,1)S(1)}, bf16[1024,128]{1,0:T(8,128)(2,1)S(1)}, u32[]{:S(2)}, u32[]{:S(2)}) collective-permute-start(bf16[1024,128]{1,0:T(8,128)(2,1)S(1)} %collective-permute-done.6.refs_4_), channel_id=1, source_target_pairs={{0,16},{8,24},{16,0},{24,8},{1,17},{9,25},{17,1},{25,9},{2,18},{10... | collective-permute-start | bytes 786440 | tf_op jit(solution)/shard_map/ppermute | solution.py:24
  42.0 7.0 %collective-permute-start.17 = (bf16[512,128]{1,0:T(8,128)(2,1)S(1)}, bf16[512,128]{1,0:T(8,128)(2,1)S(1)}, u32[]{:S(2)}, u32[]{:S(2)}) collective-permute-start(bf16[512,128]{1,0:T(8,128)(2,1)S(1)} %get-tuple-element.71.near_a), channel_id=1, source_target_pairs={{0,2},{1,3},{2,4},{3,5},{4,6},{5,7},{6,0},{7,1},{8,10},{9,11},{10,... | collective-permute-start | bytes 393224 | tf_op jit(solution)/shard_map/ppermute | solution.py:33
  49.5 10.3 %collective-permute-start.18 = (bf16[1408,128]{1,0:T(8,128)(2,1)S(1)}, bf16[1408,128]{1,0:T(8,128)(2,1)S(1)}, u32[]{:S(2)}, u32[]{:S(2)}) collective-permute-start(bf16[1408,128]{1,0:T(8,128)(2,1)S(1)} %shard_map.80.near_b.near_a), channel_id=1, source_target_pairs={{0,2},{1,3},{2,4},{3,5},{4,6},{5,7},{6,0},{7,1},{8,10},{9,11},{10,... | collective-permute-start | bytes 1081352 | tf_op jit(solution)/shard_map/ppermute | solution.py:33
  49.6 6.6 %collective-permute-start.19 = (bf16[512,128]{1,0:T(8,128)(2,1)S(1)}, bf16[512,128]{1,0:T(8,128)(2,1)S(1)}, u32[]{:S(2)}, u32[]{:S(2)}) collective-permute-start(bf16[512,128]{1,0:T(8,128)(2,1)S(1)} %slice.23), channel_id=1, source_target_pairs={{0,16},{8,24},{16,0},{24,8},{1,17},{9,25},{17,1},{25,9},{2,18},{10... | collective-permute-start | bytes 393224 | tf_op jit(solution)/shard_map/ppermute | solution.py:24
  50.8 5.5 %collective-permute-start.20 = (bf16[512,128]{1,0:T(8,128)(2,1)S(1)}, bf16[512,128]{1,0:T(8,128)(2,1)S(1)}, u32[]{:S(2)}, u32[]{:S(2)}) collective-permute-start(bf16[512,128]{1,0:T(8,128)(2,1)S(1)} %slice.24), channel_id=1, source_target_pairs={{0,8},{8,0},{16,24},{24,16},{1,9},{9,1},{17,25},{25,17},{2,10},{10... | collective-permute-start | bytes 393224 | tf_op jit(solution)/shard_map/ppermute | solution.py:24
  51.7 5.0 %collective-permute-start.21 = (bf16[512,128]{1,0:T(8,128)(2,1)S(1)}, bf16[512,128]{1,0:T(8,128)(2,1)S(1)}, u32[]{:S(2)}, u32[]{:S(2)}) collective-permute-start(bf16[512,128]{1,0:T(8,128)(2,1)S(1)} %slice.25), channel_id=1, source_target_pairs={{0,16},{8,24},{16,0},{24,8},{1,17},{9,25},{17,1},{25,9},{2,18},{10... | collective-permute-start | bytes 393224 | tf_op jit(solution)/shard_map/ppermute | solution.py:24
  60.5 8.9 %collective-permute-start.23 = (bf16[1280,128]{1,0:T(8,128)(2,1)S(1)}, bf16[1280,128]{1,0:T(8,128)(2,1)S(1)}, u32[]{:S(2)}, u32[]{:S(2)}) collective-permute-start(bf16[1280,128]{1,0:T(8,128)(2,1)S(1)} %shard_map.83.near_b), channel_id=1, source_target_pairs={{0,2},{1,3},{2,4},{3,5},{4,6},{5,7},{6,0},{7,1},{8,10},{9,11},{10,... | collective-permute-start | bytes 983048 | tf_op jit(solution)/shard_map/ppermute | solution.py:33
  69.4 6.5 %collective-permute-start.24 = (bf16[384,128]{1,0:T(8,128)(2,1)S(1)}, bf16[384,128]{1,0:T(8,128)(2,1)S(1)}, u32[]{:S(2)}, u32[]{:S(2)}) collective-permute-start(bf16[384,128]{1,0:T(8,128)(2,1)S(1)} %slice.30), channel_id=1, source_target_pairs={{0,2},{1,3},{2,4},{3,5},{4,6},{5,7},{6,0},{7,1},{8,10},{9,11},{10,... | collective-permute-start | bytes 294920 | tf_op jit(solution)/shard_map/ppermute | solution.py:33
  70.6 8.1 %collective-permute-start.25 = (bf16[256,512]{1,0:T(8,128)(2,1)S(1)}, bf16[256,512]{1,0:T(8,128)(2,1)S(1)}, u32[]{:S(2)}, u32[]{:S(2)}) collective-permute-start(bf16[256,512]{1,0:T(8,128)(2,1)S(1)} %get-tuple-element.96), channel_id=1, source_target_pairs={{0,1},{1,0},{2,3},{3,2},{4,5},{5,4},{6,7},{7,6},{8,9},{9,8},{10,11... | collective-permute-start | bytes 786440 | tf_op jit(solution)/shard_map/ppermute | solution.py:28
  (9 other events, 52.3 us)

commit v4 on v3

--- a/solution.py
+++ b/solution.py
@@ -33,11 +33,21 @@
     return lax.ppermute(array, "ctx", [(i, (i + 2 * pairs) % size) for i in range(size)])
 
 
+def neighbours(array):
+    return lax.ppermute(array, "ctx", [(i, i ^ 2) for i in range(lax.axis_size("ctx"))])
+
+
+def mirrored(array):
+    size = lax.axis_size("ctx")
+    pairs = [(i, size - 2 - 2 * (i // 2) + i % 2) for i in range(size)]
+    return lax.ppermute(array, "ctx", pairs)
+
+
 def tie(*arrays):
     return lax.optimization_barrier(arrays)
 
 
-def project_kernel(slots, steps, sets, passed, has_sum, last, keep, depth, *refs):
+def project_kernel(steps, sets, passed, has_sum, last, keep, depth, *refs):
     refs = list(refs)
     whole = keep is not None
     tokens = [refs.pop(0) for _ in range(2 if whole else 1)]
@@ -55,8 +65,10 @@
     core, pair = device % 2, device // 2
     rows = tokens[0].shape[0] // (1 if whole else 2)
 
+    sources = (pair, pair + 1 - 2 * lax.rem(pair, 2), lax.rem(pair + 2, 4), 3 - pair)
+
     def group_columns(step, half):
-        source = lax.rem(pair + slots - step, slots)
+        source = sources[step]
         group = 2 * source + (core + half) % 2
         return pl.ds(pl.multiple_of(group * depth, depth), depth)
 
@@ -96,7 +108,7 @@
         at += end - begin
 
 
-def project(tokens, slots, steps, sets, total=None, last=True, passed=(), extra=None, keep=()):
+def project(tokens, steps, sets, total=None, last=True, passed=(), extra=None, keep=()):
     whole = len(tokens) == 2
     rows = tokens[0].shape[0] * len(tokens)
     weights = []
@@ -118,7 +130,6 @@
     got = pl.pallas_call(
         functools.partial(
             project_kernel,
-            slots,
             steps,
             count,
             passed,
@@ -492,25 +503,24 @@
     if slots == 4:
 
         def multiply(steps, sets, *rest, **more):
-            return project((own_tokens, other_tokens), slots, steps, sets, *rest, **more)
+            return project((own_tokens, other_tokens), steps, sets, *rest, **more)
 
         def multiply_kept(steps, sets, *rest, **more):
-            return project((kept,), slots, steps, sets, *rest, **more)
+            return project((kept,), steps, sets, *rest, **more)
 
         slab = jnp.concatenate([mine, others], axis=0)
+        z3 = mirrored(slab)
+        z1 = neighbours(slab)
         x0 = over_dp(slab, 1)
         y0 = over_dp(slab, 2)
-        z1 = around(slab, 1)
         stacked, facts = stack(doc_blocks, block_mask, plan, own_queries, other_queries)
         slab, x0, y0, other_tokens, stacked, facts = tie(
             slab, x0, y0, other_tokens, stacked, facts
         )
-        z3 = around(slab, 3)
         d0 = over_dp(x0, 2)
-        slab, z1 = tie(slab, z1)
-        z2 = around(slab, 2)
         x1 = over_dp(z1, 1)
         y1 = over_dp(z1, 2)
+        z2 = neighbours(z3)
         z3, d0 = tie(z3, d0)
         x3 = over_dp(z3, 1)
         y3 = over_dp(z3, 2)
@@ -519,22 +529,20 @@
         def diagonal(x, y):
             return over_dp(x[:half], 2), over_dp(y[half:], 1)
 
-        d1_low, d1_high = diagonal(x1, y1)
-        z2, d1_low, d1_high = tie(z2, d1_low, d1_high)
+        own_sum, kept = multiply((0, 1, 3), [[slab, z1, z3]], last=False, keep=(2, 3))
+        d1 = over_dp(y1, 1)
         x2 = over_dp(z2, 1)
         y2 = over_dp(z2, 2)
-        slab, z1, z2, z3, x1, y1 = tie(slab, z1, z2, z3, x1, y1)
-        own_near, kept = multiply((0, 1, 2, 3), [[slab, z1, z2, z3]], keep=(2, 3))
+        own_near = multiply_kept((2,), [[z2]], own_sum)
         own_back = around(own_near, 1)
         own_near, x3, y3 = tie(own_near, x3, y3)
         xy_sum = multiply((0, 1, 3), [[x0, x1, x3], [y0, y1, y3]], last=False)
         xy_sum, x2, y2, x3, y3 = tie(xy_sum, x2, y2, x3, y3)
-        d2 = diagonal(x2, y2)
+        d2 = over_dp(x2, 2)
         d3 = diagonal(x3, y3)
         xy_near = multiply_kept((2,), [[x2], [y2]], xy_sum, passed=step_xy, extra=own_back)
         xy_back = around(xy_near, 1)
-        d0, d1_low, d1_high, xy_near = tie(d0, d1_low, d1_high, xy_near)
-        d1 = (d1_low, d1_high)
+        d0, d1, xy_near = tie(d0, d1, xy_near)
         d_sum = multiply((0, 1), [[d0, d1]], last=False)
         d_near = multiply_kept((2, 3), [[d2, d3]], d_sum, passed=step_d, extra=xy_back)
         d_back = around(d_near, 1)

time: 80.2 us -> 75.1 us (0.936)
  waiting for transfers between devices: 32.7 us -> 20.6 us
  starting transfers between devices: 21.4 us -> 28.2 us
    ppermute x7 -> x4, waiting for transfers between devices: 18.9 us -> 7.09 us  [around(): lax.ppermute(array, 'ctx', [(i, (i + 2 * pairs) % size) for i in range(si...]
    ppermute x0 -> x3, starting transfers between devices: none -> 9.24 us  [the longest x2 5.64 us: neighbours(): lax.ppermute(array, 'ctx', [(i, i ^ 2) for i in range(lax.axis_size('ctx'...]
    ppermute x15 -> x13, waiting for transfers between devices: 11.3 us -> 8.51 us  [over_dp(): lax.ppermute(array, 'dp', [(i, i ^ mask) for i in range(lax.axis_size('dp...]
    ppermute x0 -> x3, waiting for transfers between devices: none -> 2.54 us  [the longest x2 1.58 us: neighbours(): lax.ppermute(array, 'ctx', [(i, i ^ 2) for i in range(lax.axis_size('ctx'...]
    ppermute x7 -> x4, starting transfers between devices: 4.75 us -> 2.86 us  [around(): lax.ppermute(array, 'ctx', [(i, (i + 2 * pairs) % size) for i in range(si...]
    ppermute x15 -> x13, starting transfers between devices: 14.9 us -> 14.4 us  [over_dp(): lax.ppermute(array, 'dp', [(i, i ^ mask) for i in range(lax.axis_size('dp...]
    pallas_call x5 -> x6, Pallas kernels: 9.06 us -> 9.26 us  [project(): pl.pallas_call(functools.partial(project_kernel, steps, count, passed, to...]
  transfers between devices with their start and end apart: 29 -> 27, of which waited for: 15 -> 15; matrix products, arithmetic and copies ran while one was open for 2% -> 2% of each run, Pallas kernels for 23% -> 25%
where the time goes in v4:
time: 75.1 us; the launch traced here: 74.7 us
  starting transfers between devices  28.2 us (38%)
  Pallas kernels  20.8 us (28%)
  waiting for transfers between devices  20.6 us (27%)
  local copies, waits for them, and re-layouts  4.26 us (6%)
  between operations  0.83 us (1%)
    ppermute x13, starting transfers between devices, over_dp(): lax.ppermute(array, 'dp', [(i, i ^ mask) for i in range(lax.axis_size('dp...  14.4 us
    pallas_call x6, Pallas kernels, project(): pl.pallas_call(functools.partial(project_kernel, steps, count, passed, to...  9.26 us
    ppermute x13, waiting for transfers between devices, over_dp(): lax.ppermute(array, 'dp', [(i, i ^ mask) for i in range(lax.axis_size('dp...  8.51 us
    ppermute x4, waiting for transfers between devices, around(): lax.ppermute(array, 'ctx', [(i, (i + 2 * pairs) % size) for i in range(si...  7.09 us
    pallas_call x2, Pallas kernels, attend_near(): pl.pallas_call(functools.partial(near_kernel, second, (start_a, start_b))...  6.56 us
    ppermute x2, starting transfers between devices, neighbours(): lax.ppermute(array, 'ctx', [(i, i ^ 2) for i in range(lax.axis_size('ctx'...  5.64 us
    ppermute x1, starting transfers between devices, mirrored(): return lax.ppermute(array, 'ctx', pairs)  3.6 us
    unnamed x9, local copies, waits for them, and re-layouts  3.3 us
  transfers between devices with their start and end apart: 27, of which 15 were waited for; matrix products, arithmetic and copies ran while one was open for 2% of the time, Pallas kernels for 25%

profile of v4, /device:TPU:0, one launch (start us, length us, event | category | flops | bytes accessed | tf_op | source)
XLA Modules:
  0.0 74.7 jit_solution(16701933672110182498)
XLA Ops:
  1.2 1.4 %collective-permute-done = bf16[512,256]{1,0:T(8,128)(2,1)S(1)} collective-permute-done((bf16[512,256]{1,0:T(8,128)(2,1)}, bf16[512,256]{1,0:T(8,128)(2,1)S(1)}, u32[]{:S(2)}, u32[]{:S(2)}) %collective-permute-start) | collective-permute-done | bytes 262176 | tf_op jit(solution)/shard_map/ppermute | solution.py:28
  4.0 2.9 %collective-permute-start.1 = (bf16[1024,128]{1,0:T(8,128)(2,1)S(1)}, bf16[1024,128]{1,0:T(8,128)(2,1)}, u32[]{:S(2)}, u32[]{:S(2)}) collective-permute-start(bf16[1024,128]{1,0:T(8,128)(2,1)S(1)} %pad_maximum_fusion.refs_2_), channel_id=1, source_target_pairs={{0,8},{8,0},{16,24},{24,16},{1,9},{9,1},{17,25},{25,17},{2,10},{10... | collective-permute-start | bytes 786440 | tf_op jit(solution)/shard_map/ppermute | solution.py:24
  6.9 1.5 %collective-permute-start.2 = (bf16[1024,128]{1,0:T(8,128)(2,1)S(1)}, bf16[1024,128]{1,0:T(8,128)(2,1)}, u32[]{:S(2)}, u32[]{:S(2)}) collective-permute-start(bf16[1024,128]{1,0:T(8,128)(2,1)S(1)} %pad_maximum_fusion.refs_2_), channel_id=1, source_target_pairs={{0,16},{8,24},{16,0},{24,8},{1,17},{9,25},{17,1},{25,9},{2,18},{10... | collective-permute-start | bytes 786440 | tf_op jit(solution)/shard_map/ppermute | solution.py:24
  9.2 3.6 %collective-permute-start.6 = (bf16[1024,128]{1,0:T(8,128)(2,1)S(1)}, bf16[1024,128]{1,0:T(8,128)(2,1)S(1)}, u32[]{:S(2)}, u32[]{:S(2)}) collective-permute-start(bf16[1024,128]{1,0:T(8,128)(2,1)S(1)} %pad_maximum_fusion.refs_2_), channel_id=1, source_target_pairs={{0,6},{1,7},{2,4},{3,5},{4,2},{5,3},{6,0},{7,1},{8,14},{9,15},{10,... | collective-permute-start | bytes 786440 | tf_op jit(solution)/shard_map/ppermute | solution.py:43
  12.8 1.2 %copy-done.1 = bf16[1,256,2048]{2,1,0:T(8,128)(2,1)S(1)} copy-done((bf16[1,256,2048]{2,1,0:T(8,128)(2,1)S(1)}, bf16[1,256,2048]{2,1,0:T(8,128)(2,1)}, u32[]{:S(2)}) %copy-start.1) | copy-done | bytes 1048600
  15.4 1.6 %shard_map.77 = (bf16[2,4,512,128]{3,2,1,0:T(8,128)(2,1)S(1)}, s32[4,9]{1,0:T(4,128)S(1)}) custom-call(s32[1,4]{1,0:T(1,128)S(1)} %copy-done.2, s32[1,16,7]{2,1,0:T(8,128)S(1)} %copy.8.mask_ref, s32[1,16]{1,0:T(1,128)S(1)} %copy-done.3, bf16[256,2048]{1,0:T(8,128)(2,1)S(1)} %bitcast.7, bf16[256,2048]{1,0:T(8,128)(2,1)S(1)} %collective-permute-done.4.q_other_ref), custom_call_target="tpu_custom_call" | custom-call | bytes 1048576 | tf_op jit(solution)/shard_map/pallas_call | solution.py:233
  19.2 5.0 %collective-permute-start.8 = (bf16[1024,128]{1,0:T(8,128)(2,1)S(1)}, bf16[1024,128]{1,0:T(8,128)(2,1)S(1)}, u32[]{:S(2)}, u32[]{:S(2)}) collective-permute-start(bf16[1024,128]{1,0:T(8,128)(2,1)S(1)} %collective-permute-done.6.refs_4_), channel_id=1, source_target_pairs={{0,2},{1,3},{2,0},{3,1},{4,6},{5,7},{6,4},{7,5},{8,10},{9,11},{10,... | collective-permute-start | bytes 786440 | tf_op jit(solution)/shard_map/ppermute | solution.py:37
  25.9 2.1 %collective-permute-start.11 = (bf16[1024,128]{1,0:T(8,128)(2,1)S(1)}, bf16[1024,128]{1,0:T(8,128)(2,1)S(1)}, u32[]{:S(2)}, u32[]{:S(2)}) collective-permute-start(bf16[1024,128]{1,0:T(8,128)(2,1)S(1)} %collective-permute-done.5.refs_3_), channel_id=1, source_target_pairs={{0,16},{8,24},{16,0},{24,8},{1,17},{9,25},{17,1},{25,9},{2,18},{10... | collective-permute-start | bytes 786440 | tf_op jit(solution)/shard_map/ppermute | solution.py:24
  28.9 1.6 %collective-permute-done.8.refs_1_ = bf16[1024,128]{1,0:T(8,128)(2,1)S(1)} collective-permute-done((bf16[1024,128]{1,0:T(8,128)(2,1)S(1)}, bf16[1024,128]{1,0:T(8,128)(2,1)S(1)}, u32[]{:S(2)}, u32[]{:S(2)}) %collective-permute-start.8) | collective-permute-done | bytes 262176 | tf_op jit(solution)/shard_map/ppermute | solution.py:37
  31.0 3.1 %collective-permute-done.10.refs_7_ = bf16[1024,128]{1,0:T(8,128)(2,1)S(1)} collective-permute-done((bf16[1024,128]{1,0:T(8,128)(2,1)S(1)}, bf16[1024,128]{1,0:T(8,128)(2,1)S(1)}, u32[]{:S(2)}, u32[]{:S(2)}) %collective-permute-start.10) | collective-permute-done | bytes 262176 | tf_op jit(solution)/shard_map/ppermute | solution.py:24
  34.6 2.7 %shard_map.78 = (f32[512,128]{1,0:T(8,128)S(1)}, bf16[512,2048]{1,0:T(8,128)(2,1)S(1)}) custom-call(bf16[256,4096]{1,0:T(8,128)(2,1)S(1)} %bitcast.3, bf16[256,4096]{1,0:T(8,128)(2,1)} %collective-permute-done.3.refs_1_, bf16[1024,128]{1,0:T(8,128)(2,1)S(1)} %pad_maximum_fusion.refs_2_, bf16[1024,128]{1,0:T(8,128)(2,1)S(1)} %collective-permute-done.5.refs_3_, ...), custom_call_target="tpu_custom_call" | custom-call | flops 402653184 | bytes 3145728 | tf_op jit(solution)/shard_map/pallas_call | solution.py:130
  38.2 1.5 %collective-permute-done.11.refs_6_ = bf16[1024,128]{1,0:T(8,128)(2,1)S(1)} collective-permute-done((bf16[1024,128]{1,0:T(8,128)(2,1)S(1)}, bf16[1024,128]{1,0:T(8,128)(2,1)S(1)}, u32[]{:S(2)}, u32[]{:S(2)}) %collective-permute-start.11) | collective-permute-done | bytes 262176 | tf_op jit(solution)/shard_map/ppermute | solution.py:24
  40.1 2.7 %shard_map.80.refs_3_ = f32[512,256]{1,0:T(8,128)S(1)} custom-call(bf16[256,4096]{1,0:T(8,128)(2,1)S(1)} %bitcast.4, bf16[256,4096]{1,0:T(8,128)(2,1)} %collective-permute-done.3.refs_1_, bf16[1024,128]{1,0:T(8,128)(2,1)} %collective-permute-done.1.refs_2_, bf16[1024,128]{1,0:T(8,128)(2,1)S(1)} %collective-permute-done.13.refs_3_, ...), custom_call_target="tpu_custom_call" | custom-call | flops 805306368 | bytes 3145728 | tf_op jit(solution)/shard_map/pallas_call | solution.py:130
  42.9 1.7 %collective-permute-done.16.refs_4_.back_a = bf16[512,128]{1,0:T(8,128)(2,1)S(1)} collective-permute-done((bf16[512,128]{1,0:T(8,128)(2,1)S(1)}, bf16[512,128]{1,0:T(8,128)(2,1)S(1)}, u32[]{:S(2)}, u32[]{:S(2)}) %collective-permute-start.16) | collective-permute-done | bytes 131104 | tf_op jit(solution)/shard_map/ppermute | solution.py:33
  46.0 1.2 %collective-permute-start.18 = (bf16[1024,128]{1,0:T(8,128)(2,1)S(1)}, bf16[1024,128]{1,0:T(8,128)(2,1)S(1)}, u32[]{:S(2)}, u32[]{:S(2)}) collective-permute-start(bf16[1024,128]{1,0:T(8,128)(2,1)S(1)} %collective-permute-done.14.refs_1_), channel_id=1, source_target_pairs={{0,16},{8,24},{16,0},{24,8},{1,17},{9,25},{17,1},{25,9},{2,18},{10... | collective-permute-start | bytes 786440 | tf_op jit(solution)/shard_map/ppermute | solution.py:24
  48.1 1.2 %collective-permute-start.20 = (bf16[512,128]{1,0:T(8,128)(2,1)S(1)}, bf16[512,128]{1,0:T(8,128)(2,1)S(1)}, u32[]{:S(2)}, u32[]{:S(2)}) collective-permute-start(bf16[512,128]{1,0:T(8,128)(2,1)S(1)} %slice.10), channel_id=1, source_target_pairs={{0,8},{8,0},{16,24},{24,16},{1,9},{9,1},{17,25},{25,17},{2,10},{10... | collective-permute-start | bytes 393224 | tf_op jit(solution)/shard_map/ppermute | solution.py:24
  49.4 2.5 %collective-permute-done.12.refs_3_ = bf16[1024,128]{1,0:T(8,128)(2,1)S(1)} collective-permute-done((bf16[1024,128]{1,0:T(8,128)(2,1)S(1)}, bf16[1024,128]{1,0:T(8,128)(2,1)S(1)}, u32[]{:S(2)}, u32[]{:S(2)}) %collective-permute-start.12) | collective-permute-done | bytes 262176 | tf_op jit(solution)/shard_map/ppermute | solution.py:24
  51.9 2.3 %shard_map.83.refs_4_ = f32[512,128]{1,0:T(8,128)S(1)} custom-call(bf16[256,4096]{1,0:T(8,128)(2,1)S(1)} %bitcast.5, bf16[256,4096]{1,0:T(8,128)(2,1)} %collective-permute-done.3.refs_1_, bf16[1024,128]{1,0:T(8,128)(2,1)S(1)} %collective-permute-done.7.refs_2_, bf16[1024,128]{1,0:T(8,128)(2,1)S(1)} %collective-permute-done.12.refs_3_), custom_call_target="tpu_custom_call" | custom-call | flops 268435456 | bytes 2097152 | tf_op jit(solution)/shard_map/pallas_call | solution.py:130
  55.2 1.6 %collective-permute-start.21 = (bf16[1280,128]{1,0:T(8,128)(2,1)S(1)}, bf16[1280,128]{1,0:T(8,128)(2,1)S(1)}, u32[]{:S(2)}, u32[]{:S(2)}) collective-permute-start(bf16[1280,128]{1,0:T(8,128)(2,1)S(1)} %shard_map.84.near_b), channel_id=1, source_target_pairs={{0,2},{1,3},{2,4},{3,5},{4,6},{5,7},{6,0},{7,1},{8,10},{9,11},{10,... | collective-permute-start | bytes 983048 | tf_op jit(solution)/shard_map/ppermute | solution.py:33
  56.8 3.2 %shard_map.82 = (f32[4,128,512]{2,1,0:T(8,128)S(1)}, f32[4,8,512]{2,1,0:T(8,128)S(1)}) custom-call(s32[4,9]{1,0:T(4,128)S(1)} %get-tuple-element.45.facts, bf16[2,4,512,128]{3,2,1,0:T(8,128)(2,1)S(1)} %get-tuple-element.46.queries_ref, bf16[512,128]{1,0:T(8,128)(2,1)S(1)} %shard_map.79.near_a, bf16[1408,128]{1,0:T(8,128)(2,1)S(1)} %shard_map.81.near_b.near_a, ...), custom_call_target="tpu_custom_call" | custom-call | flops 1073741824 | bytes 4194304 | tf_op jit(solution)/shard_map/pallas_call | solution.py:402
  60.0 4.2 %collective-permute-done.21.far_b.back_b.far_a = bf16[1280,128]{1,0:T(8,128)(2,1)S(1)} collective-permute-done((bf16[1280,128]{1,0:T(8,128)(2,1)S(1)}, bf16[1280,128]{1,0:T(8,128)(2,1)S(1)}, u32[]{:S(2)}, u32[]{:S(2)}) %collective-permute-start.21) | collective-permute-done | bytes 327712 | tf_op jit(solution)/shard_map/ppermute | solution.py:33
  66.2 3.4 %shard_map.86 = (f32[4,128,512]{2,1,0:T(8,128)S(1)}, f32[4,8,512]{2,1,0:T(8,128)S(1)}) custom-call(s32[4,9]{1,0:T(4,128)S(1)} %get-tuple-element.45.facts, bf16[2,4,512,128]{3,2,1,0:T(8,128)(2,1)S(1)} %get-tuple-element.46.queries_ref, bf16[1408,128]{1,0:T(8,128)(2,1)S(1)} %shard_map.81.near_b.near_a, bf16[1280,128]{1,0:T(8,128)(2,1)S(1)} %shard_map.84.near_b, ...), custom_call_target="tpu_custom_call" | custom-call | flops 1073741824 | bytes 4194304 | tf_op jit(solution)/shard_map/pallas_call | solution.py:402
  69.6 1.1 %collective-permute-done.22.far_b = bf16[384,128]{1,0:T(8,128)(2,1)S(1)} collective-permute-done((bf16[384,128]{1,0:T(8,128)(2,1)S(1)}, bf16[384,128]{1,0:T(8,128)(2,1)S(1)}, u32[]{:S(2)}, u32[]{:S(2)}) %collective-permute-start.22) | collective-permute-done | bytes 98336 | tf_op jit(solution)/shard_map/ppermute | solution.py:33
  70.7 1.1 %shard_map.87 = (bf16[256,512]{1,0:T(8,128)(2,1)S(1)}, bf16[256,512]{1,0:T(8,128)(2,1)S(1)}, f32[2,4,128]{2,1,0:T(4,128)S(1)}, f32[2,4,128]{2,1,0:T(4,128)S(1)}) custom-call(s32[4,9]{1,0:T(4,128)S(1)} %get-tuple-element.45.facts, f32[4,128,512]{2,1,0:T(8,128)S(1)} %get-tuple-element.69.summed_ref, f32[4,8,512]{2,1,0:T(8,128)S(1)} %get-tuple-element.70.stat_ref, ...), custom_call_target="tpu_custom_call" | custom-call | flops 402653184 | bytes 1048576 | tf_op jit(solution)/shard_map/pallas_call | solution.py:435
  (57 shorter events, 19.3 us)
Async XLA Ops:
  0.6 1.9 %collective-permute-start = (bf16[512,256]{1,0:T(8,128)(2,1)}, bf16[512,256]{1,0:T(8,128)(2,1)S(1)}, u32[]{:S(2)}, u32[]{:S(2)}) collective-permute-start(bf16[512,256]{1,0:T(8,128)(2,1)} %param.8), channel_id=1, source_target_pairs={{0,1},{1,0},{2,3},{3,2},{4,5},{5,4},{6,7},{7,6},{8,9},{9,8},{10,11... | collective-permute-start | bytes 786440 | tf_op jit(solution)/shard_map/ppermute | solution.py:28
  2.5 14.5 %collective-permute-start.3 = (bf16[256,4096]{1,0:T(8,128)(2,1)}, bf16[256,4096]{1,0:T(8,128)(2,1)}, u32[]{:S(2)}, u32[]{:S(2)}) collective-permute-start(bf16[256,4096]{1,0:T(8,128)(2,1)} %bitcast.2), channel_id=1, source_target_pairs={{0,1},{1,0},{2,3},{3,2},{4,5},{5,4},{6,7},{7,6},{8,9},{9,8},{10,11... | collective-permute-start | bytes 6291464 | tf_op jit(solution)/shard_map/ppermute | solution.py:28
  2.9 9.9 %collective-permute-start.4 = (bf16[256,2048]{1,0:T(8,128)(2,1)}, bf16[256,2048]{1,0:T(8,128)(2,1)S(1)}, u32[]{:S(2)}, u32[]{:S(2)}) collective-permute-start(bf16[256,2048]{1,0:T(8,128)(2,1)} %bitcast.6), channel_id=1, source_target_pairs={{0,1},{1,0},{2,3},{3,2},{4,5},{5,4},{6,7},{7,6},{8,9},{9,8},{10,11... | collective-permute-start | bytes 3145736 | tf_op jit(solution)/shard_map/ppermute | solution.py:28
  4.0 13.0 %collective-permute-start.1 = (bf16[1024,128]{1,0:T(8,128)(2,1)S(1)}, bf16[1024,128]{1,0:T(8,128)(2,1)}, u32[]{:S(2)}, u32[]{:S(2)}) collective-permute-start(bf16[1024,128]{1,0:T(8,128)(2,1)S(1)} %pad_maximum_fusion.refs_2_), channel_id=1, source_target_pairs={{0,8},{8,0},{16,24},{24,16},{1,9},{9,1},{17,25},{25,17},{2,10},{10... | collective-permute-start | bytes 786440 | tf_op jit(solution)/shard_map/ppermute | solution.py:24
  6.9 10.1 %collective-permute-start.2 = (bf16[1024,128]{1,0:T(8,128)(2,1)S(1)}, bf16[1024,128]{1,0:T(8,128)(2,1)}, u32[]{:S(2)}, u32[]{:S(2)}) collective-permute-start(bf16[1024,128]{1,0:T(8,128)(2,1)S(1)} %pad_maximum_fusion.refs_2_), channel_id=1, source_target_pairs={{0,16},{8,24},{16,0},{24,8},{1,17},{9,25},{17,1},{25,9},{2,18},{10... | collective-permute-start | bytes 786440 | tf_op jit(solution)/shard_map/ppermute | solution.py:24
  9.2 10.0 %collective-permute-start.6 = (bf16[1024,128]{1,0:T(8,128)(2,1)S(1)}, bf16[1024,128]{1,0:T(8,128)(2,1)S(1)}, u32[]{:S(2)}, u32[]{:S(2)}) collective-permute-start(bf16[1024,128]{1,0:T(8,128)(2,1)S(1)} %pad_maximum_fusion.refs_2_), channel_id=1, source_target_pairs={{0,6},{1,7},{2,4},{3,5},{4,2},{5,3},{6,0},{7,1},{8,14},{9,15},{10,... | collective-permute-start | bytes 786440 | tf_op jit(solution)/shard_map/ppermute | solution.py:43
  17.0 7.8 %collective-permute-start.7 = (bf16[1024,128]{1,0:T(8,128)(2,1)}, bf16[1024,128]{1,0:T(8,128)(2,1)S(1)}, u32[]{:S(2)}, u32[]{:S(2)}) collective-permute-start(bf16[1024,128]{1,0:T(8,128)(2,1)} %collective-permute-done.1.refs_2_), channel_id=1, source_target_pairs={{0,16},{8,24},{16,0},{24,8},{1,17},{9,25},{17,1},{25,9},{2,18},{10... | collective-permute-start | bytes 786440 | tf_op jit(solution)/shard_map/ppermute | solution.py:24
  17.6 8.3 %collective-permute-start.5 = (bf16[1024,128]{1,0:T(8,128)(2,1)S(1)}, bf16[1024,128]{1,0:T(8,128)(2,1)S(1)}, u32[]{:S(2)}, u32[]{:S(2)}) collective-permute-start(bf16[1024,128]{1,0:T(8,128)(2,1)S(1)} %pad_maximum_fusion.refs_2_), channel_id=1, source_target_pairs={{0,2},{1,3},{2,0},{3,1},{4,6},{5,7},{6,4},{7,5},{8,10},{9,11},{10,... | collective-permute-start | bytes 786440 | tf_op jit(solution)/shard_map/ppermute | solution.py:37
  19.2 11.3 %collective-permute-start.8 = (bf16[1024,128]{1,0:T(8,128)(2,1)S(1)}, bf16[1024,128]{1,0:T(8,128)(2,1)S(1)}, u32[]{:S(2)}, u32[]{:S(2)}) collective-permute-start(bf16[1024,128]{1,0:T(8,128)(2,1)S(1)} %collective-permute-done.6.refs_4_), channel_id=1, source_target_pairs={{0,2},{1,3},{2,0},{3,1},{4,6},{5,7},{6,4},{7,5},{8,10},{9,11},{10,... | collective-permute-start | bytes 786440 | tf_op jit(solution)/shard_map/ppermute | solution.py:37
  24.8 9.2 %collective-permute-start.10 = (bf16[1024,128]{1,0:T(8,128)(2,1)S(1)}, bf16[1024,128]{1,0:T(8,128)(2,1)S(1)}, u32[]{:S(2)}, u32[]{:S(2)}) collective-permute-start(bf16[1024,128]{1,0:T(8,128)(2,1)S(1)} %collective-permute-done.6.refs_4_), channel_id=1, source_target_pairs={{0,16},{8,24},{16,0},{24,8},{1,17},{9,25},{17,1},{25,9},{2,18},{10... | collective-permute-start | bytes 786440 | tf_op jit(solution)/shard_map/ppermute | solution.py:24
  25.3 12.4 %collective-permute-start.9 = (bf16[1024,128]{1,0:T(8,128)(2,1)S(1)}, bf16[1024,128]{1,0:T(8,128)(2,1)S(1)}, u32[]{:S(2)}, u32[]{:S(2)}) collective-permute-start(bf16[1024,128]{1,0:T(8,128)(2,1)S(1)} %collective-permute-done.6.refs_4_), channel_id=1, source_target_pairs={{0,8},{8,0},{16,24},{24,16},{1,9},{9,1},{17,25},{25,17},{2,10},{10... | collective-permute-start | bytes 786440 | tf_op jit(solution)/shard_map/ppermute | solution.py:24
  25.9 13.8 %collective-permute-start.11 = (bf16[1024,128]{1,0:T(8,128)(2,1)S(1)}, bf16[1024,128]{1,0:T(8,128)(2,1)S(1)}, u32[]{:S(2)}, u32[]{:S(2)}) collective-permute-start(bf16[1024,128]{1,0:T(8,128)(2,1)S(1)} %collective-permute-done.5.refs_3_), channel_id=1, source_target_pairs={{0,16},{8,24},{16,0},{24,8},{1,17},{9,25},{17,1},{25,9},{2,18},{10... | collective-permute-start | bytes 786440 | tf_op jit(solution)/shard_map/ppermute | solution.py:24
  28.0 12.1 %collective-permute-start.13 = (bf16[1024,128]{1,0:T(8,128)(2,1)S(1)}, bf16[1024,128]{1,0:T(8,128)(2,1)S(1)}, u32[]{:S(2)}, u32[]{:S(2)}) collective-permute-start(bf16[1024,128]{1,0:T(8,128)(2,1)S(1)} %collective-permute-done.5.refs_3_), channel_id=1, source_target_pairs={{0,8},{8,0},{16,24},{24,16},{1,9},{9,1},{17,25},{25,17},{2,10},{10... | collective-permute-start | bytes 786440 | tf_op jit(solution)/shard_map/ppermute | solution.py:24
  30.4 12.4 %collective-permute-start.14 = (bf16[1024,128]{1,0:T(8,128)(2,1)S(1)}, bf16[1024,128]{1,0:T(8,128)(2,1)S(1)}, u32[]{:S(2)}, u32[]{:S(2)}) collective-permute-start(bf16[1024,128]{1,0:T(8,128)(2,1)S(1)} %collective-permute-done.8.refs_1_), channel_id=1, source_target_pairs={{0,8},{8,0},{16,24},{24,16},{1,9},{9,1},{17,25},{25,17},{2,10},{10... | collective-permute-start | bytes 786440 | tf_op jit(solution)/shard_map/ppermute | solution.py:24
  34.1 8.8 %collective-permute-start.15 = (bf16[1024,128]{1,0:T(8,128)(2,1)S(1)}, bf16[1024,128]{1,0:T(8,128)(2,1)S(1)}, u32[]{:S(2)}, u32[]{:S(2)}) collective-permute-start(bf16[1024,128]{1,0:T(8,128)(2,1)S(1)} %collective-permute-done.8.refs_1_), channel_id=1, source_target_pairs={{0,16},{8,24},{16,0},{24,8},{1,17},{9,25},{17,1},{25,9},{2,18},{10... | collective-permute-start | bytes 786440 | tf_op jit(solution)/shard_map/ppermute | solution.py:24
  37.8 6.8 %collective-permute-start.16 = (bf16[512,128]{1,0:T(8,128)(2,1)S(1)}, bf16[512,128]{1,0:T(8,128)(2,1)S(1)}, u32[]{:S(2)}, u32[]{:S(2)}) collective-permute-start(bf16[512,128]{1,0:T(8,128)(2,1)S(1)} %shard_map.79.near_a), channel_id=1, source_target_pairs={{0,2},{1,3},{2,4},{3,5},{4,6},{5,7},{6,0},{7,1},{8,10},{9,11},{10,... | collective-permute-start | bytes 393224 | tf_op jit(solution)/shard_map/ppermute | solution.py:33
  45.0 9.5 %collective-permute-start.17 = (bf16[1408,128]{1,0:T(8,128)(2,1)S(1)}, bf16[1408,128]{1,0:T(8,128)(2,1)S(1)}, u32[]{:S(2)}, u32[]{:S(2)}) collective-permute-start(bf16[1408,128]{1,0:T(8,128)(2,1)S(1)} %shard_map.81.near_b.near_a), channel_id=1, source_target_pairs={{0,2},{1,3},{2,4},{3,5},{4,6},{5,7},{6,0},{7,1},{8,10},{9,11},{10,... | collective-permute-start | bytes 1081352 | tf_op jit(solution)/shard_map/ppermute | solution.py:33
  45.1 6.8 %collective-permute-start.12 = (bf16[1024,128]{1,0:T(8,128)(2,1)S(1)}, bf16[1024,128]{1,0:T(8,128)(2,1)S(1)}, u32[]{:S(2)}, u32[]{:S(2)}) collective-permute-start(bf16[1024,128]{1,0:T(8,128)(2,1)S(1)} %collective-permute-done.11.refs_6_), channel_id=1, source_target_pairs={{0,8},{8,0},{16,24},{24,16},{1,9},{9,1},{17,25},{25,17},{2,10},{10... | collective-permute-start | bytes 786440 | tf_op jit(solution)/shard_map/ppermute | solution.py:24
  46.0 8.4 %collective-permute-start.18 = (bf16[1024,128]{1,0:T(8,128)(2,1)S(1)}, bf16[1024,128]{1,0:T(8,128)(2,1)S(1)}, u32[]{:S(2)}, u32[]{:S(2)}) collective-permute-start(bf16[1024,128]{1,0:T(8,128)(2,1)S(1)} %collective-permute-done.14.refs_1_), channel_id=1, source_target_pairs={{0,16},{8,24},{16,0},{24,8},{1,17},{9,25},{17,1},{25,9},{2,18},{10... | collective-permute-start | bytes 786440 | tf_op jit(solution)/shard_map/ppermute | solution.py:24
  47.2 7.2 %collective-permute-start.19 = (bf16[512,128]{1,0:T(8,128)(2,1)S(1)}, bf16[512,128]{1,0:T(8,128)(2,1)S(1)}, u32[]{:S(2)}, u32[]{:S(2)}) collective-permute-start(bf16[512,128]{1,0:T(8,128)(2,1)S(1)} %slice.9), channel_id=1, source_target_pairs={{0,16},{8,24},{16,0},{24,8},{1,17},{9,25},{17,1},{25,9},{2,18},{10... | collective-permute-start | bytes 393224 | tf_op jit(solution)/shard_map/ppermute | solution.py:24
  48.1 6.3 %collective-permute-start.20 = (bf16[512,128]{1,0:T(8,128)(2,1)S(1)}, bf16[512,128]{1,0:T(8,128)(2,1)S(1)}, u32[]{:S(2)}, u32[]{:S(2)}) collective-permute-start(bf16[512,128]{1,0:T(8,128)(2,1)S(1)} %slice.10), channel_id=1, source_target_pairs={{0,8},{8,0},{16,24},{24,16},{1,9},{9,1},{17,25},{25,17},{2,10},{10... | collective-permute-start | bytes 393224 | tf_op jit(solution)/shard_map/ppermute | solution.py:24
  55.2 9.1 %collective-permute-start.21 = (bf16[1280,128]{1,0:T(8,128)(2,1)S(1)}, bf16[1280,128]{1,0:T(8,128)(2,1)S(1)}, u32[]{:S(2)}, u32[]{:S(2)}) collective-permute-start(bf16[1280,128]{1,0:T(8,128)(2,1)S(1)} %shard_map.84.near_b), channel_id=1, source_target_pairs={{0,2},{1,3},{2,4},{3,5},{4,6},{5,7},{6,0},{7,1},{8,10},{9,11},{10,... | collective-permute-start | bytes 983048 | tf_op jit(solution)/shard_map/ppermute | solution.py:33
  64.3 6.5 %collective-permute-start.22 = (bf16[384,128]{1,0:T(8,128)(2,1)S(1)}, bf16[384,128]{1,0:T(8,128)(2,1)S(1)}, u32[]{:S(2)}, u32[]{:S(2)}) collective-permute-start(bf16[384,128]{1,0:T(8,128)(2,1)S(1)} %slice.12), channel_id=1, source_target_pairs={{0,2},{1,3},{2,4},{3,5},{4,6},{5,7},{6,0},{7,1},{8,10},{9,11},{10,... | collective-permute-start | bytes 294920 | tf_op jit(solution)/shard_map/ppermute | solution.py:33
  66.1 7.5 %collective-permute-start.23 = (bf16[256,512]{1,0:T(8,128)(2,1)S(1)}, bf16[256,512]{1,0:T(8,128)(2,1)S(1)}, u32[]{:S(2)}, u32[]{:S(2)}) collective-permute-start(bf16[256,512]{1,0:T(8,128)(2,1)S(1)} %get-tuple-element.72), channel_id=1, source_target_pairs={{0,1},{1,0},{2,3},{3,2},{4,5},{5,4},{6,7},{7,6},{8,9},{9,8},{10,11... | collective-permute-start | bytes 786440 | tf_op jit(solution)/shard_map/ppermute | solution.py:28
  (7 other events, 40.9 us)

commit v5 on v4

--- a/solution.py
+++ b/solution.py
@@ -15,6 +15,7 @@
 MAXDOC = 8
 GROUP = QH // KVH
 LANES = GROUP * BLK
+KEPT = (1, 2, 3)
 VMEM_LIMIT = 20 * 1024 * 1024
 SCALE = 1.0 / math.sqrt(HD)
 LOG2E = 1.0 / math.log(2.0)
@@ -84,7 +85,7 @@
                 if whole:
                     piece = tokens[side][:, group_columns(step, half)]
                 else:
-                    at = (2 * (step - steps[0]) + half) * depth
+                    at = (2 * (step - KEPT[0]) + half) * depth
                     piece = tokens[0][side * rows : (side + 1) * rows, at : at + depth]
                 parts = [weights[s * len(steps) + position][half] for s in range(sets)]
                 weight = jnp.concatenate([array[at : at + depth, :] for array, at in parts], axis=1)
@@ -108,7 +109,9 @@
         at += end - begin
 
 
-def project(tokens, steps, sets, total=None, last=True, passed=(), extra=None, keep=()):
+def project(
+    tokens, steps, sets, total=None, last=True, passed=(), extra=None, keep=(), cost=1
+):
     whole = len(tokens) == 2
     rows = tokens[0].shape[0] * len(tokens)
     weights = []
@@ -143,8 +146,8 @@
         out_specs=(spec,) * len(out),
         compiler_params=pltpu.CompilerParams(vmem_limit_bytes=VMEM_LIMIT),
         cost_estimate=pl.CostEstimate(
-            flops=4 * rows * depth * HD * len(steps) * count,
-            bytes_accessed=4 * rows * depth * len(steps),
+            flops=4 * rows * depth * HD * len(steps) * count * cost,
+            bytes_accessed=4 * rows * depth * len(steps) * cost,
             transcendentals=0,
         ),
     )(*tokens, *weights, *extras)
@@ -294,19 +297,25 @@
         low, high = range(half), range(half, MAXDOC)
         stat[item, 0:1, :] = score_blocks(keys, rows, low, found, causal, table)
 
-        @pl.when(found > half)
-        def _():
+        few = jnp.logical_and(found > half, found <= half + 2)
+        many = found > half + 2
+
+        def score_rest(steps):
             stat[item, 0:1, :] = jnp.maximum(
-                stat[item, 0:1, :], score_blocks(keys, rows, high, found, None, table)
+                stat[item, 0:1, :], score_blocks(keys, rows, steps, found, None, table)
             )
 
-        stat[item, 1:2, :], summed[item] = weigh_blocks(values, low, stat[item, 0:1, :], table)
-
-        @pl.when(found > half)
-        def _():
-            more, part = weigh_blocks(values, high, stat[item, 0:1, :], table)
+        def weigh_rest(steps):
+            more, part = weigh_blocks(values, steps, stat[item, 0:1, :], table)
             stat[item, 1:2, :] += more
             summed[item] += part
+
+        pl.when(few)(functools.partial(score_rest, high[:2]))
+        pl.when(many)(functools.partial(score_rest, high))
+        stat[item, 1:2, :], summed[item] = weigh_blocks(values, low, stat[item, 0:1, :], table)
+
+        pl.when(few)(functools.partial(weigh_rest, high[:2]))
+        pl.when(many)(functools.partial(weigh_rest, high))
 
 
 def far_kernel(
@@ -318,18 +327,26 @@
     queries_ref,
     far_a,
     far_b,
-    out_own,
-    out_other,
-    stats_own,
-    stats_other,
-    kv,
-    table,
-    top,
-    total,
-    summed,
-    places,
+    *refs,
 ):
+    before_own, before_other = refs[:2] if second else (None, None)
+    (
+        out_own,
+        out_other,
+        stats_own,
+        stats_other,
+        kv,
+        table,
+        top,
+        total,
+        summed,
+        places,
+    ) = refs[2 * second :]
     core, _, kind, _ = where_am_i(second)
+    if second:
+        dev = before_own.shape[0]
+        stats_own[dev:, :, :] = before_own[...]
+        stats_other[dev:, :, :] = before_other[...]
     pair_blocks = queries_ref.shape[1]
     dev_blocks = pair_blocks // 2
     far_blocks = (MAXDOC - 1) % pair_blocks
@@ -421,7 +438,7 @@
     )(facts, queries, near_a, near_b, back_a, back_b)
 
 
-def attend_far(second, facts, queries, carried, first_set, second_set):
+def attend_far(second, facts, queries, carried, first_set, second_set, before=()):
     vmem = pl.BlockSpec(memory_space=pltpu.VMEM)
     smem = pl.BlockSpec(memory_space=pltpu.SMEM)
     items = queries.shape[1]
@@ -431,11 +448,11 @@
     (_, _, far_a), start_a = first_set
     (_, _, far_b), start_b = second_set
     out = jax.ShapeDtypeStruct((rows, LANES), jnp.bfloat16)
-    stats = jax.ShapeDtypeStruct((dev_blocks, GROUP, BLK), jnp.float32)
+    stats = jax.ShapeDtypeStruct(((1 + second) * dev_blocks, GROUP, BLK), jnp.float32)
     return pl.pallas_call(
         functools.partial(far_kernel, second, (start_a, start_b)),
         out_shape=(out, out, stats, stats),
-        in_specs=[smem] + [vmem] * 5,
+        in_specs=[smem] + [vmem] * (5 + len(before)),
         out_specs=(vmem,) * 4,
         scratch_shapes=[
             pltpu.VMEM((2, far_blocks * BLK, HD), jnp.bfloat16),
@@ -451,12 +468,10 @@
             bytes_accessed=8 * rows * LANES,
             transcendentals=items * far_blocks * BLK * LANES,
         ),
-    )(facts, *carried, queries, far_a, far_b)
-
-
-def finish_kernel(
-    own_a, own_b, got_a, got_b, st_own_a, st_own_b, st_got_a, st_got_b, out_ref, stats_ref
-):
+    )(facts, *carried, queries, far_a, far_b, *before)
+
+
+def finish_kernel(own_a, own_b, got_a, got_b, st_own, st_got, out_ref, stats_ref):
     core = lax.axis_index("ctx") % 2
     column = lax.axis_index("dp") % 2
     pieces = (
@@ -471,9 +486,8 @@
     for head in range(KVH):
         is_a = head // 2 == column
         is_own = head % 2 == core
-        own = jnp.where(is_a, st_own_a[...], st_own_b[...])
-        got = jnp.where(is_a, st_got_a[...], st_got_b[...])
-        lse = jnp.where(is_own, own, got)
+        both = jnp.where(is_own, st_own[...], st_got[...])
+        lse = jnp.where(is_a, both[both.shape[0] // 2 :], both[: both.shape[0] // 2])
         for place in range(lse.shape[0]):
             stats_ref[0, head * GROUP : (head + 1) * GROUP, place * BLK : (place + 1) * BLK] = lse[place]
 
@@ -499,7 +513,6 @@
     spare = tall - (MAXDOC - 1) % (tall // BLK) * BLK
     short = tall - spare
     step_xy = ((spare, tall),)
-    step_d = ((spare, tall), (tall + spare, 2 * tall))
     if slots == 4:
 
         def multiply(steps, sets, *rest, **more):
@@ -529,7 +542,7 @@
         def diagonal(x, y):
             return over_dp(x[:half], 2), over_dp(y[half:], 1)
 
-        own_sum, kept = multiply((0, 1, 3), [[slab, z1, z3]], last=False, keep=(2, 3))
+        own_sum, kept = multiply((0, 1, 3), [[slab, z1, z3]], last=False, keep=KEPT)
         d1 = over_dp(y1, 1)
         x2 = over_dp(z2, 1)
         y2 = over_dp(z2, 2)
@@ -540,13 +553,15 @@
         xy_sum, x2, y2, x3, y3 = tie(xy_sum, x2, y2, x3, y3)
         d2 = over_dp(x2, 2)
         d3 = diagonal(x3, y3)
-        xy_near = multiply_kept((2,), [[x2], [y2]], xy_sum, passed=step_xy, extra=own_back)
+        xy_near = multiply_kept(
+            (2,), [[x2], [y2]], xy_sum, passed=step_xy, extra=own_back, cost=0
+        )
         xy_back = around(xy_near, 1)
-        d0, d1, xy_near = tie(d0, d1, xy_near)
-        d_sum = multiply((0, 1), [[d0, d1]], last=False)
-        d_near = multiply_kept((2, 3), [[d2, d3]], d_sum, passed=step_d, extra=xy_back)
+        d_sum = multiply((0,), [[d0]], last=False, cost=0)
+        xy_far = around(xy_back[spare : 2 * tall], 1)
+        d_near = multiply_kept((1, 2, 3), [[d1, d2, d3]], d_sum)
         d_back = around(d_near, 1)
-        d_far = around(d_back[spare:tall], 1)
+        d_far = around(d_back[spare:], 1)
     else:
         stacked, facts = stack(doc_blocks, block_mask, plan, own_queries, other_queries)
         even = jnp.where(core == 0, mine, others)
@@ -575,20 +590,21 @@
         own_back = around(own_near, 1)
         xy_near = multiply([x_set, y_set], step_xy, own_back)
         xy_back = around(xy_near, 1)
-        d_near = multiply([d_set], step_d, xy_back)
+        d_near = multiply([d_set])
+        xy_far = around(xy_back[spare : 2 * tall], 1)
         d_back = around(d_near, 1)
-        d_far = around(d_back[spare:tall], 1)
+        d_far = around(d_back[spare:], 1)
 
     own_set = (own_near, own_back, xy_back), (0, 0, 2 * tall)
-    y_set = (xy_near, xy_back, d_back), (tall, tall, tall + short)
-    x_set = (xy_near, xy_back, d_back), (0, 0, tall)
+    y_set = (xy_near, xy_back, xy_far), (tall, tall, tall)
+    x_set = (xy_near, xy_back, xy_far), (0, 0, 0)
     d_set = (d_near, d_back, d_far), (0, 0, 0)
     near_a = attend_near(0, facts, stacked, own_set, y_set)
     near_b = attend_near(1, facts, stacked, x_set, d_set)
     first = attend_far(0, facts, stacked, near_a, own_set, y_set)
-    second = attend_far(1, facts, stacked, near_b, x_set, d_set)
+    second = attend_far(1, facts, stacked, near_b, x_set, d_set, first[2:])
     got_a, got_b = other_core(first[1]), other_core(second[1])
-    st_got_a, st_got_b = other_core(first[3]), other_core(second[3])
+    st_got = other_core(second[3])
     vmem = pl.BlockSpec(memory_space=pltpu.VMEM)
     return pl.pallas_call(
         finish_kernel,
@@ -596,10 +612,10 @@
             jax.ShapeDtypeStruct((1, rows, QH * HD), jnp.bfloat16),
             jax.ShapeDtypeStruct((1, QH, rows), jnp.float32),
         ),
-        in_specs=[vmem] * 8,
+        in_specs=[vmem] * 6,
         out_specs=(vmem, vmem),
         compiler_params=pltpu.CompilerParams(vmem_limit_bytes=VMEM_LIMIT),
-    )(first[0], second[0], got_a, got_b, first[2], second[2], st_got_a, st_got_b)
+    )(first[0], second[0], got_a, got_b, second[2], st_got)
 
 
 def solution(mesh):

time: 75.1 us -> 73.3 us (0.976)
  waiting for transfers between devices: 20.6 us -> 16.6 us
  starting transfers between devices: 28.2 us -> 30.4 us
    ppermute x4 -> x5, waiting for transfers between devices: 7.09 us -> 2.65 us  [around(): lax.ppermute(array, 'ctx', [(i, (i + 2 * pairs) % size) for i in range(si...]
    ppermute x4 -> x5, starting transfers between devices: 2.86 us -> 5.13 us  [around(): lax.ppermute(array, 'ctx', [(i, (i + 2 * pairs) % size) for i in range(si...]
    ppermute x7 -> x6, waiting for transfers between devices: 2.47 us -> 2.72 us  [other_core(): lax.ppermute(array, 'ctx', [(i, i ^ 1) for i in range(lax.axis_size('ctx'...]
    ppermute x7 -> x6, starting transfers between devices: 1.75 us -> 1.67 us  [other_core(): lax.ppermute(array, 'ctx', [(i, i ^ 1) for i in range(lax.axis_size('ctx'...]
  transfers between devices with their start and end apart: 27 -> 27, of which waited for: 15 -> 13; matrix products, arithmetic and copies ran while one was open for 2% -> 2% of each run, Pallas kernels for 25% -> 25%
where the time goes in v5:
time: 73.3 us; the launch traced here: 72.9 us
  starting transfers between devices  30.4 us (41%)
  Pallas kernels  20.8 us (28%)
  waiting for transfers between devices  16.6 us (23%)
  local copies, waits for them, and re-layouts  4.27 us (6%)
  between operations  0.83 us (1%)
    ppermute x13, starting transfers between devices, over_dp(): lax.ppermute(array, 'dp', [(i, i ^ mask) for i in range(lax.axis_size('dp...  14.4 us
    pallas_call x6, Pallas kernels, project(): pl.pallas_call(functools.partial(project_kernel, steps, count, passed, to...  9.31 us
    ppermute x13, waiting for transfers between devices, over_dp(): lax.ppermute(array, 'dp', [(i, i ^ mask) for i in range(lax.axis_size('dp...  8.68 us
    pallas_call x2, Pallas kernels, attend_near(): pl.pallas_call(functools.partial(near_kernel, second, (start_a, start_b))...  6.58 us
    ppermute x2, starting transfers between devices, neighbours(): lax.ppermute(array, 'ctx', [(i, i ^ 2) for i in range(lax.axis_size('ctx'...  5.64 us
    ppermute x5, starting transfers between devices, around(): lax.ppermute(array, 'ctx', [(i, (i + 2 * pairs) % size) for i in range(si...  5.13 us
    ppermute x1, starting transfers between devices, mirrored(): return lax.ppermute(array, 'ctx', pairs)  3.6 us
    unnamed x9, local copies, waits for them, and re-layouts  3.3 us
  transfers between devices with their start and end apart: 27, of which 13 were waited for; matrix products, arithmetic and copies ran while one was open for 2% of the time, Pallas kernels for 25%

profile of v5, /device:TPU:0, one launch (start us, length us, event | category | flops | bytes accessed | tf_op | source)
XLA Modules:
  0.0 72.9 jit_solution(5057603485250896673)
XLA Ops:
  1.2 1.4 %collective-permute-done = bf16[512,256]{1,0:T(8,128)(2,1)S(1)} collective-permute-done((bf16[512,256]{1,0:T(8,128)(2,1)}, bf16[512,256]{1,0:T(8,128)(2,1)S(1)}, u32[]{:S(2)}, u32[]{:S(2)}) %collective-permute-start) | collective-permute-done | bytes 262176 | tf_op jit(solution)/shard_map/ppermute | solution.py:29
  4.0 2.9 %collective-permute-start.1 = (bf16[1024,128]{1,0:T(8,128)(2,1)S(1)}, bf16[1024,128]{1,0:T(8,128)(2,1)}, u32[]{:S(2)}, u32[]{:S(2)}) collective-permute-start(bf16[1024,128]{1,0:T(8,128)(2,1)S(1)} %pad_maximum_fusion.refs_2_), channel_id=1, source_target_pairs={{0,8},{8,0},{16,24},{24,16},{1,9},{9,1},{17,25},{25,17},{2,10},{10... | collective-permute-start | bytes 786440 | tf_op jit(solution)/shard_map/ppermute | solution.py:25
  6.9 1.5 %collective-permute-start.2 = (bf16[1024,128]{1,0:T(8,128)(2,1)S(1)}, bf16[1024,128]{1,0:T(8,128)(2,1)}, u32[]{:S(2)}, u32[]{:S(2)}) collective-permute-start(bf16[1024,128]{1,0:T(8,128)(2,1)S(1)} %pad_maximum_fusion.refs_2_), channel_id=1, source_target_pairs={{0,16},{8,24},{16,0},{24,8},{1,17},{9,25},{17,1},{25,9},{2,18},{10... | collective-permute-start | bytes 786440 | tf_op jit(solution)/shard_map/ppermute | solution.py:25
  9.2 3.6 %collective-permute-start.6 = (bf16[1024,128]{1,0:T(8,128)(2,1)S(1)}, bf16[1024,128]{1,0:T(8,128)(2,1)S(1)}, u32[]{:S(2)}, u32[]{:S(2)}) collective-permute-start(bf16[1024,128]{1,0:T(8,128)(2,1)S(1)} %pad_maximum_fusion.refs_2_), channel_id=1, source_target_pairs={{0,6},{1,7},{2,4},{3,5},{4,2},{5,3},{6,0},{7,1},{8,14},{9,15},{10,... | collective-permute-start | bytes 786440 | tf_op jit(solution)/shard_map/ppermute | solution.py:44
  15.4 1.6 %shard_map.77 = (bf16[2,4,512,128]{3,2,1,0:T(8,128)(2,1)S(1)}, s32[4,9]{1,0:T(4,128)S(1)}) custom-call(s32[1,4]{1,0:T(1,128)S(1)} %copy-done.2, s32[1,16,7]{2,1,0:T(8,128)S(1)} %copy.8.mask_ref, s32[1,16]{1,0:T(1,128)S(1)} %copy-done.3, bf16[256,2048]{1,0:T(8,128)(2,1)S(1)} %bitcast.7, bf16[256,2048]{1,0:T(8,128)(2,1)S(1)} %collective-permute-done.4.q_other_ref), custom_call_target="tpu_custom_call" | custom-call | bytes 1048576 | tf_op jit(solution)/shard_map/pallas_call | solution.py:236
  19.2 5.0 %collective-permute-start.8 = (bf16[1024,128]{1,0:T(8,128)(2,1)S(1)}, bf16[1024,128]{1,0:T(8,128)(2,1)S(1)}, u32[]{:S(2)}, u32[]{:S(2)}) collective-permute-start(bf16[1024,128]{1,0:T(8,128)(2,1)S(1)} %collective-permute-done.6.refs_4_), channel_id=1, source_target_pairs={{0,2},{1,3},{2,0},{3,1},{4,6},{5,7},{6,4},{7,5},{8,10},{9,11},{10,... | collective-permute-start | bytes 786440 | tf_op jit(solution)/shard_map/ppermute | solution.py:38
  25.9 1.5 %collective-permute-start.11 = (bf16[1024,128]{1,0:T(8,128)(2,1)S(1)}, bf16[1024,128]{1,0:T(8,128)(2,1)S(1)}, u32[]{:S(2)}, u32[]{:S(2)}) collective-permute-start(bf16[1024,128]{1,0:T(8,128)(2,1)S(1)} %collective-permute-done.5.refs_3_), channel_id=1, source_target_pairs={{0,8},{8,0},{16,24},{24,16},{1,9},{9,1},{17,25},{25,17},{2,10},{10... | collective-permute-start | bytes 786440 | tf_op jit(solution)/shard_map/ppermute | solution.py:25
  27.3 1.5 %collective-permute-start.12 = (bf16[1024,128]{1,0:T(8,128)(2,1)S(1)}, bf16[1024,128]{1,0:T(8,128)(2,1)S(1)}, u32[]{:S(2)}, u32[]{:S(2)}) collective-permute-start(bf16[1024,128]{1,0:T(8,128)(2,1)S(1)} %collective-permute-done.5.refs_3_), channel_id=1, source_target_pairs={{0,16},{8,24},{16,0},{24,8},{1,17},{9,25},{17,1},{25,9},{2,18},{10... | collective-permute-start | bytes 786440 | tf_op jit(solution)/shard_map/ppermute | solution.py:25
  28.9 1.6 %collective-permute-done.8.refs_1_ = bf16[1024,128]{1,0:T(8,128)(2,1)S(1)} collective-permute-done((bf16[1024,128]{1,0:T(8,128)(2,1)S(1)}, bf16[1024,128]{1,0:T(8,128)(2,1)S(1)}, u32[]{:S(2)}, u32[]{:S(2)}) %collective-permute-start.8) | collective-permute-done | bytes 262176 | tf_op jit(solution)/shard_map/ppermute | solution.py:38
  31.0 3.1 %collective-permute-done.10.refs_7_ = bf16[1024,128]{1,0:T(8,128)(2,1)S(1)} collective-permute-done((bf16[1024,128]{1,0:T(8,128)(2,1)S(1)}, bf16[1024,128]{1,0:T(8,128)(2,1)S(1)}, u32[]{:S(2)}, u32[]{:S(2)}) %collective-permute-start.10) | collective-permute-done | bytes 262176 | tf_op jit(solution)/shard_map/ppermute | solution.py:25
  34.6 2.8 %shard_map.78 = (f32[512,128]{1,0:T(8,128)S(1)}, bf16[512,3072]{1,0:T(8,128)(2,1)S(1)}) custom-call(bf16[256,4096]{1,0:T(8,128)(2,1)S(1)} %bitcast.3, bf16[256,4096]{1,0:T(8,128)(2,1)} %collective-permute-done.3.refs_1_, bf16[1024,128]{1,0:T(8,128)(2,1)S(1)} %pad_maximum_fusion.refs_2_, bf16[1024,128]{1,0:T(8,128)(2,1)S(1)} %collective-permute-done.5.refs_3_, ...), custom_call_target="tpu_custom_call" | custom-call | flops 402653184 | bytes 3145728 | tf_op jit(solution)/shard_map/pallas_call | solution.py:133
  38.2 1.8 %collective-permute-done.11.refs_3_ = bf16[1024,128]{1,0:T(8,128)(2,1)S(1)} collective-permute-done((bf16[1024,128]{1,0:T(8,128)(2,1)S(1)}, bf16[1024,128]{1,0:T(8,128)(2,1)S(1)}, u32[]{:S(2)}, u32[]{:S(2)}) %collective-permute-start.11) | collective-permute-done | bytes 262176 | tf_op jit(solution)/shard_map/ppermute | solution.py:25
  40.1 2.7 %shard_map.80.refs_3_ = f32[512,256]{1,0:T(8,128)S(1)} custom-call(bf16[256,4096]{1,0:T(8,128)(2,1)S(1)} %bitcast.4, bf16[256,4096]{1,0:T(8,128)(2,1)} %collective-permute-done.3.refs_1_, bf16[1024,128]{1,0:T(8,128)(2,1)} %collective-permute-done.1.refs_2_, bf16[1024,128]{1,0:T(8,128)(2,1)S(1)} %collective-permute-done.11.refs_3_, ...), custom_call_target="tpu_custom_call" | custom-call | flops 805306368 | bytes 3145728 | tf_op jit(solution)/shard_map/pallas_call | solution.py:133
  42.9 1.8 %collective-permute-done.15.refs_4_.back_a = bf16[512,128]{1,0:T(8,128)(2,1)S(1)} collective-permute-done((bf16[512,128]{1,0:T(8,128)(2,1)S(1)}, bf16[512,128]{1,0:T(8,128)(2,1)S(1)}, u32[]{:S(2)}, u32[]{:S(2)}) %collective-permute-start.15) | collective-permute-done | bytes 131104 | tf_op jit(solution)/shard_map/ppermute | solution.py:34
  46.0 1.2 %collective-permute-start.19 = (bf16[1024,128]{1,0:T(8,128)(2,1)S(1)}, bf16[1024,128]{1,0:T(8,128)(2,1)S(1)}, u32[]{:S(2)}, u32[]{:S(2)}) collective-permute-start(bf16[1024,128]{1,0:T(8,128)(2,1)S(1)} %collective-permute-done.13.refs_1_), channel_id=1, source_target_pairs={{0,16},{8,24},{16,0},{24,8},{1,17},{9,25},{17,1},{25,9},{2,18},{10... | collective-permute-start | bytes 786440 | tf_op jit(solution)/shard_map/ppermute | solution.py:25
  48.1 1.3 %collective-permute-start.21 = (bf16[512,128]{1,0:T(8,128)(2,1)S(1)}, bf16[512,128]{1,0:T(8,128)(2,1)S(1)}, u32[]{:S(2)}, u32[]{:S(2)}) collective-permute-start(bf16[512,128]{1,0:T(8,128)(2,1)S(1)} %slice.14), channel_id=1, source_target_pairs={{0,8},{8,0},{16,24},{24,16},{1,9},{9,1},{17,25},{25,17},{2,10},{10... | collective-permute-start | bytes 393224 | tf_op jit(solution)/shard_map/ppermute | solution.py:25
  49.4 2.0 %shard_map.84.refs_5_ = f32[512,128]{1,0:T(8,128)S(1)} custom-call(bf16[256,4096]{1,0:T(8,128)(2,1)S(1)} %bitcast.5, bf16[256,4096]{1,0:T(8,128)(2,1)} %collective-permute-done.3.refs_1_, bf16[1024,128]{1,0:T(8,128)(2,1)S(1)} %collective-permute-done.7.refs_2_), custom_call_target="tpu_custom_call" | custom-call | tf_op jit(solution)/shard_map/pallas_call | solution.py:133
  51.9 2.6 %collective-permute-done.20.refs_3_ = bf16[512,128]{1,0:T(8,128)(2,1)S(1)} collective-permute-done((bf16[512,128]{1,0:T(8,128)(2,1)S(1)}, bf16[512,128]{1,0:T(8,128)(2,1)S(1)}, u32[]{:S(2)}, u32[]{:S(2)}) %collective-permute-start.20) | collective-permute-done | bytes 131104 | tf_op jit(solution)/shard_map/ppermute | solution.py:25
  55.4 1.6 %collective-permute-start.22 = (bf16[512,128]{1,0:T(8,128)(2,1)S(1)}, bf16[512,128]{1,0:T(8,128)(2,1)S(1)}, u32[]{:S(2)}, u32[]{:S(2)}) collective-permute-start(bf16[512,128]{1,0:T(8,128)(2,1)S(1)} %shard_map.85.near_b), channel_id=1, source_target_pairs={{0,2},{1,3},{2,4},{3,5},{4,6},{5,7},{6,0},{7,1},{8,10},{9,11},{10,... | collective-permute-start | bytes 393224 | tf_op jit(solution)/shard_map/ppermute | solution.py:34
  57.1 1.6 %collective-permute-start.17 = (bf16[896,128]{1,0:T(8,128)(2,1)S(1)}, bf16[896,128]{1,0:T(8,128)(2,1)S(1)}, u32[]{:S(2)}, u32[]{:S(2)}) collective-permute-start(bf16[896,128]{1,0:T(8,128)(2,1)S(1)} %slice.16), channel_id=1, source_target_pairs={{0,2},{1,3},{2,4},{3,5},{4,6},{5,7},{6,0},{7,1},{8,10},{9,11},{10,... | collective-permute-start | bytes 688136 | tf_op jit(solution)/shard_map/ppermute | solution.py:34
  58.7 3.2 %shard_map.82 = (f32[4,128,512]{2,1,0:T(8,128)S(1)}, f32[4,8,512]{2,1,0:T(8,128)S(1)}) custom-call(s32[4,9]{1,0:T(4,128)S(1)} %get-tuple-element.42.facts, bf16[2,4,512,128]{3,2,1,0:T(8,128)(2,1)S(1)} %get-tuple-element.43.queries_ref, bf16[512,128]{1,0:T(8,128)(2,1)S(1)} %shard_map.79.near_a, bf16[1408,128]{1,0:T(8,128)(2,1)S(1)} %shard_map.81.near_b.near_a, ...), custom_call_target="tpu_custom_call" | custom-call | flops 1073741824 | bytes 4194304 | tf_op jit(solution)/shard_map/pallas_call | solution.py:419
  62.3 1.4 %collective-permute-start.23 = (bf16[384,128]{1,0:T(8,128)(2,1)S(1)}, bf16[384,128]{1,0:T(8,128)(2,1)S(1)}, u32[]{:S(2)}, u32[]{:S(2)}) collective-permute-start(bf16[384,128]{1,0:T(8,128)(2,1)S(1)} %slice.17), channel_id=1, source_target_pairs={{0,2},{1,3},{2,4},{3,5},{4,6},{5,7},{6,0},{7,1},{8,10},{9,11},{10,... | collective-permute-start | bytes 294920 | tf_op jit(solution)/shard_map/ppermute | solution.py:34
  63.7 3.4 %shard_map.86 = (f32[4,128,512]{2,1,0:T(8,128)S(1)}, f32[4,8,512]{2,1,0:T(8,128)S(1)}) custom-call(s32[4,9]{1,0:T(4,128)S(1)} %get-tuple-element.42.facts, bf16[2,4,512,128]{3,2,1,0:T(8,128)(2,1)S(1)} %get-tuple-element.43.queries_ref, bf16[1408,128]{1,0:T(8,128)(2,1)S(1)} %shard_map.81.near_b.near_a, bf16[512,128]{1,0:T(8,128)(2,1)S(1)} %shard_map.85.near_b, ...), custom_call_target="tpu_custom_call" | custom-call | flops 1073741824 | bytes 4194304 | tf_op jit(solution)/shard_map/pallas_call | solution.py:419
  70.5 1.3 %collective-permute-done.26.st_got = f32[4,4,128]{2,1,0:T(4,128)S(1)} collective-permute-done((f32[4,4,128]{2,1,0:T(4,128)S(1)}, f32[4,4,128]{2,1,0:T(4,128)S(1)}, u32[]{:S(2)}, u32[]{:S(2)}) %collective-permute-start.26) | collective-permute-done | bytes 8224 | tf_op jit(solution)/shard_map/ppermute | solution.py:29
  (58 shorter events, 19.7 us)
Async XLA Ops:
  2.5 14.5 %collective-permute-start.3 = (bf16[256,4096]{1,0:T(8,128)(2,1)}, bf16[256,4096]{1,0:T(8,128)(2,1)}, u32[]{:S(2)}, u32[]{:S(2)}) collective-permute-start(bf16[256,4096]{1,0:T(8,128)(2,1)} %bitcast.2), channel_id=1, source_target_pairs={{0,1},{1,0},{2,3},{3,2},{4,5},{5,4},{6,7},{7,6},{8,9},{9,8},{10,11... | collective-permute-start | bytes 6291464 | tf_op jit(solution)/shard_map/ppermute | solution.py:29
  2.9 9.9 %collective-permute-start.4 = (bf16[256,2048]{1,0:T(8,128)(2,1)}, bf16[256,2048]{1,0:T(8,128)(2,1)S(1)}, u32[]{:S(2)}, u32[]{:S(2)}) collective-permute-start(bf16[256,2048]{1,0:T(8,128)(2,1)} %bitcast.6), channel_id=1, source_target_pairs={{0,1},{1,0},{2,3},{3,2},{4,5},{5,4},{6,7},{7,6},{8,9},{9,8},{10,11... | collective-permute-start | bytes 3145736 | tf_op jit(solution)/shard_map/ppermute | solution.py:29
  4.0 13.0 %collective-permute-start.1 = (bf16[1024,128]{1,0:T(8,128)(2,1)S(1)}, bf16[1024,128]{1,0:T(8,128)(2,1)}, u32[]{:S(2)}, u32[]{:S(2)}) collective-permute-start(bf16[1024,128]{1,0:T(8,128)(2,1)S(1)} %pad_maximum_fusion.refs_2_), channel_id=1, source_target_pairs={{0,8},{8,0},{16,24},{24,16},{1,9},{9,1},{17,25},{25,17},{2,10},{10... | collective-permute-start | bytes 786440 | tf_op jit(solution)/shard_map/ppermute | solution.py:25
  6.9 10.1 %collective-permute-start.2 = (bf16[1024,128]{1,0:T(8,128)(2,1)S(1)}, bf16[1024,128]{1,0:T(8,128)(2,1)}, u32[]{:S(2)}, u32[]{:S(2)}) collective-permute-start(bf16[1024,128]{1,0:T(8,128)(2,1)S(1)} %pad_maximum_fusion.refs_2_), channel_id=1, source_target_pairs={{0,16},{8,24},{16,0},{24,8},{1,17},{9,25},{17,1},{25,9},{2,18},{10... | collective-permute-start | bytes 786440 | tf_op jit(solution)/shard_map/ppermute | solution.py:25
  9.2 10.0 %collective-permute-start.6 = (bf16[1024,128]{1,0:T(8,128)(2,1)S(1)}, bf16[1024,128]{1,0:T(8,128)(2,1)S(1)}, u32[]{:S(2)}, u32[]{:S(2)}) collective-permute-start(bf16[1024,128]{1,0:T(8,128)(2,1)S(1)} %pad_maximum_fusion.refs_2_), channel_id=1, source_target_pairs={{0,6},{1,7},{2,4},{3,5},{4,2},{5,3},{6,0},{7,1},{8,14},{9,15},{10,... | collective-permute-start | bytes 786440 | tf_op jit(solution)/shard_map/ppermute | solution.py:44
  17.0 7.8 %collective-permute-start.7 = (bf16[1024,128]{1,0:T(8,128)(2,1)}, bf16[1024,128]{1,0:T(8,128)(2,1)S(1)}, u32[]{:S(2)}, u32[]{:S(2)}) collective-permute-start(bf16[1024,128]{1,0:T(8,128)(2,1)} %collective-permute-done.1.refs_2_), channel_id=1, source_target_pairs={{0,16},{8,24},{16,0},{24,8},{1,17},{9,25},{17,1},{25,9},{2,18},{10... | collective-permute-start | bytes 786440 | tf_op jit(solution)/shard_map/ppermute | solution.py:25
  17.6 8.3 %collective-permute-start.5 = (bf16[1024,128]{1,0:T(8,128)(2,1)S(1)}, bf16[1024,128]{1,0:T(8,128)(2,1)S(1)}, u32[]{:S(2)}, u32[]{:S(2)}) collective-permute-start(bf16[1024,128]{1,0:T(8,128)(2,1)S(1)} %pad_maximum_fusion.refs_2_), channel_id=1, source_target_pairs={{0,2},{1,3},{2,0},{3,1},{4,6},{5,7},{6,4},{7,5},{8,10},{9,11},{10,... | collective-permute-start | bytes 786440 | tf_op jit(solution)/shard_map/ppermute | solution.py:38
  19.2 11.3 %collective-permute-start.8 = (bf16[1024,128]{1,0:T(8,128)(2,1)S(1)}, bf16[1024,128]{1,0:T(8,128)(2,1)S(1)}, u32[]{:S(2)}, u32[]{:S(2)}) collective-permute-start(bf16[1024,128]{1,0:T(8,128)(2,1)S(1)} %collective-permute-done.6.refs_4_), channel_id=1, source_target_pairs={{0,2},{1,3},{2,0},{3,1},{4,6},{5,7},{6,4},{7,5},{8,10},{9,11},{10,... | collective-permute-start | bytes 786440 | tf_op jit(solution)/shard_map/ppermute | solution.py:38
  24.8 9.2 %collective-permute-start.10 = (bf16[1024,128]{1,0:T(8,128)(2,1)S(1)}, bf16[1024,128]{1,0:T(8,128)(2,1)S(1)}, u32[]{:S(2)}, u32[]{:S(2)}) collective-permute-start(bf16[1024,128]{1,0:T(8,128)(2,1)S(1)} %collective-permute-done.6.refs_4_), channel_id=1, source_target_pairs={{0,16},{8,24},{16,0},{24,8},{1,17},{9,25},{17,1},{25,9},{2,18},{10... | collective-permute-start | bytes 786440 | tf_op jit(solution)/shard_map/ppermute | solution.py:25
  25.3 12.5 %collective-permute-start.9 = (bf16[1024,128]{1,0:T(8,128)(2,1)S(1)}, bf16[1024,128]{1,0:T(8,128)(2,1)S(1)}, u32[]{:S(2)}, u32[]{:S(2)}) collective-permute-start(bf16[1024,128]{1,0:T(8,128)(2,1)S(1)} %collective-permute-done.6.refs_4_), channel_id=1, source_target_pairs={{0,8},{8,0},{16,24},{24,16},{1,9},{9,1},{17,25},{25,17},{2,10},{10... | collective-permute-start | bytes 786440 | tf_op jit(solution)/shard_map/ppermute | solution.py:25
  25.9 14.2 %collective-permute-start.11 = (bf16[1024,128]{1,0:T(8,128)(2,1)S(1)}, bf16[1024,128]{1,0:T(8,128)(2,1)S(1)}, u32[]{:S(2)}, u32[]{:S(2)}) collective-permute-start(bf16[1024,128]{1,0:T(8,128)(2,1)S(1)} %collective-permute-done.5.refs_3_), channel_id=1, source_target_pairs={{0,8},{8,0},{16,24},{24,16},{1,9},{9,1},{17,25},{25,17},{2,10},{10... | collective-permute-start | bytes 786440 | tf_op jit(solution)/shard_map/ppermute | solution.py:25
  27.3 12.7 %collective-permute-start.12 = (bf16[1024,128]{1,0:T(8,128)(2,1)S(1)}, bf16[1024,128]{1,0:T(8,128)(2,1)S(1)}, u32[]{:S(2)}, u32[]{:S(2)}) collective-permute-start(bf16[1024,128]{1,0:T(8,128)(2,1)S(1)} %collective-permute-done.5.refs_3_), channel_id=1, source_target_pairs={{0,16},{8,24},{16,0},{24,8},{1,17},{9,25},{17,1},{25,9},{2,18},{10... | collective-permute-start | bytes 786440 | tf_op jit(solution)/shard_map/ppermute | solution.py:25
  30.4 12.4 %collective-permute-start.13 = (bf16[1024,128]{1,0:T(8,128)(2,1)S(1)}, bf16[1024,128]{1,0:T(8,128)(2,1)S(1)}, u32[]{:S(2)}, u32[]{:S(2)}) collective-permute-start(bf16[1024,128]{1,0:T(8,128)(2,1)S(1)} %collective-permute-done.8.refs_1_), channel_id=1, source_target_pairs={{0,8},{8,0},{16,24},{24,16},{1,9},{9,1},{17,25},{25,17},{2,10},{10... | collective-permute-start | bytes 786440 | tf_op jit(solution)/shard_map/ppermute | solution.py:25
  34.1 8.8 %collective-permute-start.14 = (bf16[1024,128]{1,0:T(8,128)(2,1)S(1)}, bf16[1024,128]{1,0:T(8,128)(2,1)S(1)}, u32[]{:S(2)}, u32[]{:S(2)}) collective-permute-start(bf16[1024,128]{1,0:T(8,128)(2,1)S(1)} %collective-permute-done.8.refs_1_), channel_id=1, source_target_pairs={{0,16},{8,24},{16,0},{24,8},{1,17},{9,25},{17,1},{25,9},{2,18},{10... | collective-permute-start | bytes 786440 | tf_op jit(solution)/shard_map/ppermute | solution.py:25
  37.8 6.8 %collective-permute-start.15 = (bf16[512,128]{1,0:T(8,128)(2,1)S(1)}, bf16[512,128]{1,0:T(8,128)(2,1)S(1)}, u32[]{:S(2)}, u32[]{:S(2)}) collective-permute-start(bf16[512,128]{1,0:T(8,128)(2,1)S(1)} %shard_map.79.near_a), channel_id=1, source_target_pairs={{0,2},{1,3},{2,4},{3,5},{4,6},{5,7},{6,0},{7,1},{8,10},{9,11},{10,... | collective-permute-start | bytes 393224 | tf_op jit(solution)/shard_map/ppermute | solution.py:34
  45.1 12.0 %collective-permute-start.16 = (bf16[1408,128]{1,0:T(8,128)(2,1)S(1)}, bf16[1408,128]{1,0:T(8,128)(2,1)S(1)}, u32[]{:S(2)}, u32[]{:S(2)}) collective-permute-start(bf16[1408,128]{1,0:T(8,128)(2,1)S(1)} %shard_map.81.near_b.near_a), channel_id=1, source_target_pairs={{0,2},{1,3},{2,4},{3,5},{4,6},{5,7},{6,0},{7,1},{8,10},{9,11},{10,... | collective-permute-start | bytes 1081352 | tf_op jit(solution)/shard_map/ppermute | solution.py:34
  45.1 6.7 %collective-permute-start.18 = (bf16[1024,128]{1,0:T(8,128)(2,1)S(1)}, bf16[1024,128]{1,0:T(8,128)(2,1)S(1)}, u32[]{:S(2)}, u32[]{:S(2)}) collective-permute-start(bf16[1024,128]{1,0:T(8,128)(2,1)S(1)} %collective-permute-done.12.refs_6_), channel_id=1, source_target_pairs={{0,8},{8,0},{16,24},{24,16},{1,9},{9,1},{17,25},{25,17},{2,10},{10... | collective-permute-start | bytes 786440 | tf_op jit(solution)/shard_map/ppermute | solution.py:25
  46.0 8.4 %collective-permute-start.19 = (bf16[1024,128]{1,0:T(8,128)(2,1)S(1)}, bf16[1024,128]{1,0:T(8,128)(2,1)S(1)}, u32[]{:S(2)}, u32[]{:S(2)}) collective-permute-start(bf16[1024,128]{1,0:T(8,128)(2,1)S(1)} %collective-permute-done.13.refs_1_), channel_id=1, source_target_pairs={{0,16},{8,24},{16,0},{24,8},{1,17},{9,25},{17,1},{25,9},{2,18},{10... | collective-permute-start | bytes 786440 | tf_op jit(solution)/shard_map/ppermute | solution.py:25
  47.3 7.2 %collective-permute-start.20 = (bf16[512,128]{1,0:T(8,128)(2,1)S(1)}, bf16[512,128]{1,0:T(8,128)(2,1)S(1)}, u32[]{:S(2)}, u32[]{:S(2)}) collective-permute-start(bf16[512,128]{1,0:T(8,128)(2,1)S(1)} %slice.13), channel_id=1, source_target_pairs={{0,16},{8,24},{16,0},{24,8},{1,17},{9,25},{17,1},{25,9},{2,18},{10... | collective-permute-start | bytes 393224 | tf_op jit(solution)/shard_map/ppermute | solution.py:25
  48.1 6.3 %collective-permute-start.21 = (bf16[512,128]{1,0:T(8,128)(2,1)S(1)}, bf16[512,128]{1,0:T(8,128)(2,1)S(1)}, u32[]{:S(2)}, u32[]{:S(2)}) collective-permute-start(bf16[512,128]{1,0:T(8,128)(2,1)S(1)} %slice.14), channel_id=1, source_target_pairs={{0,8},{8,0},{16,24},{24,16},{1,9},{9,1},{17,25},{25,17},{2,10},{10... | collective-permute-start | bytes 393224 | tf_op jit(solution)/shard_map/ppermute | solution.py:25
  55.4 6.8 %collective-permute-start.22 = (bf16[512,128]{1,0:T(8,128)(2,1)S(1)}, bf16[512,128]{1,0:T(8,128)(2,1)S(1)}, u32[]{:S(2)}, u32[]{:S(2)}) collective-permute-start(bf16[512,128]{1,0:T(8,128)(2,1)S(1)} %shard_map.85.near_b), channel_id=1, source_target_pairs={{0,2},{1,3},{2,4},{3,5},{4,6},{5,7},{6,0},{7,1},{8,10},{9,11},{10,... | collective-permute-start | bytes 393224 | tf_op jit(solution)/shard_map/ppermute | solution.py:34
  57.1 10.0 %collective-permute-start.17 = (bf16[896,128]{1,0:T(8,128)(2,1)S(1)}, bf16[896,128]{1,0:T(8,128)(2,1)S(1)}, u32[]{:S(2)}, u32[]{:S(2)}) collective-permute-start(bf16[896,128]{1,0:T(8,128)(2,1)S(1)} %slice.16), channel_id=1, source_target_pairs={{0,2},{1,3},{2,4},{3,5},{4,6},{5,7},{6,0},{7,1},{8,10},{9,11},{10,... | collective-permute-start | bytes 688136 | tf_op jit(solution)/shard_map/ppermute | solution.py:34
  62.3 6.5 %collective-permute-start.23 = (bf16[384,128]{1,0:T(8,128)(2,1)S(1)}, bf16[384,128]{1,0:T(8,128)(2,1)S(1)}, u32[]{:S(2)}, u32[]{:S(2)}) collective-permute-start(bf16[384,128]{1,0:T(8,128)(2,1)S(1)} %slice.17), channel_id=1, source_target_pairs={{0,2},{1,3},{2,4},{3,5},{4,6},{5,7},{6,0},{7,1},{8,10},{9,11},{10,... | collective-permute-start | bytes 294920 | tf_op jit(solution)/shard_map/ppermute | solution.py:34
  69.9 2.0 %collective-permute-start.25 = (bf16[256,512]{1,0:T(8,128)(2,1)S(1)}, bf16[256,512]{1,0:T(8,128)(2,1)S(1)}, u32[]{:S(2)}, u32[]{:S(2)}) collective-permute-start(bf16[256,512]{1,0:T(8,128)(2,1)S(1)} %get-tuple-element.69), channel_id=1, source_target_pairs={{0,1},{1,0},{2,3},{3,2},{4,5},{5,4},{6,7},{7,6},{8,9},{9,8},{10,11... | collective-permute-start | bytes 786440 | tf_op jit(solution)/shard_map/ppermute | solution.py:29
  (7 other events, 41.7 us)

commit v6 on v5

--- a/solution.py
+++ b/solution.py
@@ -297,9 +297,6 @@
         low, high = range(half), range(half, MAXDOC)
         stat[item, 0:1, :] = score_blocks(keys, rows, low, found, causal, table)
 
-        few = jnp.logical_and(found > half, found <= half + 2)
-        many = found > half + 2
-
         def score_rest(steps):
             stat[item, 0:1, :] = jnp.maximum(
                 stat[item, 0:1, :], score_blocks(keys, rows, steps, found, None, table)
@@ -310,12 +307,16 @@
             stat[item, 1:2, :] += more
             summed[item] += part
 
-        pl.when(few)(functools.partial(score_rest, high[:2]))
-        pl.when(many)(functools.partial(score_rest, high))
+        for more_blocks in range(1, MAXDOC - half + 1):
+            pl.when(found == half + more_blocks)(
+                functools.partial(score_rest, high[:more_blocks])
+            )
         stat[item, 1:2, :], summed[item] = weigh_blocks(values, low, stat[item, 0:1, :], table)
 
-        pl.when(few)(functools.partial(weigh_rest, high[:2]))
-        pl.when(many)(functools.partial(weigh_rest, high))
+        for more_blocks in range(1, MAXDOC - half + 1):
+            pl.when(found == half + more_blocks)(
+                functools.partial(weigh_rest, high[:more_blocks])
+            )
 
 
 def far_kernel(

time: 73.3 us -> 73.7 us (level)
  no operation moved by 1% of the time
where the time goes in v6:
time: 73.7 us; the launch traced here: 72.9 us
  starting transfers between devices  29.9 us (41%)
  Pallas kernels  21 us (28%)
  waiting for transfers between devices  17 us (23%)
  local copies, waits for them, and re-layouts  4.27 us (6%)
  between operations  0.83 us (1%)
    ppermute x13, starting transfers between devices, over_dp(): lax.ppermute(array, 'dp', [(i, i ^ mask) for i in range(lax.axis_size('dp...  14.4 us
    pallas_call x6, Pallas kernels, project(): pl.pallas_call(functools.partial(project_kernel, steps, count, passed, to...  9.31 us
    ppermute x13, waiting for transfers between devices, over_dp(): lax.ppermute(array, 'dp', [(i, i ^ mask) for i in range(lax.axis_size('dp...  8.68 us
    pallas_call x2, Pallas kernels, attend_near(): pl.pallas_call(functools.partial(near_kernel, second, (start_a, start_b))...  6.72 us
    ppermute x2, starting transfers between devices, neighbours(): lax.ppermute(array, 'ctx', [(i, i ^ 2) for i in range(lax.axis_size('ctx'...  5.64 us
    ppermute x5, starting transfers between devices, around(): lax.ppermute(array, 'ctx', [(i, (i + 2 * pairs) % size) for i in range(si...  4.6 us
    ppermute x1, starting transfers between devices, mirrored(): return lax.ppermute(array, 'ctx', pairs)  3.6 us
    unnamed x9, local copies, waits for them, and re-layouts  3.3 us
  transfers between devices with their start and end apart: 27, of which 13 were waited for; matrix products, arithmetic and copies ran while one was open for 2% of the time, Pallas kernels for 25%

profile of v6, /device:TPU:0, one launch (start us, length us, event | category | flops | bytes accessed | tf_op | source)
XLA Modules:
  0.0 72.9 jit_solution(16807026298962604157)
XLA Ops:
  1.2 1.4 %collective-permute-done = bf16[512,256]{1,0:T(8,128)(2,1)S(1)} collective-permute-done((bf16[512,256]{1,0:T(8,128)(2,1)}, bf16[512,256]{1,0:T(8,128)(2,1)S(1)}, u32[]{:S(2)}, u32[]{:S(2)}) %collective-permute-start) | collective-permute-done | bytes 262176 | tf_op jit(solution)/shard_map/ppermute | solution.py:29
  4.0 2.9 %collective-permute-start.1 = (bf16[1024,128]{1,0:T(8,128)(2,1)S(1)}, bf16[1024,128]{1,0:T(8,128)(2,1)}, u32[]{:S(2)}, u32[]{:S(2)}) collective-permute-start(bf16[1024,128]{1,0:T(8,128)(2,1)S(1)} %pad_maximum_fusion.refs_2_), channel_id=1, source_target_pairs={{0,8},{8,0},{16,24},{24,16},{1,9},{9,1},{17,25},{25,17},{2,10},{10... | collective-permute-start | bytes 786440 | tf_op jit(solution)/shard_map/ppermute | solution.py:25
  6.9 1.5 %collective-permute-start.2 = (bf16[1024,128]{1,0:T(8,128)(2,1)S(1)}, bf16[1024,128]{1,0:T(8,128)(2,1)}, u32[]{:S(2)}, u32[]{:S(2)}) collective-permute-start(bf16[1024,128]{1,0:T(8,128)(2,1)S(1)} %pad_maximum_fusion.refs_2_), channel_id=1, source_target_pairs={{0,16},{8,24},{16,0},{24,8},{1,17},{9,25},{17,1},{25,9},{2,18},{10... | collective-permute-start | bytes 786440 | tf_op jit(solution)/shard_map/ppermute | solution.py:25
  9.2 3.6 %collective-permute-start.6 = (bf16[1024,128]{1,0:T(8,128)(2,1)S(1)}, bf16[1024,128]{1,0:T(8,128)(2,1)S(1)}, u32[]{:S(2)}, u32[]{:S(2)}) collective-permute-start(bf16[1024,128]{1,0:T(8,128)(2,1)S(1)} %pad_maximum_fusion.refs_2_), channel_id=1, source_target_pairs={{0,6},{1,7},{2,4},{3,5},{4,2},{5,3},{6,0},{7,1},{8,14},{9,15},{10,... | collective-permute-start | bytes 786440 | tf_op jit(solution)/shard_map/ppermute | solution.py:44
  12.8 1.2 %copy-done.1 = bf16[1,256,2048]{2,1,0:T(8,128)(2,1)S(1)} copy-done((bf16[1,256,2048]{2,1,0:T(8,128)(2,1)S(1)}, bf16[1,256,2048]{2,1,0:T(8,128)(2,1)}, u32[]{:S(2)}) %copy-start.1) | copy-done | bytes 1048600
  15.4 1.6 %shard_map.77 = (bf16[2,4,512,128]{3,2,1,0:T(8,128)(2,1)S(1)}, s32[4,9]{1,0:T(4,128)S(1)}) custom-call(s32[1,4]{1,0:T(1,128)S(1)} %copy-done.2, s32[1,16,7]{2,1,0:T(8,128)S(1)} %copy.8.mask_ref, s32[1,16]{1,0:T(1,128)S(1)} %copy-done.3, bf16[256,2048]{1,0:T(8,128)(2,1)S(1)} %bitcast.7, bf16[256,2048]{1,0:T(8,128)(2,1)S(1)} %collective-permute-done.4.q_other_ref), custom_call_target="tpu_custom_call" | custom-call | bytes 1048576 | tf_op jit(solution)/shard_map/pallas_call | solution.py:236
  19.2 5.0 %collective-permute-start.8 = (bf16[1024,128]{1,0:T(8,128)(2,1)S(1)}, bf16[1024,128]{1,0:T(8,128)(2,1)S(1)}, u32[]{:S(2)}, u32[]{:S(2)}) collective-permute-start(bf16[1024,128]{1,0:T(8,128)(2,1)S(1)} %collective-permute-done.6.refs_4_), channel_id=1, source_target_pairs={{0,2},{1,3},{2,0},{3,1},{4,6},{5,7},{6,4},{7,5},{8,10},{9,11},{10,... | collective-permute-start | bytes 786440 | tf_op jit(solution)/shard_map/ppermute | solution.py:38
  25.9 1.5 %collective-permute-start.11 = (bf16[1024,128]{1,0:T(8,128)(2,1)S(1)}, bf16[1024,128]{1,0:T(8,128)(2,1)S(1)}, u32[]{:S(2)}, u32[]{:S(2)}) collective-permute-start(bf16[1024,128]{1,0:T(8,128)(2,1)S(1)} %collective-permute-done.5.refs_3_), channel_id=1, source_target_pairs={{0,8},{8,0},{16,24},{24,16},{1,9},{9,1},{17,25},{25,17},{2,10},{10... | collective-permute-start | bytes 786440 | tf_op jit(solution)/shard_map/ppermute | solution.py:25
  27.3 1.5 %collective-permute-start.12 = (bf16[1024,128]{1,0:T(8,128)(2,1)S(1)}, bf16[1024,128]{1,0:T(8,128)(2,1)S(1)}, u32[]{:S(2)}, u32[]{:S(2)}) collective-permute-start(bf16[1024,128]{1,0:T(8,128)(2,1)S(1)} %collective-permute-done.5.refs_3_), channel_id=1, source_target_pairs={{0,16},{8,24},{16,0},{24,8},{1,17},{9,25},{17,1},{25,9},{2,18},{10... | collective-permute-start | bytes 786440 | tf_op jit(solution)/shard_map/ppermute | solution.py:25
  28.9 1.6 %collective-permute-done.8.refs_1_ = bf16[1024,128]{1,0:T(8,128)(2,1)S(1)} collective-permute-done((bf16[1024,128]{1,0:T(8,128)(2,1)S(1)}, bf16[1024,128]{1,0:T(8,128)(2,1)S(1)}, u32[]{:S(2)}, u32[]{:S(2)}) %collective-permute-start.8) | collective-permute-done | bytes 262176 | tf_op jit(solution)/shard_map/ppermute | solution.py:38
  31.0 3.1 %collective-permute-done.10.refs_7_ = bf16[1024,128]{1,0:T(8,128)(2,1)S(1)} collective-permute-done((bf16[1024,128]{1,0:T(8,128)(2,1)S(1)}, bf16[1024,128]{1,0:T(8,128)(2,1)S(1)}, u32[]{:S(2)}, u32[]{:S(2)}) %collective-permute-start.10) | collective-permute-done | bytes 262176 | tf_op jit(solution)/shard_map/ppermute | solution.py:25
  34.6 2.8 %shard_map.78 = (f32[512,128]{1,0:T(8,128)S(1)}, bf16[512,3072]{1,0:T(8,128)(2,1)S(1)}) custom-call(bf16[256,4096]{1,0:T(8,128)(2,1)S(1)} %bitcast.3, bf16[256,4096]{1,0:T(8,128)(2,1)} %collective-permute-done.3.refs_1_, bf16[1024,128]{1,0:T(8,128)(2,1)S(1)} %pad_maximum_fusion.refs_2_, bf16[1024,128]{1,0:T(8,128)(2,1)S(1)} %collective-permute-done.5.refs_3_, ...), custom_call_target="tpu_custom_call" | custom-call | flops 402653184 | bytes 3145728 | tf_op jit(solution)/shard_map/pallas_call | solution.py:133
  38.2 1.8 %collective-permute-done.11.refs_3_ = bf16[1024,128]{1,0:T(8,128)(2,1)S(1)} collective-permute-done((bf16[1024,128]{1,0:T(8,128)(2,1)S(1)}, bf16[1024,128]{1,0:T(8,128)(2,1)S(1)}, u32[]{:S(2)}, u32[]{:S(2)}) %collective-permute-start.11) | collective-permute-done | bytes 262176 | tf_op jit(solution)/shard_map/ppermute | solution.py:25
  40.1 2.7 %shard_map.80.refs_3_ = f32[512,256]{1,0:T(8,128)S(1)} custom-call(bf16[256,4096]{1,0:T(8,128)(2,1)S(1)} %bitcast.4, bf16[256,4096]{1,0:T(8,128)(2,1)} %collective-permute-done.3.refs_1_, bf16[1024,128]{1,0:T(8,128)(2,1)} %collective-permute-done.1.refs_2_, bf16[1024,128]{1,0:T(8,128)(2,1)S(1)} %collective-permute-done.11.refs_3_, ...), custom_call_target="tpu_custom_call" | custom-call | flops 805306368 | bytes 3145728 | tf_op jit(solution)/shard_map/pallas_call | solution.py:133
  42.9 1.8 %collective-permute-done.15.refs_4_.back_a = bf16[512,128]{1,0:T(8,128)(2,1)S(1)} collective-permute-done((bf16[512,128]{1,0:T(8,128)(2,1)S(1)}, bf16[512,128]{1,0:T(8,128)(2,1)S(1)}, u32[]{:S(2)}, u32[]{:S(2)}) %collective-permute-start.15) | collective-permute-done | bytes 131104 | tf_op jit(solution)/shard_map/ppermute | solution.py:34
  46.0 1.2 %collective-permute-start.19 = (bf16[1024,128]{1,0:T(8,128)(2,1)S(1)}, bf16[1024,128]{1,0:T(8,128)(2,1)S(1)}, u32[]{:S(2)}, u32[]{:S(2)}) collective-permute-start(bf16[1024,128]{1,0:T(8,128)(2,1)S(1)} %collective-permute-done.13.refs_1_), channel_id=1, source_target_pairs={{0,16},{8,24},{16,0},{24,8},{1,17},{9,25},{17,1},{25,9},{2,18},{10... | collective-permute-start | bytes 786440 | tf_op jit(solution)/shard_map/ppermute | solution.py:25
  48.1 1.3 %collective-permute-start.21 = (bf16[512,128]{1,0:T(8,128)(2,1)S(1)}, bf16[512,128]{1,0:T(8,128)(2,1)S(1)}, u32[]{:S(2)}, u32[]{:S(2)}) collective-permute-start(bf16[512,128]{1,0:T(8,128)(2,1)S(1)} %slice.14), channel_id=1, source_target_pairs={{0,8},{8,0},{16,24},{24,16},{1,9},{9,1},{17,25},{25,17},{2,10},{10... | collective-permute-start | bytes 393224 | tf_op jit(solution)/shard_map/ppermute | solution.py:25
  49.4 2.0 %shard_map.84.refs_5_ = f32[512,128]{1,0:T(8,128)S(1)} custom-call(bf16[256,4096]{1,0:T(8,128)(2,1)S(1)} %bitcast.5, bf16[256,4096]{1,0:T(8,128)(2,1)} %collective-permute-done.3.refs_1_, bf16[1024,128]{1,0:T(8,128)(2,1)S(1)} %collective-permute-done.7.refs_2_), custom_call_target="tpu_custom_call" | custom-call | tf_op jit(solution)/shard_map/pallas_call | solution.py:133
  51.9 2.6 %collective-permute-done.20.refs_3_ = bf16[512,128]{1,0:T(8,128)(2,1)S(1)} collective-permute-done((bf16[512,128]{1,0:T(8,128)(2,1)S(1)}, bf16[512,128]{1,0:T(8,128)(2,1)S(1)}, u32[]{:S(2)}, u32[]{:S(2)}) %collective-permute-start.20) | collective-permute-done | bytes 131104 | tf_op jit(solution)/shard_map/ppermute | solution.py:25
  55.4 1.6 %collective-permute-start.22 = (bf16[512,128]{1,0:T(8,128)(2,1)S(1)}, bf16[512,128]{1,0:T(8,128)(2,1)S(1)}, u32[]{:S(2)}, u32[]{:S(2)}) collective-permute-start(bf16[512,128]{1,0:T(8,128)(2,1)S(1)} %shard_map.85.near_b), channel_id=1, source_target_pairs={{0,2},{1,3},{2,4},{3,5},{4,6},{5,7},{6,0},{7,1},{8,10},{9,11},{10,... | collective-permute-start | bytes 393224 | tf_op jit(solution)/shard_map/ppermute | solution.py:34
  57.1 1.6 %collective-permute-start.17 = (bf16[896,128]{1,0:T(8,128)(2,1)S(1)}, bf16[896,128]{1,0:T(8,128)(2,1)S(1)}, u32[]{:S(2)}, u32[]{:S(2)}) collective-permute-start(bf16[896,128]{1,0:T(8,128)(2,1)S(1)} %slice.16), channel_id=1, source_target_pairs={{0,2},{1,3},{2,4},{3,5},{4,6},{5,7},{6,0},{7,1},{8,10},{9,11},{10,... | collective-permute-start | bytes 688136 | tf_op jit(solution)/shard_map/ppermute | solution.py:34
  58.7 3.4 %shard_map.82 = (f32[4,128,512]{2,1,0:T(8,128)S(1)}, f32[4,8,512]{2,1,0:T(8,128)S(1)}) custom-call(s32[4,9]{1,0:T(4,128)S(1)} %get-tuple-element.42.facts, bf16[2,4,512,128]{3,2,1,0:T(8,128)(2,1)S(1)} %get-tuple-element.43.queries_ref, bf16[512,128]{1,0:T(8,128)(2,1)S(1)} %shard_map.79.near_a, bf16[1408,128]{1,0:T(8,128)(2,1)S(1)} %shard_map.81.near_b.near_a, ...), custom_call_target="tpu_custom_call" | custom-call | flops 1073741824 | bytes 4194304 | tf_op jit(solution)/shard_map/pallas_call | solution.py:420
  63.1 3.3 %shard_map.86 = (f32[4,128,512]{2,1,0:T(8,128)S(1)}, f32[4,8,512]{2,1,0:T(8,128)S(1)}) custom-call(s32[4,9]{1,0:T(4,128)S(1)} %get-tuple-element.42.facts, bf16[2,4,512,128]{3,2,1,0:T(8,128)(2,1)S(1)} %get-tuple-element.43.queries_ref, bf16[1408,128]{1,0:T(8,128)(2,1)S(1)} %shard_map.81.near_b.near_a, bf16[512,128]{1,0:T(8,128)(2,1)S(1)} %shard_map.85.near_b, ...), custom_call_target="tpu_custom_call" | custom-call | flops 1073741824 | bytes 4194304 | tf_op jit(solution)/shard_map/pallas_call | solution.py:420
  70.5 1.3 %collective-permute-done.26.st_got = f32[4,4,128]{2,1,0:T(4,128)S(1)} collective-permute-done((f32[4,4,128]{2,1,0:T(4,128)S(1)}, f32[4,4,128]{2,1,0:T(4,128)S(1)}, u32[]{:S(2)}, u32[]{:S(2)}) %collective-permute-start.26) | collective-permute-done | bytes 8224 | tf_op jit(solution)/shard_map/ppermute | solution.py:29
  (58 shorter events, 19.7 us)
Async XLA Ops:
  2.5 14.5 %collective-permute-start.3 = (bf16[256,4096]{1,0:T(8,128)(2,1)}, bf16[256,4096]{1,0:T(8,128)(2,1)}, u32[]{:S(2)}, u32[]{:S(2)}) collective-permute-start(bf16[256,4096]{1,0:T(8,128)(2,1)} %bitcast.2), channel_id=1, source_target_pairs={{0,1},{1,0},{2,3},{3,2},{4,5},{5,4},{6,7},{7,6},{8,9},{9,8},{10,11... | collective-permute-start | bytes 6291464 | tf_op jit(solution)/shard_map/ppermute | solution.py:29
  2.9 9.9 %collective-permute-start.4 = (bf16[256,2048]{1,0:T(8,128)(2,1)}, bf16[256,2048]{1,0:T(8,128)(2,1)S(1)}, u32[]{:S(2)}, u32[]{:S(2)}) collective-permute-start(bf16[256,2048]{1,0:T(8,128)(2,1)} %bitcast.6), channel_id=1, source_target_pairs={{0,1},{1,0},{2,3},{3,2},{4,5},{5,4},{6,7},{7,6},{8,9},{9,8},{10,11... | collective-permute-start | bytes 3145736 | tf_op jit(solution)/shard_map/ppermute | solution.py:29
  4.0 13.0 %collective-permute-start.1 = (bf16[1024,128]{1,0:T(8,128)(2,1)S(1)}, bf16[1024,128]{1,0:T(8,128)(2,1)}, u32[]{:S(2)}, u32[]{:S(2)}) collective-permute-start(bf16[1024,128]{1,0:T(8,128)(2,1)S(1)} %pad_maximum_fusion.refs_2_), channel_id=1, source_target_pairs={{0,8},{8,0},{16,24},{24,16},{1,9},{9,1},{17,25},{25,17},{2,10},{10... | collective-permute-start | bytes 786440 | tf_op jit(solution)/shard_map/ppermute | solution.py:25
  6.9 10.1 %collective-permute-start.2 = (bf16[1024,128]{1,0:T(8,128)(2,1)S(1)}, bf16[1024,128]{1,0:T(8,128)(2,1)}, u32[]{:S(2)}, u32[]{:S(2)}) collective-permute-start(bf16[1024,128]{1,0:T(8,128)(2,1)S(1)} %pad_maximum_fusion.refs_2_), channel_id=1, source_target_pairs={{0,16},{8,24},{16,0},{24,8},{1,17},{9,25},{17,1},{25,9},{2,18},{10... | collective-permute-start | bytes 786440 | tf_op jit(solution)/shard_map/ppermute | solution.py:25
  9.2 10.0 %collective-permute-start.6 = (bf16[1024,128]{1,0:T(8,128)(2,1)S(1)}, bf16[1024,128]{1,0:T(8,128)(2,1)S(1)}, u32[]{:S(2)}, u32[]{:S(2)}) collective-permute-start(bf16[1024,128]{1,0:T(8,128)(2,1)S(1)} %pad_maximum_fusion.refs_2_), channel_id=1, source_target_pairs={{0,6},{1,7},{2,4},{3,5},{4,2},{5,3},{6,0},{7,1},{8,14},{9,15},{10,... | collective-permute-start | bytes 786440 | tf_op jit(solution)/shard_map/ppermute | solution.py:44
  17.0 7.8 %collective-permute-start.7 = (bf16[1024,128]{1,0:T(8,128)(2,1)}, bf16[1024,128]{1,0:T(8,128)(2,1)S(1)}, u32[]{:S(2)}, u32[]{:S(2)}) collective-permute-start(bf16[1024,128]{1,0:T(8,128)(2,1)} %collective-permute-done.1.refs_2_), channel_id=1, source_target_pairs={{0,16},{8,24},{16,0},{24,8},{1,17},{9,25},{17,1},{25,9},{2,18},{10... | collective-permute-start | bytes 786440 | tf_op jit(solution)/shard_map/ppermute | solution.py:25
  17.6 8.3 %collective-permute-start.5 = (bf16[1024,128]{1,0:T(8,128)(2,1)S(1)}, bf16[1024,128]{1,0:T(8,128)(2,1)S(1)}, u32[]{:S(2)}, u32[]{:S(2)}) collective-permute-start(bf16[1024,128]{1,0:T(8,128)(2,1)S(1)} %pad_maximum_fusion.refs_2_), channel_id=1, source_target_pairs={{0,2},{1,3},{2,0},{3,1},{4,6},{5,7},{6,4},{7,5},{8,10},{9,11},{10,... | collective-permute-start | bytes 786440 | tf_op jit(solution)/shard_map/ppermute | solution.py:38
  19.2 11.3 %collective-permute-start.8 = (bf16[1024,128]{1,0:T(8,128)(2,1)S(1)}, bf16[1024,128]{1,0:T(8,128)(2,1)S(1)}, u32[]{:S(2)}, u32[]{:S(2)}) collective-permute-start(bf16[1024,128]{1,0:T(8,128)(2,1)S(1)} %collective-permute-done.6.refs_4_), channel_id=1, source_target_pairs={{0,2},{1,3},{2,0},{3,1},{4,6},{5,7},{6,4},{7,5},{8,10},{9,11},{10,... | collective-permute-start | bytes 786440 | tf_op jit(solution)/shard_map/ppermute | solution.py:38
  24.8 9.2 %collective-permute-start.10 = (bf16[1024,128]{1,0:T(8,128)(2,1)S(1)}, bf16[1024,128]{1,0:T(8,128)(2,1)S(1)}, u32[]{:S(2)}, u32[]{:S(2)}) collective-permute-start(bf16[1024,128]{1,0:T(8,128)(2,1)S(1)} %collective-permute-done.6.refs_4_), channel_id=1, source_target_pairs={{0,16},{8,24},{16,0},{24,8},{1,17},{9,25},{17,1},{25,9},{2,18},{10... | collective-permute-start | bytes 786440 | tf_op jit(solution)/shard_map/ppermute | solution.py:25
  25.3 12.5 %collective-permute-start.9 = (bf16[1024,128]{1,0:T(8,128)(2,1)S(1)}, bf16[1024,128]{1,0:T(8,128)(2,1)S(1)}, u32[]{:S(2)}, u32[]{:S(2)}) collective-permute-start(bf16[1024,128]{1,0:T(8,128)(2,1)S(1)} %collective-permute-done.6.refs_4_), channel_id=1, source_target_pairs={{0,8},{8,0},{16,24},{24,16},{1,9},{9,1},{17,25},{25,17},{2,10},{10... | collective-permute-start | bytes 786440 | tf_op jit(solution)/shard_map/ppermute | solution.py:25
  25.9 14.2 %collective-permute-start.11 = (bf16[1024,128]{1,0:T(8,128)(2,1)S(1)}, bf16[1024,128]{1,0:T(8,128)(2,1)S(1)}, u32[]{:S(2)}, u32[]{:S(2)}) collective-permute-start(bf16[1024,128]{1,0:T(8,128)(2,1)S(1)} %collective-permute-done.5.refs_3_), channel_id=1, source_target_pairs={{0,8},{8,0},{16,24},{24,16},{1,9},{9,1},{17,25},{25,17},{2,10},{10... | collective-permute-start | bytes 786440 | tf_op jit(solution)/shard_map/ppermute | solution.py:25
  27.3 12.7 %collective-permute-start.12 = (bf16[1024,128]{1,0:T(8,128)(2,1)S(1)}, bf16[1024,128]{1,0:T(8,128)(2,1)S(1)}, u32[]{:S(2)}, u32[]{:S(2)}) collective-permute-start(bf16[1024,128]{1,0:T(8,128)(2,1)S(1)} %collective-permute-done.5.refs_3_), channel_id=1, source_target_pairs={{0,16},{8,24},{16,0},{24,8},{1,17},{9,25},{17,1},{25,9},{2,18},{10... | collective-permute-start | bytes 786440 | tf_op jit(solution)/shard_map/ppermute | solution.py:25
  30.4 12.4 %collective-permute-start.13 = (bf16[1024,128]{1,0:T(8,128)(2,1)S(1)}, bf16[1024,128]{1,0:T(8,128)(2,1)S(1)}, u32[]{:S(2)}, u32[]{:S(2)}) collective-permute-start(bf16[1024,128]{1,0:T(8,128)(2,1)S(1)} %collective-permute-done.8.refs_1_), channel_id=1, source_target_pairs={{0,8},{8,0},{16,24},{24,16},{1,9},{9,1},{17,25},{25,17},{2,10},{10... | collective-permute-start | bytes 786440 | tf_op jit(solution)/shard_map/ppermute | solution.py:25
  34.1 8.8 %collective-permute-start.14 = (bf16[1024,128]{1,0:T(8,128)(2,1)S(1)}, bf16[1024,128]{1,0:T(8,128)(2,1)S(1)}, u32[]{:S(2)}, u32[]{:S(2)}) collective-permute-start(bf16[1024,128]{1,0:T(8,128)(2,1)S(1)} %collective-permute-done.8.refs_1_), channel_id=1, source_target_pairs={{0,16},{8,24},{16,0},{24,8},{1,17},{9,25},{17,1},{25,9},{2,18},{10... | collective-permute-start | bytes 786440 | tf_op jit(solution)/shard_map/ppermute | solution.py:25
  37.8 6.8 %collective-permute-start.15 = (bf16[512,128]{1,0:T(8,128)(2,1)S(1)}, bf16[512,128]{1,0:T(8,128)(2,1)S(1)}, u32[]{:S(2)}, u32[]{:S(2)}) collective-permute-start(bf16[512,128]{1,0:T(8,128)(2,1)S(1)} %shard_map.79.near_a), channel_id=1, source_target_pairs={{0,2},{1,3},{2,4},{3,5},{4,6},{5,7},{6,0},{7,1},{8,10},{9,11},{10,... | collective-permute-start | bytes 393224 | tf_op jit(solution)/shard_map/ppermute | solution.py:34
  45.1 12.0 %collective-permute-start.16 = (bf16[1408,128]{1,0:T(8,128)(2,1)S(1)}, bf16[1408,128]{1,0:T(8,128)(2,1)S(1)}, u32[]{:S(2)}, u32[]{:S(2)}) collective-permute-start(bf16[1408,128]{1,0:T(8,128)(2,1)S(1)} %shard_map.81.near_b.near_a), channel_id=1, source_target_pairs={{0,2},{1,3},{2,4},{3,5},{4,6},{5,7},{6,0},{7,1},{8,10},{9,11},{10,... | collective-permute-start | bytes 1081352 | tf_op jit(solution)/shard_map/ppermute | solution.py:34
  45.1 6.7 %collective-permute-start.18 = (bf16[1024,128]{1,0:T(8,128)(2,1)S(1)}, bf16[1024,128]{1,0:T(8,128)(2,1)S(1)}, u32[]{:S(2)}, u32[]{:S(2)}) collective-permute-start(bf16[1024,128]{1,0:T(8,128)(2,1)S(1)} %collective-permute-done.12.refs_6_), channel_id=1, source_target_pairs={{0,8},{8,0},{16,24},{24,16},{1,9},{9,1},{17,25},{25,17},{2,10},{10... | collective-permute-start | bytes 786440 | tf_op jit(solution)/shard_map/ppermute | solution.py:25
  46.0 8.4 %collective-permute-start.19 = (bf16[1024,128]{1,0:T(8,128)(2,1)S(1)}, bf16[1024,128]{1,0:T(8,128)(2,1)S(1)}, u32[]{:S(2)}, u32[]{:S(2)}) collective-permute-start(bf16[1024,128]{1,0:T(8,128)(2,1)S(1)} %collective-permute-done.13.refs_1_), channel_id=1, source_target_pairs={{0,16},{8,24},{16,0},{24,8},{1,17},{9,25},{17,1},{25,9},{2,18},{10... | collective-permute-start | bytes 786440 | tf_op jit(solution)/shard_map/ppermute | solution.py:25
  47.3 7.2 %collective-permute-start.20 = (bf16[512,128]{1,0:T(8,128)(2,1)S(1)}, bf16[512,128]{1,0:T(8,128)(2,1)S(1)}, u32[]{:S(2)}, u32[]{:S(2)}) collective-permute-start(bf16[512,128]{1,0:T(8,128)(2,1)S(1)} %slice.13), channel_id=1, source_target_pairs={{0,16},{8,24},{16,0},{24,8},{1,17},{9,25},{17,1},{25,9},{2,18},{10... | collective-permute-start | bytes 393224 | tf_op jit(solution)/shard_map/ppermute | solution.py:25
  48.1 6.3 %collective-permute-start.21 = (bf16[512,128]{1,0:T(8,128)(2,1)S(1)}, bf16[512,128]{1,0:T(8,128)(2,1)S(1)}, u32[]{:S(2)}, u32[]{:S(2)}) collective-permute-start(bf16[512,128]{1,0:T(8,128)(2,1)S(1)} %slice.14), channel_id=1, source_target_pairs={{0,8},{8,0},{16,24},{24,16},{1,9},{9,1},{17,25},{25,17},{2,10},{10... | collective-permute-start | bytes 393224 | tf_op jit(solution)/shard_map/ppermute | solution.py:25
  55.4 6.8 %collective-permute-start.22 = (bf16[512,128]{1,0:T(8,128)(2,1)S(1)}, bf16[512,128]{1,0:T(8,128)(2,1)S(1)}, u32[]{:S(2)}, u32[]{:S(2)}) collective-permute-start(bf16[512,128]{1,0:T(8,128)(2,1)S(1)} %shard_map.85.near_b), channel_id=1, source_target_pairs={{0,2},{1,3},{2,4},{3,5},{4,6},{5,7},{6,0},{7,1},{8,10},{9,11},{10,... | collective-permute-start | bytes 393224 | tf_op jit(solution)/shard_map/ppermute | solution.py:34
  57.1 9.3 %collective-permute-start.17 = (bf16[896,128]{1,0:T(8,128)(2,1)S(1)}, bf16[896,128]{1,0:T(8,128)(2,1)S(1)}, u32[]{:S(2)}, u32[]{:S(2)}) collective-permute-start(bf16[896,128]{1,0:T(8,128)(2,1)S(1)} %slice.16), channel_id=1, source_target_pairs={{0,2},{1,3},{2,4},{3,5},{4,6},{5,7},{6,0},{7,1},{8,10},{9,11},{10,... | collective-permute-start | bytes 688136 | tf_op jit(solution)/shard_map/ppermute | solution.py:34
  62.3 6.5 %collective-permute-start.23 = (bf16[384,128]{1,0:T(8,128)(2,1)S(1)}, bf16[384,128]{1,0:T(8,128)(2,1)S(1)}, u32[]{:S(2)}, u32[]{:S(2)}) collective-permute-start(bf16[384,128]{1,0:T(8,128)(2,1)S(1)} %slice.17), channel_id=1, source_target_pairs={{0,2},{1,3},{2,4},{3,5},{4,6},{5,7},{6,0},{7,1},{8,10},{9,11},{10,... | collective-permute-start | bytes 294920 | tf_op jit(solution)/shard_map/ppermute | solution.py:34
  69.9 2.0 %collective-permute-start.25 = (bf16[256,512]{1,0:T(8,128)(2,1)S(1)}, bf16[256,512]{1,0:T(8,128)(2,1)S(1)}, u32[]{:S(2)}, u32[]{:S(2)}) collective-permute-start(bf16[256,512]{1,0:T(8,128)(2,1)S(1)} %get-tuple-element.69), channel_id=1, source_target_pairs={{0,1},{1,0},{2,3},{3,2},{4,5},{5,4},{6,7},{7,6},{8,9},{9,8},{10,11... | collective-permute-start | bytes 786440 | tf_op jit(solution)/shard_map/ppermute | solution.py:29
  (7 other events, 41.7 us)

commit v7 on v5

--- a/solution.py
+++ b/solution.py
@@ -561,7 +561,7 @@
         xy_far = around(xy_back[spare : 2 * tall], 1)
         d_near = multiply_kept((1, 2, 3), [[d1, d2, d3]], d_sum)
         d_back = around(d_near, 1)
-        d_far = around(d_back[spare:], 1)
+        d_far = around(d_near[spare:], 2)
     else:
         stacked, facts = stack(doc_blocks, block_mask, plan, own_queries, other_queries)
         even = jnp.where(core == 0, mine, others)
@@ -593,7 +593,7 @@
         d_near = multiply([d_set])
         xy_far = around(xy_back[spare : 2 * tall], 1)
         d_back = around(d_near, 1)
-        d_far = around(d_back[spare:], 1)
+        d_far = around(d_near[spare:], 2)
 
     own_set = (own_near, own_back, xy_back), (0, 0, 2 * tall)
     y_set = (xy_near, xy_back, xy_far), (tall, tall, tall)

time: 73.3 us -> 72.8 us (level)
  transfers between devices with their start and end apart: 27 -> 27, of which waited for: 13 -> 12; matrix products, arithmetic and copies ran while one was open for 2% -> 2% of each run, Pallas kernels for 25% -> 25%
where the time goes in v7:
time: 72.8 us; the launch traced here: 72.5 us
  starting transfers between devices  30.3 us (42%)
  Pallas kernels  20.8 us (29%)
  waiting for transfers between devices  16.2 us (22%)
  local copies, waits for them, and re-layouts  4.27 us (6%)
  between operations  0.83 us (1%)
    ppermute x13, starting transfers between devices, over_dp(): lax.ppermute(array, 'dp', [(i, i ^ mask) for i in range(lax.axis_size('dp...  14.4 us
    pallas_call x6, Pallas kernels, project(): pl.pallas_call(functools.partial(project_kernel, steps, count, passed, to...  9.31 us
    ppermute x13, waiting for transfers between devices, over_dp(): lax.ppermute(array, 'dp', [(i, i ^ mask) for i in range(lax.axis_size('dp...  8.68 us
    pallas_call x2, Pallas kernels, attend_near(): pl.pallas_call(functools.partial(near_kernel, second, (start_a, start_b))...  6.58 us
    ppermute x2, starting transfers between devices, neighbours(): lax.ppermute(array, 'ctx', [(i, i ^ 2) for i in range(lax.axis_size('ctx'...  5.64 us
    ppermute x5, starting transfers between devices, around(): lax.ppermute(array, 'ctx', [(i, (i + 2 * pairs) % size) for i in range(si...  5.04 us
    ppermute x1, starting transfers between devices, mirrored(): return lax.ppermute(array, 'ctx', pairs)  3.6 us
    unnamed x9, local copies, waits for them, and re-layouts  3.3 us
  transfers between devices with their start and end apart: 27, of which 12 were waited for; matrix products, arithmetic and copies ran while one was open for 2% of the time, Pallas kernels for 25%

profile of v7, /device:TPU:0, one launch (start us, length us, event | category | flops | bytes accessed | tf_op | source)
XLA Modules:
  0.0 72.5 jit_solution(12924687100360434821)
XLA Ops:
  1.2 1.4 %collective-permute-done = bf16[512,256]{1,0:T(8,128)(2,1)S(1)} collective-permute-done((bf16[512,256]{1,0:T(8,128)(2,1)}, bf16[512,256]{1,0:T(8,128)(2,1)S(1)}, u32[]{:S(2)}, u32[]{:S(2)}) %collective-permute-start) | collective-permute-done | bytes 262176 | tf_op jit(solution)/shard_map/ppermute | solution.py:29
  4.0 2.9 %collective-permute-start.1 = (bf16[1024,128]{1,0:T(8,128)(2,1)S(1)}, bf16[1024,128]{1,0:T(8,128)(2,1)}, u32[]{:S(2)}, u32[]{:S(2)}) collective-permute-start(bf16[1024,128]{1,0:T(8,128)(2,1)S(1)} %pad_maximum_fusion.refs_2_), channel_id=1, source_target_pairs={{0,8},{8,0},{16,24},{24,16},{1,9},{9,1},{17,25},{25,17},{2,10},{10... | collective-permute-start | bytes 786440 | tf_op jit(solution)/shard_map/ppermute | solution.py:25
  6.9 1.5 %collective-permute-start.2 = (bf16[1024,128]{1,0:T(8,128)(2,1)S(1)}, bf16[1024,128]{1,0:T(8,128)(2,1)}, u32[]{:S(2)}, u32[]{:S(2)}) collective-permute-start(bf16[1024,128]{1,0:T(8,128)(2,1)S(1)} %pad_maximum_fusion.refs_2_), channel_id=1, source_target_pairs={{0,16},{8,24},{16,0},{24,8},{1,17},{9,25},{17,1},{25,9},{2,18},{10... | collective-permute-start | bytes 786440 | tf_op jit(solution)/shard_map/ppermute | solution.py:25
  9.2 3.6 %collective-permute-start.6 = (bf16[1024,128]{1,0:T(8,128)(2,1)S(1)}, bf16[1024,128]{1,0:T(8,128)(2,1)S(1)}, u32[]{:S(2)}, u32[]{:S(2)}) collective-permute-start(bf16[1024,128]{1,0:T(8,128)(2,1)S(1)} %pad_maximum_fusion.refs_2_), channel_id=1, source_target_pairs={{0,6},{1,7},{2,4},{3,5},{4,2},{5,3},{6,0},{7,1},{8,14},{9,15},{10,... | collective-permute-start | bytes 786440 | tf_op jit(solution)/shard_map/ppermute | solution.py:44
  15.4 1.6 %shard_map.77 = (bf16[2,4,512,128]{3,2,1,0:T(8,128)(2,1)S(1)}, s32[4,9]{1,0:T(4,128)S(1)}) custom-call(s32[1,4]{1,0:T(1,128)S(1)} %copy-done.2, s32[1,16,7]{2,1,0:T(8,128)S(1)} %copy.8.mask_ref, s32[1,16]{1,0:T(1,128)S(1)} %copy-done.3, bf16[256,2048]{1,0:T(8,128)(2,1)S(1)} %bitcast.7, bf16[256,2048]{1,0:T(8,128)(2,1)S(1)} %collective-permute-done.4.q_other_ref), custom_call_target="tpu_custom_call" | custom-call | bytes 1048576 | tf_op jit(solution)/shard_map/pallas_call | solution.py:236
  19.2 5.0 %collective-permute-start.8 = (bf16[1024,128]{1,0:T(8,128)(2,1)S(1)}, bf16[1024,128]{1,0:T(8,128)(2,1)S(1)}, u32[]{:S(2)}, u32[]{:S(2)}) collective-permute-start(bf16[1024,128]{1,0:T(8,128)(2,1)S(1)} %collective-permute-done.6.refs_4_), channel_id=1, source_target_pairs={{0,2},{1,3},{2,0},{3,1},{4,6},{5,7},{6,4},{7,5},{8,10},{9,11},{10,... | collective-permute-start | bytes 786440 | tf_op jit(solution)/shard_map/ppermute | solution.py:38
  25.9 1.5 %collective-permute-start.11 = (bf16[1024,128]{1,0:T(8,128)(2,1)S(1)}, bf16[1024,128]{1,0:T(8,128)(2,1)S(1)}, u32[]{:S(2)}, u32[]{:S(2)}) collective-permute-start(bf16[1024,128]{1,0:T(8,128)(2,1)S(1)} %collective-permute-done.5.refs_3_), channel_id=1, source_target_pairs={{0,8},{8,0},{16,24},{24,16},{1,9},{9,1},{17,25},{25,17},{2,10},{10... | collective-permute-start | bytes 786440 | tf_op jit(solution)/shard_map/ppermute | solution.py:25
  27.3 1.5 %collective-permute-start.12 = (bf16[1024,128]{1,0:T(8,128)(2,1)S(1)}, bf16[1024,128]{1,0:T(8,128)(2,1)S(1)}, u32[]{:S(2)}, u32[]{:S(2)}) collective-permute-start(bf16[1024,128]{1,0:T(8,128)(2,1)S(1)} %collective-permute-done.5.refs_3_), channel_id=1, source_target_pairs={{0,16},{8,24},{16,0},{24,8},{1,17},{9,25},{17,1},{25,9},{2,18},{10... | collective-permute-start | bytes 786440 | tf_op jit(solution)/shard_map/ppermute | solution.py:25
  28.9 1.6 %collective-permute-done.8.refs_1_ = bf16[1024,128]{1,0:T(8,128)(2,1)S(1)} collective-permute-done((bf16[1024,128]{1,0:T(8,128)(2,1)S(1)}, bf16[1024,128]{1,0:T(8,128)(2,1)S(1)}, u32[]{:S(2)}, u32[]{:S(2)}) %collective-permute-start.8) | collective-permute-done | bytes 262176 | tf_op jit(solution)/shard_map/ppermute | solution.py:38
  31.0 3.1 %collective-permute-done.10.refs_7_ = bf16[1024,128]{1,0:T(8,128)(2,1)S(1)} collective-permute-done((bf16[1024,128]{1,0:T(8,128)(2,1)S(1)}, bf16[1024,128]{1,0:T(8,128)(2,1)S(1)}, u32[]{:S(2)}, u32[]{:S(2)}) %collective-permute-start.10) | collective-permute-done | bytes 262176 | tf_op jit(solution)/shard_map/ppermute | solution.py:25
  34.6 2.8 %shard_map.78 = (f32[512,128]{1,0:T(8,128)S(1)}, bf16[512,3072]{1,0:T(8,128)(2,1)S(1)}) custom-call(bf16[256,4096]{1,0:T(8,128)(2,1)S(1)} %bitcast.3, bf16[256,4096]{1,0:T(8,128)(2,1)} %collective-permute-done.3.refs_1_, bf16[1024,128]{1,0:T(8,128)(2,1)S(1)} %pad_maximum_fusion.refs_2_, bf16[1024,128]{1,0:T(8,128)(2,1)S(1)} %collective-permute-done.5.refs_3_, ...), custom_call_target="tpu_custom_call" | custom-call | flops 402653184 | bytes 3145728 | tf_op jit(solution)/shard_map/pallas_call | solution.py:133
  38.2 1.8 %collective-permute-done.11.refs_3_ = bf16[1024,128]{1,0:T(8,128)(2,1)S(1)} collective-permute-done((bf16[1024,128]{1,0:T(8,128)(2,1)S(1)}, bf16[1024,128]{1,0:T(8,128)(2,1)S(1)}, u32[]{:S(2)}, u32[]{:S(2)}) %collective-permute-start.11) | collective-permute-done | bytes 262176 | tf_op jit(solution)/shard_map/ppermute | solution.py:25
  40.1 2.7 %shard_map.80.refs_3_ = f32[512,256]{1,0:T(8,128)S(1)} custom-call(bf16[256,4096]{1,0:T(8,128)(2,1)S(1)} %bitcast.4, bf16[256,4096]{1,0:T(8,128)(2,1)} %collective-permute-done.3.refs_1_, bf16[1024,128]{1,0:T(8,128)(2,1)} %collective-permute-done.1.refs_2_, bf16[1024,128]{1,0:T(8,128)(2,1)S(1)} %collective-permute-done.11.refs_3_, ...), custom_call_target="tpu_custom_call" | custom-call | flops 805306368 | bytes 3145728 | tf_op jit(solution)/shard_map/pallas_call | solution.py:133
  42.9 1.8 %collective-permute-done.15.refs_4_.back_a = bf16[512,128]{1,0:T(8,128)(2,1)S(1)} collective-permute-done((bf16[512,128]{1,0:T(8,128)(2,1)S(1)}, bf16[512,128]{1,0:T(8,128)(2,1)S(1)}, u32[]{:S(2)}, u32[]{:S(2)}) %collective-permute-start.15) | collective-permute-done | bytes 131104 | tf_op jit(solution)/shard_map/ppermute | solution.py:34
  46.0 1.2 %collective-permute-start.19 = (bf16[1024,128]{1,0:T(8,128)(2,1)S(1)}, bf16[1024,128]{1,0:T(8,128)(2,1)S(1)}, u32[]{:S(2)}, u32[]{:S(2)}) collective-permute-start(bf16[1024,128]{1,0:T(8,128)(2,1)S(1)} %collective-permute-done.13.refs_1_), channel_id=1, source_target_pairs={{0,16},{8,24},{16,0},{24,8},{1,17},{9,25},{17,1},{25,9},{2,18},{10... | collective-permute-start | bytes 786440 | tf_op jit(solution)/shard_map/ppermute | solution.py:25
  48.1 1.3 %collective-permute-start.21 = (bf16[512,128]{1,0:T(8,128)(2,1)S(1)}, bf16[512,128]{1,0:T(8,128)(2,1)S(1)}, u32[]{:S(2)}, u32[]{:S(2)}) collective-permute-start(bf16[512,128]{1,0:T(8,128)(2,1)S(1)} %slice.14), channel_id=1, source_target_pairs={{0,8},{8,0},{16,24},{24,16},{1,9},{9,1},{17,25},{25,17},{2,10},{10... | collective-permute-start | bytes 393224 | tf_op jit(solution)/shard_map/ppermute | solution.py:25
  49.4 2.0 %shard_map.84.refs_5_ = f32[512,128]{1,0:T(8,128)S(1)} custom-call(bf16[256,4096]{1,0:T(8,128)(2,1)S(1)} %bitcast.5, bf16[256,4096]{1,0:T(8,128)(2,1)} %collective-permute-done.3.refs_1_, bf16[1024,128]{1,0:T(8,128)(2,1)S(1)} %collective-permute-done.7.refs_2_), custom_call_target="tpu_custom_call" | custom-call | tf_op jit(solution)/shard_map/pallas_call | solution.py:133
  51.9 2.6 %collective-permute-done.20.refs_3_ = bf16[512,128]{1,0:T(8,128)(2,1)S(1)} collective-permute-done((bf16[512,128]{1,0:T(8,128)(2,1)S(1)}, bf16[512,128]{1,0:T(8,128)(2,1)S(1)}, u32[]{:S(2)}, u32[]{:S(2)}) %collective-permute-start.20) | collective-permute-done | bytes 131104 | tf_op jit(solution)/shard_map/ppermute | solution.py:25
  55.4 1.6 %collective-permute-start.22 = (bf16[512,128]{1,0:T(8,128)(2,1)S(1)}, bf16[512,128]{1,0:T(8,128)(2,1)S(1)}, u32[]{:S(2)}, u32[]{:S(2)}) collective-permute-start(bf16[512,128]{1,0:T(8,128)(2,1)S(1)} %shard_map.85.near_b), channel_id=1, source_target_pairs={{0,2},{1,3},{2,4},{3,5},{4,6},{5,7},{6,0},{7,1},{8,10},{9,11},{10,... | collective-permute-start | bytes 393224 | tf_op jit(solution)/shard_map/ppermute | solution.py:34
  57.1 1.6 %collective-permute-start.17 = (bf16[896,128]{1,0:T(8,128)(2,1)S(1)}, bf16[896,128]{1,0:T(8,128)(2,1)S(1)}, u32[]{:S(2)}, u32[]{:S(2)}) collective-permute-start(bf16[896,128]{1,0:T(8,128)(2,1)S(1)} %slice.16), channel_id=1, source_target_pairs={{0,2},{1,3},{2,4},{3,5},{4,6},{5,7},{6,0},{7,1},{8,10},{9,11},{10,... | collective-permute-start | bytes 688136 | tf_op jit(solution)/shard_map/ppermute | solution.py:34
  58.7 1.3 %collective-permute-start.23 = (bf16[384,128]{1,0:T(8,128)(2,1)S(1)}, bf16[384,128]{1,0:T(8,128)(2,1)S(1)}, u32[]{:S(2)}, u32[]{:S(2)}) collective-permute-start(bf16[384,128]{1,0:T(8,128)(2,1)S(1)} %slice.17), channel_id=1, source_target_pairs={{0,4},{1,5},{2,6},{3,7},{4,0},{5,1},{6,2},{7,3},{8,12},{9,13},{10,... | collective-permute-start | bytes 294920 | tf_op jit(solution)/shard_map/ppermute | solution.py:34
  60.0 3.2 %shard_map.82 = (f32[4,128,512]{2,1,0:T(8,128)S(1)}, f32[4,8,512]{2,1,0:T(8,128)S(1)}) custom-call(s32[4,9]{1,0:T(4,128)S(1)} %get-tuple-element.42.facts, bf16[2,4,512,128]{3,2,1,0:T(8,128)(2,1)S(1)} %get-tuple-element.43.queries_ref, bf16[512,128]{1,0:T(8,128)(2,1)S(1)} %shard_map.79.near_a, bf16[1408,128]{1,0:T(8,128)(2,1)S(1)} %shard_map.81.near_b.near_a, ...), custom_call_target="tpu_custom_call" | custom-call | flops 1073741824 | bytes 4194304 | tf_op jit(solution)/shard_map/pallas_call | solution.py:419
  63.2 3.4 %shard_map.86 = (f32[4,128,512]{2,1,0:T(8,128)S(1)}, f32[4,8,512]{2,1,0:T(8,128)S(1)}) custom-call(s32[4,9]{1,0:T(4,128)S(1)} %get-tuple-element.42.facts, bf16[2,4,512,128]{3,2,1,0:T(8,128)(2,1)S(1)} %get-tuple-element.43.queries_ref, bf16[1408,128]{1,0:T(8,128)(2,1)S(1)} %shard_map.81.near_b.near_a, bf16[512,128]{1,0:T(8,128)(2,1)S(1)} %shard_map.85.near_b, ...), custom_call_target="tpu_custom_call" | custom-call | flops 1073741824 | bytes 4194304 | tf_op jit(solution)/shard_map/pallas_call | solution.py:419
  70.1 1.3 %collective-permute-done.26.st_got = f32[4,4,128]{2,1,0:T(4,128)S(1)} collective-permute-done((f32[4,4,128]{2,1,0:T(4,128)S(1)}, f32[4,4,128]{2,1,0:T(4,128)S(1)}, u32[]{:S(2)}, u32[]{:S(2)}) %collective-permute-start.26) | collective-permute-done | bytes 8224 | tf_op jit(solution)/shard_map/ppermute | solution.py:29
  (58 shorter events, 19.3 us)
Async XLA Ops:
  2.5 14.5 %collective-permute-start.3 = (bf16[256,4096]{1,0:T(8,128)(2,1)}, bf16[256,4096]{1,0:T(8,128)(2,1)}, u32[]{:S(2)}, u32[]{:S(2)}) collective-permute-start(bf16[256,4096]{1,0:T(8,128)(2,1)} %bitcast.2), channel_id=1, source_target_pairs={{0,1},{1,0},{2,3},{3,2},{4,5},{5,4},{6,7},{7,6},{8,9},{9,8},{10,11... | collective-permute-start | bytes 6291464 | tf_op jit(solution)/shard_map/ppermute | solution.py:29
  2.9 9.9 %collective-permute-start.4 = (bf16[256,2048]{1,0:T(8,128)(2,1)}, bf16[256,2048]{1,0:T(8,128)(2,1)S(1)}, u32[]{:S(2)}, u32[]{:S(2)}) collective-permute-start(bf16[256,2048]{1,0:T(8,128)(2,1)} %bitcast.6), channel_id=1, source_target_pairs={{0,1},{1,0},{2,3},{3,2},{4,5},{5,4},{6,7},{7,6},{8,9},{9,8},{10,11... | collective-permute-start | bytes 3145736 | tf_op jit(solution)/shard_map/ppermute | solution.py:29
  4.0 13.0 %collective-permute-start.1 = (bf16[1024,128]{1,0:T(8,128)(2,1)S(1)}, bf16[1024,128]{1,0:T(8,128)(2,1)}, u32[]{:S(2)}, u32[]{:S(2)}) collective-permute-start(bf16[1024,128]{1,0:T(8,128)(2,1)S(1)} %pad_maximum_fusion.refs_2_), channel_id=1, source_target_pairs={{0,8},{8,0},{16,24},{24,16},{1,9},{9,1},{17,25},{25,17},{2,10},{10... | collective-permute-start | bytes 786440 | tf_op jit(solution)/shard_map/ppermute | solution.py:25
  6.9 10.1 %collective-permute-start.2 = (bf16[1024,128]{1,0:T(8,128)(2,1)S(1)}, bf16[1024,128]{1,0:T(8,128)(2,1)}, u32[]{:S(2)}, u32[]{:S(2)}) collective-permute-start(bf16[1024,128]{1,0:T(8,128)(2,1)S(1)} %pad_maximum_fusion.refs_2_), channel_id=1, source_target_pairs={{0,16},{8,24},{16,0},{24,8},{1,17},{9,25},{17,1},{25,9},{2,18},{10... | collective-permute-start | bytes 786440 | tf_op jit(solution)/shard_map/ppermute | solution.py:25
  9.2 10.0 %collective-permute-start.6 = (bf16[1024,128]{1,0:T(8,128)(2,1)S(1)}, bf16[1024,128]{1,0:T(8,128)(2,1)S(1)}, u32[]{:S(2)}, u32[]{:S(2)}) collective-permute-start(bf16[1024,128]{1,0:T(8,128)(2,1)S(1)} %pad_maximum_fusion.refs_2_), channel_id=1, source_target_pairs={{0,6},{1,7},{2,4},{3,5},{4,2},{5,3},{6,0},{7,1},{8,14},{9,15},{10,... | collective-permute-start | bytes 786440 | tf_op jit(solution)/shard_map/ppermute | solution.py:44
  17.0 7.8 %collective-permute-start.7 = (bf16[1024,128]{1,0:T(8,128)(2,1)}, bf16[1024,128]{1,0:T(8,128)(2,1)S(1)}, u32[]{:S(2)}, u32[]{:S(2)}) collective-permute-start(bf16[1024,128]{1,0:T(8,128)(2,1)} %collective-permute-done.1.refs_2_), channel_id=1, source_target_pairs={{0,16},{8,24},{16,0},{24,8},{1,17},{9,25},{17,1},{25,9},{2,18},{10... | collective-permute-start | bytes 786440 | tf_op jit(solution)/shard_map/ppermute | solution.py:25
  17.6 8.3 %collective-permute-start.5 = (bf16[1024,128]{1,0:T(8,128)(2,1)S(1)}, bf16[1024,128]{1,0:T(8,128)(2,1)S(1)}, u32[]{:S(2)}, u32[]{:S(2)}) collective-permute-start(bf16[1024,128]{1,0:T(8,128)(2,1)S(1)} %pad_maximum_fusion.refs_2_), channel_id=1, source_target_pairs={{0,2},{1,3},{2,0},{3,1},{4,6},{5,7},{6,4},{7,5},{8,10},{9,11},{10,... | collective-permute-start | bytes 786440 | tf_op jit(solution)/shard_map/ppermute | solution.py:38
  19.2 11.3 %collective-permute-start.8 = (bf16[1024,128]{1,0:T(8,128)(2,1)S(1)}, bf16[1024,128]{1,0:T(8,128)(2,1)S(1)}, u32[]{:S(2)}, u32[]{:S(2)}) collective-permute-start(bf16[1024,128]{1,0:T(8,128)(2,1)S(1)} %collective-permute-done.6.refs_4_), channel_id=1, source_target_pairs={{0,2},{1,3},{2,0},{3,1},{4,6},{5,7},{6,4},{7,5},{8,10},{9,11},{10,... | collective-permute-start | bytes 786440 | tf_op jit(solution)/shard_map/ppermute | solution.py:38
  24.8 9.2 %collective-permute-start.10 = (bf16[1024,128]{1,0:T(8,128)(2,1)S(1)}, bf16[1024,128]{1,0:T(8,128)(2,1)S(1)}, u32[]{:S(2)}, u32[]{:S(2)}) collective-permute-start(bf16[1024,128]{1,0:T(8,128)(2,1)S(1)} %collective-permute-done.6.refs_4_), channel_id=1, source_target_pairs={{0,16},{8,24},{16,0},{24,8},{1,17},{9,25},{17,1},{25,9},{2,18},{10... | collective-permute-start | bytes 786440 | tf_op jit(solution)/shard_map/ppermute | solution.py:25
  25.3 12.5 %collective-permute-start.9 = (bf16[1024,128]{1,0:T(8,128)(2,1)S(1)}, bf16[1024,128]{1,0:T(8,128)(2,1)S(1)}, u32[]{:S(2)}, u32[]{:S(2)}) collective-permute-start(bf16[1024,128]{1,0:T(8,128)(2,1)S(1)} %collective-permute-done.6.refs_4_), channel_id=1, source_target_pairs={{0,8},{8,0},{16,24},{24,16},{1,9},{9,1},{17,25},{25,17},{2,10},{10... | collective-permute-start | bytes 786440 | tf_op jit(solution)/shard_map/ppermute | solution.py:25
  25.9 14.2 %collective-permute-start.11 = (bf16[1024,128]{1,0:T(8,128)(2,1)S(1)}, bf16[1024,128]{1,0:T(8,128)(2,1)S(1)}, u32[]{:S(2)}, u32[]{:S(2)}) collective-permute-start(bf16[1024,128]{1,0:T(8,128)(2,1)S(1)} %collective-permute-done.5.refs_3_), channel_id=1, source_target_pairs={{0,8},{8,0},{16,24},{24,16},{1,9},{9,1},{17,25},{25,17},{2,10},{10... | collective-permute-start | bytes 786440 | tf_op jit(solution)/shard_map/ppermute | solution.py:25
  27.3 12.7 %collective-permute-start.12 = (bf16[1024,128]{1,0:T(8,128)(2,1)S(1)}, bf16[1024,128]{1,0:T(8,128)(2,1)S(1)}, u32[]{:S(2)}, u32[]{:S(2)}) collective-permute-start(bf16[1024,128]{1,0:T(8,128)(2,1)S(1)} %collective-permute-done.5.refs_3_), channel_id=1, source_target_pairs={{0,16},{8,24},{16,0},{24,8},{1,17},{9,25},{17,1},{25,9},{2,18},{10... | collective-permute-start | bytes 786440 | tf_op jit(solution)/shard_map/ppermute | solution.py:25
  30.4 12.4 %collective-permute-start.13 = (bf16[1024,128]{1,0:T(8,128)(2,1)S(1)}, bf16[1024,128]{1,0:T(8,128)(2,1)S(1)}, u32[]{:S(2)}, u32[]{:S(2)}) collective-permute-start(bf16[1024,128]{1,0:T(8,128)(2,1)S(1)} %collective-permute-done.8.refs_1_), channel_id=1, source_target_pairs={{0,8},{8,0},{16,24},{24,16},{1,9},{9,1},{17,25},{25,17},{2,10},{10... | collective-permute-start | bytes 786440 | tf_op jit(solution)/shard_map/ppermute | solution.py:25
  34.1 8.8 %collective-permute-start.14 = (bf16[1024,128]{1,0:T(8,128)(2,1)S(1)}, bf16[1024,128]{1,0:T(8,128)(2,1)S(1)}, u32[]{:S(2)}, u32[]{:S(2)}) collective-permute-start(bf16[1024,128]{1,0:T(8,128)(2,1)S(1)} %collective-permute-done.8.refs_1_), channel_id=1, source_target_pairs={{0,16},{8,24},{16,0},{24,8},{1,17},{9,25},{17,1},{25,9},{2,18},{10... | collective-permute-start | bytes 786440 | tf_op jit(solution)/shard_map/ppermute | solution.py:25
  37.8 6.8 %collective-permute-start.15 = (bf16[512,128]{1,0:T(8,128)(2,1)S(1)}, bf16[512,128]{1,0:T(8,128)(2,1)S(1)}, u32[]{:S(2)}, u32[]{:S(2)}) collective-permute-start(bf16[512,128]{1,0:T(8,128)(2,1)S(1)} %shard_map.79.near_a), channel_id=1, source_target_pairs={{0,2},{1,3},{2,4},{3,5},{4,6},{5,7},{6,0},{7,1},{8,10},{9,11},{10,... | collective-permute-start | bytes 393224 | tf_op jit(solution)/shard_map/ppermute | solution.py:34
  45.1 12.0 %collective-permute-start.16 = (bf16[1408,128]{1,0:T(8,128)(2,1)S(1)}, bf16[1408,128]{1,0:T(8,128)(2,1)S(1)}, u32[]{:S(2)}, u32[]{:S(2)}) collective-permute-start(bf16[1408,128]{1,0:T(8,128)(2,1)S(1)} %shard_map.81.near_b.near_a), channel_id=1, source_target_pairs={{0,2},{1,3},{2,4},{3,5},{4,6},{5,7},{6,0},{7,1},{8,10},{9,11},{10,... | collective-permute-start | bytes 1081352 | tf_op jit(solution)/shard_map/ppermute | solution.py:34
  45.1 6.7 %collective-permute-start.18 = (bf16[1024,128]{1,0:T(8,128)(2,1)S(1)}, bf16[1024,128]{1,0:T(8,128)(2,1)S(1)}, u32[]{:S(2)}, u32[]{:S(2)}) collective-permute-start(bf16[1024,128]{1,0:T(8,128)(2,1)S(1)} %collective-permute-done.12.refs_6_), channel_id=1, source_target_pairs={{0,8},{8,0},{16,24},{24,16},{1,9},{9,1},{17,25},{25,17},{2,10},{10... | collective-permute-start | bytes 786440 | tf_op jit(solution)/shard_map/ppermute | solution.py:25
  46.0 8.4 %collective-permute-start.19 = (bf16[1024,128]{1,0:T(8,128)(2,1)S(1)}, bf16[1024,128]{1,0:T(8,128)(2,1)S(1)}, u32[]{:S(2)}, u32[]{:S(2)}) collective-permute-start(bf16[1024,128]{1,0:T(8,128)(2,1)S(1)} %collective-permute-done.13.refs_1_), channel_id=1, source_target_pairs={{0,16},{8,24},{16,0},{24,8},{1,17},{9,25},{17,1},{25,9},{2,18},{10... | collective-permute-start | bytes 786440 | tf_op jit(solution)/shard_map/ppermute | solution.py:25
  47.3 7.2 %collective-permute-start.20 = (bf16[512,128]{1,0:T(8,128)(2,1)S(1)}, bf16[512,128]{1,0:T(8,128)(2,1)S(1)}, u32[]{:S(2)}, u32[]{:S(2)}) collective-permute-start(bf16[512,128]{1,0:T(8,128)(2,1)S(1)} %slice.13), channel_id=1, source_target_pairs={{0,16},{8,24},{16,0},{24,8},{1,17},{9,25},{17,1},{25,9},{2,18},{10... | collective-permute-start | bytes 393224 | tf_op jit(solution)/shard_map/ppermute | solution.py:25
  48.1 6.3 %collective-permute-start.21 = (bf16[512,128]{1,0:T(8,128)(2,1)S(1)}, bf16[512,128]{1,0:T(8,128)(2,1)S(1)}, u32[]{:S(2)}, u32[]{:S(2)}) collective-permute-start(bf16[512,128]{1,0:T(8,128)(2,1)S(1)} %slice.14), channel_id=1, source_target_pairs={{0,8},{8,0},{16,24},{24,16},{1,9},{9,1},{17,25},{25,17},{2,10},{10... | collective-permute-start | bytes 393224 | tf_op jit(solution)/shard_map/ppermute | solution.py:25
  55.4 7.8 %collective-permute-start.22 = (bf16[512,128]{1,0:T(8,128)(2,1)S(1)}, bf16[512,128]{1,0:T(8,128)(2,1)S(1)}, u32[]{:S(2)}, u32[]{:S(2)}) collective-permute-start(bf16[512,128]{1,0:T(8,128)(2,1)S(1)} %shard_map.85.near_b), channel_id=1, source_target_pairs={{0,2},{1,3},{2,4},{3,5},{4,6},{5,7},{6,0},{7,1},{8,10},{9,11},{10,... | collective-permute-start | bytes 393224 | tf_op jit(solution)/shard_map/ppermute | solution.py:34
  57.1 9.5 %collective-permute-start.17 = (bf16[896,128]{1,0:T(8,128)(2,1)S(1)}, bf16[896,128]{1,0:T(8,128)(2,1)S(1)}, u32[]{:S(2)}, u32[]{:S(2)}) collective-permute-start(bf16[896,128]{1,0:T(8,128)(2,1)S(1)} %slice.16), channel_id=1, source_target_pairs={{0,2},{1,3},{2,4},{3,5},{4,6},{5,7},{6,0},{7,1},{8,10},{9,11},{10,... | collective-permute-start | bytes 688136 | tf_op jit(solution)/shard_map/ppermute | solution.py:34
  58.7 9.6 %collective-permute-start.23 = (bf16[384,128]{1,0:T(8,128)(2,1)S(1)}, bf16[384,128]{1,0:T(8,128)(2,1)S(1)}, u32[]{:S(2)}, u32[]{:S(2)}) collective-permute-start(bf16[384,128]{1,0:T(8,128)(2,1)S(1)} %slice.17), channel_id=1, source_target_pairs={{0,4},{1,5},{2,6},{3,7},{4,0},{5,1},{6,2},{7,3},{8,12},{9,13},{10,... | collective-permute-start | bytes 294920 | tf_op jit(solution)/shard_map/ppermute | solution.py:34
  69.4 2.0 %collective-permute-start.25 = (bf16[256,512]{1,0:T(8,128)(2,1)S(1)}, bf16[256,512]{1,0:T(8,128)(2,1)S(1)}, u32[]{:S(2)}, u32[]{:S(2)}) collective-permute-start(bf16[256,512]{1,0:T(8,128)(2,1)S(1)} %get-tuple-element.69), channel_id=1, source_target_pairs={{0,1},{1,0},{2,3},{3,2},{4,5},{5,4},{6,7},{7,6},{8,9},{9,8},{10,11... | collective-permute-start | bytes 786440 | tf_op jit(solution)/shard_map/ppermute | solution.py:29
  (7 other events, 41.7 us)
